TPU v7x, 128 devices: a whole 4x4x4 slice. The times are simulated.
128 devices in a mesh: tp: 8 (over z_hi, x), grp: 16 (over z_lo, y, core).
Axes of the slice: x: 4, y: 4, z: 4 (z_hi: 2, z_lo: 2; z = z_hi * 2 + z_lo), core: 2. Of those that a mesh axis runs over, the one named last changes fastest.
Arguments:
- queries: bfloat16 [16, 16, 16, 9216], P('grp', None, None, 'tp'), may hold values from -8 to 8
- responses: bfloat16 [16, 16, 16, 3072], P('grp', None, None, 'tp'), may hold values from -8 to 8
- cache_pool: bfloat16 [2048, 64, 3072], P('grp', None, 'tp'), may hold values from -8 to 8
- page_table: int32 [16, 64], P('grp'), may hold values from 0 to 127, as said below
- lengths: int32 [16, 16], replicated, may hold values from 8 to 16
- routes: int32 [16, 16, 1], P('grp'), may hold values from 0 to 15; in each aligned block of 16 rows (0 to 15, 16 to 31, ..., all dimensions but the last counted through in order) at most 2 rows name the same one
- student_rows: bfloat16 [16, 32, 16, 6144], P('grp'), may hold values from -6 to 6
- projection: bfloat16 [6144, 9216], P(None, 'tp'), may hold values from -0.078125 to 0.078125
Outputs:
- grad_proj: bfloat16 [6144, 9216], P('grp', 'tp')
Inputs may be any that keep to these rules, and one draw needn't show every extreme that they name: `page_table`: each row names 64 different pages of its prompt's pool. `routes`: of the 16 responses of one prompt at most 2 go to one student group; every student group receives at least one response.
All inputs are finite; a program needn't handle non-finite values.
Results may differ from a plain program's by a relative error of at most 0.02.
Values may be sent and summed in bfloat16 or wider, within the bound.
No kernel may reach another device: no remote copies, remote signals or barrier semaphores. Data moves between devices by JAX's collectives and lax.ppermute only.
A program may use at most 128 MiB of HBM per device.

v0:
```python
import jax
import jax.numpy as jnp
from jax import lax
from jax.sharding import PartitionSpec as P

HD = 192
MOST = 2
GQA = 6


NEG_FILL = -1e30


def attention(query_rows, cache_resp, prefix):
    kv_heads = prefix.shape[-1] // (2 * HD)
    resp_count = query_rows.shape[0]
    resp_len = query_rows.shape[1]
    total_rows = resp_count * resp_len
    scaling = float(HD) ** (-0.5)
    grouped = query_rows.reshape(total_rows, kv_heads, GQA, HD)
    prefix_kv = prefix.reshape(-1, kv_heads, 2, HD)
    prefix_scores = (
        jnp.einsum(
            "nkgd,mkd->kgnm", grouped, prefix_kv[:, :, 0], preferred_element_type=jnp.float32
        )
        * scaling
    )
    prefix_max = jnp.max(prefix_scores, axis=-1)
    prefix_exp = jnp.exp(prefix_scores - prefix_max[..., None])
    prefix_total = jnp.sum(prefix_exp, axis=-1)
    prefix_out = jnp.einsum(
        "kgnm,mkd->kgnd",
        prefix_exp.astype(jnp.bfloat16),
        prefix_kv[:, :, 1],
        preferred_element_type=jnp.float32,
    )
    query_resp = query_rows.reshape(resp_count, resp_len, kv_heads, GQA, HD)
    resp_kv = cache_resp.reshape(resp_count, resp_len, kv_heads, 2, HD)
    resp_scores = (
        jnp.einsum(
            "rnkgd,rmkd->rkgnm", query_resp, resp_kv[:, :, :, 0], preferred_element_type=jnp.float32
        )
        * scaling
    )
    positions = jnp.arange(resp_len)
    causal = positions[:, None] >= positions[None, :]
    resp_scores = jnp.where(causal, resp_scores, NEG_FILL)
    resp_max = jnp.max(resp_scores, axis=-1)
    resp_exp = jnp.exp(resp_scores - resp_max[..., None])
    resp_total = jnp.sum(resp_exp, axis=-1)
    resp_out = jnp.einsum(
        "rkgnm,rmkd->rkgnd",
        resp_exp.astype(jnp.bfloat16),
        resp_kv[:, :, :, 1],
        preferred_element_type=jnp.float32,
    )
    resp_max = resp_max.transpose(1, 2, 0, 3).reshape(kv_heads, GQA, total_rows)
    resp_total = resp_total.transpose(1, 2, 0, 3).reshape(kv_heads, GQA, total_rows)
    resp_out = resp_out.transpose(1, 2, 0, 3, 4).reshape(kv_heads, GQA, total_rows, HD)
    joint_max = jnp.maximum(prefix_max, resp_max)
    prefix_factor = jnp.exp(prefix_max - joint_max)
    resp_factor = jnp.exp(resp_max - joint_max)
    merged = (prefix_out * prefix_factor[..., None] + resp_out * resp_factor[..., None]) / (
        prefix_total * prefix_factor + resp_total * resp_factor
    )[..., None]
    return (
        merged.transpose(2, 0, 1, 3).reshape(total_rows, kv_heads * GQA * HD).astype(jnp.bfloat16)
    )


def to_slots(sender, source):
    resp_count = source.shape[0]
    resp_len = source.shape[1]
    placed = jnp.dot(sender, source.reshape(resp_count, -1), preferred_element_type=jnp.float32)
    return placed.astype(jnp.bfloat16).reshape(sender.shape[0] * resp_len, source.shape[2])


def body(queries, responses, cache_pool, page_table, lengths, routes, student_rows, projection):
    groups = lax.axis_size("grp")
    my_index = lax.axis_index("grp")
    resp_count = queries.shape[1]
    resp_len = queries.shape[2]
    prefix = jnp.take(cache_pool, page_table[0], axis=0).reshape(-1, cache_pool.shape[-1])
    tap_rows = attention(queries[0], responses[0], prefix)
    my_lengths = lax.dynamic_index_in_dim(lengths, my_index, 0, keepdims=False)
    live_rows = (jnp.arange(resp_len)[None, :] < my_lengths[:, None]).astype(jnp.bfloat16)
    target = routes[0, :, 0]
    hit_table = (target[:, None] == jnp.arange(groups)[None, :]).astype(jnp.int32)
    before = jnp.cumsum(hit_table, axis=0) - hit_table
    slot_rank = jnp.sum(before * hit_table, axis=1)
    slot_index = target * MOST + slot_rank
    slot_total = groups * MOST
    sender = (jnp.arange(slot_total)[:, None] == slot_index[None, :]).astype(jnp.bfloat16)
    tap_slots = to_slots(sender, tap_rows.reshape(resp_count, resp_len, -1))
    live_slots = to_slots(sender, live_rows[:, :, None]).reshape(-1)
    tap_recv, live_recv = (
        lax.all_to_all(tap_slots, "grp", split_axis=0, concat_axis=0, tiled=True),
        lax.all_to_all(live_slots, "grp", split_axis=0, concat_axis=0, tiled=True),
    )
    full_rows = student_rows[0].reshape(-1, student_rows.shape[-1])
    live_float = live_recv.astype(jnp.float32)
    token_count = jnp.sum(live_float)
    predicted = jnp.dot(full_rows, projection, preferred_element_type=jnp.float32)
    weight = live_float * (1.0 / token_count)
    grad_pred = ((predicted - tap_recv.astype(jnp.float32)) * weight[:, None]).astype(jnp.bfloat16)
    share_rows = projection.shape[0] // groups
    partial_value = lax.dot_general(
        full_rows, grad_pred, (((0,), (0,)), ((), ())), preferred_element_type=jnp.float32
    )
    summed = lax.psum(partial_value.astype(jnp.bfloat16), "grp").astype(jnp.float32)
    result = lax.dynamic_slice_in_dim(summed, my_index * share_rows, share_rows, 0)
    return result.astype(jnp.bfloat16)


def solution(mesh):
    return jax.shard_map(
        body,
        mesh=mesh,
        in_specs=(
            P("grp", None, None, "tp"),
            P("grp", None, None, "tp"),
            P("grp", None, "tp"),
            P("grp", None),
            P(),
            P("grp", None, None),
            P("grp", None, None, None),
            P(None, "tp"),
        ),
        out_specs=P("grp", "tp"),
        check_vma=False,
    )
```

profile of v0, /device:TPU:1, one launch (start us, length us, event | category | flops | bytes accessed | tf_op | source)
XLA Modules:
  0.0 304.3 jit_solution(1488850358062496386)
XLA Ops:
  6.5 0.0 copy-start
  6.5 0.0 copy-start.3
  6.5 0.8 fusion.34
  7.3 0.8 select_reduce_fusion
  8.2 0.7 multiply_add_fusion.1
  8.8 0.0 copy-done
  8.9 0.3 convolution_convert_fusion.2
  9.1 0.1 copy.56
  9.2 0.7 all_to_all.16
  9.9 7.3 %all-to-all-start.1 = ((bf16[16,32,1]{1,2,0:T(2,128)(2,1)}), bf16[16,32,1]{1,2,0:T(2,128)(2,1)S(1)}, u32[]{:S(2)}, u32[]{:S(2)}) async-start(bf16[16,32,1]{1,2,0:T(2,128)(2,1)} %all_to_all.16), calls=%async_computation.1 | async-start | bytes 16384 | tf_op jit(solution)/shard_map/all_to_all | solution.py:98
  17.2 0.7 fusion.36
  17.9 0.7 compare_and_fusion
  18.6 2.0 reshape.214
  20.6 2.8 reshape.210
  23.4 0.1 broadcast_in_dim.22
  23.5 0.1 broadcast_in_dim.36
  23.6 0.0 copy-done.3
  23.6 0.2 reshape_squeeze.9
  23.7 0.6 fusion.40
  24.3 1.0 fusion.41
  25.4 0.1 reshape.215
  25.5 0.2 fusion.25
  25.7 0.1 reshape.219
  25.8 0.4 convolution_bitcast_fusion
  26.3 0.2 copy.52
  26.4 1.5 copy.53
  27.9 4.0 %gather_fusion = bf16[64,64,384]{2,1,0:T(8,128)(2,1)S(1)} fusion(bf16[128,64,384]{2,1,0:T(8,128)(2,1)} %param.10, s32[1024]{0:T(1024)S(1)} %pad_clamp_fusion), kind=kCustom, calls=%fused_computation | custom fusion | bytes 6291712 | tf_op jit(solution)/shard_map/jit(_take)/gather | solution.py:83
  31.9 3.8 %gather.7 = bf16[4096,1,2,192]{3,2,0,1:T(2,128)(2,1)} reshape(bf16[64,64,384]{2,1,0:T(8,128)(2,1)S(1)} %gather_fusion) | data formatting | bytes 6291456 | tf_op jit(solution)/shard_map/jit(_take)/gather | solution.py:83
  35.7 9.2 %copy.44 = bf16[4096,1,2,192]{0,3,2,1:T(8,128)(2,1)S(1)} copy(bf16[4096,1,2,192]{3,2,0,1:T(2,128)(2,1)} %gather.7) | data formatting | bytes 6291456 | tf_op jit(solution)/shard_map/jit(_take)/gather | solution.py:83
  44.9 2.0 broadcast_select_fusion
  47.0 5.3 %bitcast_reduce_fusion = (f32[6,256]{1,0:T(8,128)S(1)}, f32[4096,256,6]{1,0,2:T(8,128)S(1)}) fusion(bf16[256,6,192]{2,1,0:T(8,128)(2,1)} %reshape.210, bf16[4096,1,2,192]{0,3,2,1:T(8,128)(2,1)} %broadcast_select_fusion), kind=kOutput, calls=%fused_computation.2 | convolution fusion | flops 2428500480 | bytes 27793408 | tf_op jit(solution)/shard_map/nkgd,mkd->kgnm/dot_general | solution.py:23
  52.2 0.0 copy-start.2
  52.2 4.6 %fusion.1 = f32[6,256]{1,0:T(8,128)S(1)} fusion(f32[4096,256,6]{1,0,2:T(8,128)S(1)} %get-tuple-element.13, f32[6,256]{1,0:T(8,128)S(1)} %get-tuple-element.12), kind=kLoop, calls=%fused_computation.5 | loop fusion | flops 18872832 | bytes 25178112 | tf_op jit(solution)/shard_map/reduce_sum | solution.py:30
  56.9 3.7 %copy-done.2 = f32[4096,256,6]{1,0,2:T(8,128)} copy-done((f32[4096,256,6]{1,0,2:T(8,128)}, f32[4096,256,6]{1,0,2:T(8,128)S(1)}, u32[]{:S(2)}) %copy-start.2) | copy-done | bytes 25165848
  60.5 11.6 %fusion.20 = bf16[256,1,6,192]{0,3,2,1:T(8,128)(2,1)S(1)} fusion(f32[6,256,192]{1,2,0:T(8,128)} %copy.53, f32[4096,256,6]{1,0,2:T(8,128)} %copy-done.2, f32[6,256]{1,0:T(8,128)S(1)} %get-tuple-element.12, bf16[4096,1,2,192]{0,3,2,1:T(8,128)(2,1)} %broadcast_select_fusion, f32[6,256]{1,0:T(8,128)S(1)} %get-tuple-element.5, ...), kind=kOutput, calls=%fused_computation.27 | convolution fusion | flops 2436268032 | bytes 28532736 | tf_op jit(solution)/shard_map/kgnm,mkd->kgnd/dot_general | solution.py:31
  72.1 0.9 copy.55
  73.1 1.0 convert_element_type.66
  74.1 0.4 convolution_convert_fusion.1
  74.5 1.4 all_to_all.12
  75.9 0.0 all-to-all-done.1
  75.9 5.7 %all-to-all-start = ((bf16[16,32,1152]{2,1,0:T(8,128)(2,1)}), bf16[16,32,1152]{2,1,0:T(8,128)(2,1)S(1)}, u32[]{:S(2)}, u32[]{:S(2)}) async-start(bf16[16,32,1152]{2,1,0:T(8,128)(2,1)} %all_to_all.12), calls=%async_computation | async-start | bytes 2359296 | tf_op jit(solution)/shard_map/all_to_all | solution.py:97
  81.6 0.0 all-reduce.2.cloned.1.call-start
  81.7 0.6 convert_reduce_fusion
  83.0 0.1 mul.112
  83.1 15.8 %all-to-all-done = bf16[16,32,1152]{2,1,0:T(8,128)(2,1)S(1)} async-done(((bf16[16,32,1152]{2,1,0:T(8,128)(2,1)}), bf16[16,32,1152]{2,1,0:T(8,128)(2,1)S(1)}, u32[]{:S(2)}, u32[]{:S(2)}) %all-to-all-start) | async-done | bytes 1179680 | tf_op jit(solution)/shard_map/all_to_all | solution.py:97
  98.9 27.6 %fusion.3 = bf16[6144,1152]{0,1:T(8,128)(2,1)} fusion(bf16[512,6144]{1,0:T(8,128)(2,1)} %bitcast.124, bf16[6144,1152]{1,0:T(8,128)(2,1)} %param.15, bf16[512,1152]{1,0:T(8,128)(2,1)S(1)} %bitcast.125, f32[512]{0:T(512)S(1)} %mul.112), kind=kOutput, calls=%fused_computation.8 | convolution fusion | flops 14504951808 | bytes 35784704 | tf_op jit(solution)/shard_map/dot_general | solution.py:107
  126.5 0.0 all-reduce.2.cloned.1.call-update
  126.5 0.0 copy-start.1
  126.5 168.2 %all-reduce.2.cloned.1.call-done = bf16[6144,1152]{0,1:T(8,128)(2,1)} async-done(((bf16[6144,1152]{0,1:T(8,128)(2,1)}), bf16[6144,1152]{0,1:T(8,128)(2,1)}) %all-reduce.2.cloned.1.call-update) | async-done | bytes 14155792 | tf_op jit(solution)/shard_map/psum | solution.py:110
  294.7 1.3 convert_convert_fusion
  296.0 1.5 copy.58
  297.5 0.0 copy-done.1
  (8 shorter events, 0.1 us)
Async XLA Ops:
  6.5 2.3 copy-start
  6.5 17.0 %copy-start.3 = (bf16[1,16,16,384]{3,2,1,0:T(8,128)(2,1)S(1)}, bf16[1,16,16,384]{3,2,1,0:T(8,128)(2,1)}, u32[]{:S(2)}) copy-start(bf16[1,16,16,384]{3,2,1,0:T(8,128)(2,1)} %param.9) | copy-start | bytes 589828
  9.9 66.0 %all-to-all-start.1 = ((bf16[16,32,1]{1,2,0:T(2,128)(2,1)}), bf16[16,32,1]{1,2,0:T(2,128)(2,1)S(1)}, u32[]{:S(2)}, u32[]{:S(2)}) async-start(bf16[16,32,1]{1,2,0:T(2,128)(2,1)} %all_to_all.16), calls=%async_computation.1 | async-start | bytes 16384 | tf_op jit(solution)/shard_map/all_to_all | solution.py:98
  52.2 8.3 %copy-start.2 = (f32[4096,256,6]{1,0,2:T(8,128)}, f32[4096,256,6]{1,0,2:T(8,128)S(1)}, u32[]{:S(2)}) copy-start(f32[4096,256,6]{1,0,2:T(8,128)S(1)} %get-tuple-element.13) | copy-start | bytes 75497472
  75.9 23.0 %all-to-all-start = ((bf16[16,32,1152]{2,1,0:T(8,128)(2,1)}), bf16[16,32,1152]{2,1,0:T(8,128)(2,1)S(1)}, u32[]{:S(2)}, u32[]{:S(2)}) async-start(bf16[16,32,1152]{2,1,0:T(8,128)(2,1)} %all_to_all.12), calls=%async_computation | async-start | bytes 2359296 | tf_op jit(solution)/shard_map/all_to_all | solution.py:97
  81.6 213.1 %all-reduce.2.cloned.1.call-start = ((), (), s32[]{:S(2)}) async-start(), calls=%async_computation.2 | async-start | bytes 28311552 | tf_op jit(solution)/shard_map/psum | solution.py:110
  126.5 171.0 %copy-start.1 = (s32[16,16]{1,0:T(8,128)S(1)}, s32[16,16]{1,0:T(8,128)}, u32[]{:S(2)}) copy-start(s32[16,16]{1,0:T(8,128)} %param.12) | copy-start | bytes 3076
Sparse Core Ops, SparseCore 0:
  126.6 168.0 all-reduce.1
where the time goes:
time: 306 us; the launch traced here: 304 us
  waiting for transfers between devices  184 us (60%)
  matrix products  46.6 us (15%)
  local copies, waits for them, and re-layouts  33.9 us (11%)
  between operations  14.3 us (5%)
  starting transfers between devices  13.1 us (4%)
  other arithmetic  12.4 us (4%)
    psum x1, waiting for transfers between devices, body(): lax.psum(partial_value.astype(jnp.bfloat16), 'grp').astype(jnp.float32)  168 us
    dot_general x1, matrix products, body(): lax.dot_general(full_rows, grad_pred, (((0,), (0,)), ((), ())), preferred...  27.6 us
    gather x3, local copies, waits for them, and re-layouts, body(): jnp.take(cache_pool, page_table[0], axis=0)  17 us
    all_to_all x1, waiting for transfers between devices, body(): lax.all_to_all(tap_slots, 'grp', split_axis=0, concat_axis=0, tiled=True)  15.8 us
    dot_general x1, matrix products, attention(): jnp.einsum('kgnm,mkd->kgnd', prefix_exp.astype(jnp.bfloat16), prefix_kv[:...  11.6 us
    all_to_all x1, starting transfers between devices, body(): lax.all_to_all(live_slots, 'grp', split_axis=0, concat_axis=0, tiled=True)  7.34 us
  transfers between devices with their start and end apart: 3, of which 2 were waited for; matrix products, arithmetic and copies ran while one was open for 18% of the time, Pallas kernels for 0%

commit v1 on v0

v1 whole, which is shorter than its diff:
```python
import functools

import jax
import jax.numpy as jnp
from jax import lax
from jax.experimental import pallas as pl
from jax.experimental.pallas import tpu as pltpu
from jax.sharding import PartitionSpec as P

HD = 192
MOST = 2
GQA = 6
PAGE = 64
LMAX = 16
LOG2E = 1.4426950408889634
BF = jnp.bfloat16
F32 = jnp.float32

GRID = [(z, y, c) for z in range(2) for y in range(4) for c in range(2)]
TPGRID = [(h, x) for h in range(2) for x in range(4)]


def grp_at(z, y, c):
    return z * 8 + (y % 4) * 2 + c


def y_shift(step):
    return [(grp_at(z, y, c), grp_at(z, y + step, c)) for z, y, c in GRID]


Z_SWAP = [(grp_at(z, y, c), grp_at(1 - z, y, c)) for z, y, c in GRID]
C_SWAP = [(grp_at(z, y, c), grp_at(z, y, 1 - c)) for z, y, c in GRID]
H_SWAP = [(h * 4 + x, (1 - h) * 4 + x) for h, x in TPGRID]


def x_shift(step):
    return [(h * 4 + x, h * 4 + (x + step) % 4) for h, x in TPGRID]


def attention_kernel(table, q_ref, resp_ref, pool_ref, out_ref, kv, kt, vx, acc, sem, *, chunk):
    pages = table.shape[0]
    keys = pages * PAGE

    @pl.when(pl.program_id(0) == 0)
    def _():
        for j in range(pages):
            pltpu.make_async_copy(
                pool_ref.at[table[j]], kv.at[pl.ds(j * PAGE, PAGE)], sem.at[j * PAGE // chunk]
            ).start()

        def prepare(lo, n, rows):
            kt[:, lo : lo + n] = rows[:, 0:256].T
            values = rows[:, 128:384]
            lane = lax.broadcasted_iota(jnp.int32, values.shape, 1)
            ones = jnp.where(lane == 0, 1.0, 0.0).astype(BF)
            vx[lo : lo + n, :] = jnp.where(lane < 64, ones, values)

        prepare(keys, resp_ref.shape[0], resp_ref[...])
        for b in range(keys // chunk):
            block = kv.at[pl.ds(b * chunk, chunk)]
            pltpu.make_async_copy(block, block, sem.at[b]).wait()
            prepare(b * chunk, chunk, kv[b * chunk : (b + 1) * chunk, :])

    q = q_ref[...]
    n = q.shape[0]
    pad = jnp.zeros((n, 256 - HD), BF)
    q2 = jnp.concatenate(
        [jnp.concatenate([q[:, :HD], pad], 1), jnp.concatenate([q[:, HD:], pad], 1)], 0
    )
    scale = LOG2E * float(HD) ** -0.5
    bounds = [(keys, keys + n)] + [(b * chunk, (b + 1) * chunk) for b in range(keys // chunk)]
    top = None
    for lo, hi in bounds:
        s = jnp.dot(q2, kt[:, lo:hi], preferred_element_type=F32)
        if top is None:
            row = lax.broadcasted_iota(jnp.int32, s.shape, 0) % n
            col = lax.broadcasted_iota(jnp.int32, s.shape, 1)
            s = jnp.where((row // LMAX == col // LMAX) & (col <= row), s, -1e30)
        here = jnp.max(s, axis=1, keepdims=True) * scale
        new = here if top is None else jnp.maximum(top, here)
        p = jnp.exp2(s * scale - new).astype(BF)
        o = jnp.dot(p, vx[lo:hi, :], preferred_element_type=F32)
        acc[...] = o if top is None else acc[...] * jnp.exp2(top - new) + o
        top = new
    total = acc[...]
    ratio = total[:, 64:] / total[:, 0:1]
    out_ref[...] = jnp.concatenate([ratio[:n], ratio[n:]], 1).astype(BF)


def attention(q, resp, pool, table, chunk=512):
    n = q.shape[0]
    keys = table.shape[0] * PAGE
    pairs = q.shape[1] // (2 * HD)
    return pl.pallas_call(
        functools.partial(attention_kernel, chunk=chunk),
        grid_spec=pltpu.PrefetchScalarGridSpec(
            num_scalar_prefetch=1,
            grid=(pairs,),
            in_specs=[
                pl.BlockSpec((n, 2 * HD), lambda i, t: (0, i)),
                pl.BlockSpec(resp.shape, lambda i, t: (0, 0)),
                pl.BlockSpec(memory_space=pl.ANY),
            ],
            out_specs=pl.BlockSpec((n, 2 * HD), lambda i, t: (0, i)),
            scratch_shapes=[
                pltpu.VMEM((keys, 2 * HD), BF),
                pltpu.VMEM((256, keys + n), BF),
                pltpu.VMEM((keys + n, 256), BF),
                pltpu.VMEM((2 * n, 256), F32),
                pltpu.SemaphoreType.DMA((keys // chunk,)),
            ],
        ),
        out_shape=jax.ShapeDtypeStruct(q.shape, BF),
        compiler_params=pltpu.CompilerParams(vmem_limit_bytes=48 * 2**20),
        cost_estimate=pl.CostEstimate(
            flops=4 * GQA * n * (keys + n) * 256,
            bytes_accessed=8 * 2**20,
            transcendentals=GQA * n * (keys + n),
        ),
        name="attention",
    )(table, q, resp, pool)


def predict_kernel(x_ref, p_ref, out_ref, acc):
    k = pl.program_id(0)
    part = jnp.dot(x_ref[...], p_ref[...], preferred_element_type=F32)

    @pl.when(k == 0)
    def _():
        acc[...] = part

    @pl.when(k > 0)
    def _():
        acc[...] += part

    @pl.when(k == pl.num_programs(0) - 1)
    def _():
        out_ref[...] = acc[...].astype(BF)


def predict(x, p, block=768):
    n, k = x.shape
    m = p.shape[1]
    return pl.pallas_call(
        predict_kernel,
        grid=(k // block,),
        in_specs=[
            pl.BlockSpec((n, block), lambda i: (0, i)),
            pl.BlockSpec((block, m), lambda i: (i, 0)),
        ],
        out_specs=pl.BlockSpec((n, m), lambda i: (0, 0)),
        out_shape=jax.ShapeDtypeStruct((n, m), BF),
        scratch_shapes=[pltpu.VMEM((n, m), F32)],
        compiler_params=pltpu.CompilerParams(vmem_limit_bytes=32 * 2**20),
        cost_estimate=pl.CostEstimate(
            flops=2 * n * m * k, bytes_accessed=2 * (n * k + k * m + n * m), transcendentals=0
        ),
        name="predict",
    )(x, p)


def pick_kernel(place, x_ref, out_ref, sem):
    x, h = place[0], place[1]
    copies = []
    for z, y, c in GRID:
        prompt = z * 8 + x * 2 + c
        cf = c ^ (1 - h)
        for i, zf in enumerate((1 - z, z)):
            col = pl.multiple_of((zf * 8 + y * 2 + cf) * 384, 384)
            row = pl.multiple_of(prompt * 32, 32)
            copies.append(
                pltpu.make_async_copy(
                    x_ref.at[pl.ds(row, 32), pl.ds(col, 384)],
                    out_ref.at[pl.ds(grp_at(z, y, c) * 32, 32), pl.ds(i * 384, 384)],
                    sem,
                )
            )
            copies[-1].start()
    pltpu.make_async_copy(out_ref, out_ref, sem).wait()


def pick(x, place):
    return pl.pallas_call(
        pick_kernel,
        grid_spec=pltpu.PrefetchScalarGridSpec(
            num_scalar_prefetch=1,
            grid=(),
            in_specs=[pl.BlockSpec(memory_space=pl.ANY)],
            out_specs=pl.BlockSpec(memory_space=pl.ANY),
            scratch_shapes=[pltpu.SemaphoreType.DMA(())],
        ),
        out_shape=jax.ShapeDtypeStruct((512, 768), BF),
        name="pick",
    )(place, x)


def compact_kernel(slot_ref, x_ref, out_ref):
    n = x_ref.shape[0]
    rows = lax.broadcasted_iota(jnp.int32, (n, 256), 0)
    sel = (rows == slot_ref[...]).astype(F32).astype(BF)
    out_ref[...] = lax.dot_general(
        x_ref[...], sel, (((0,), (0,)), ((), ())), preferred_element_type=F32
    ).astype(BF)


def compact(slot, x):
    return pl.pallas_call(
        compact_kernel,
        out_shape=jax.ShapeDtypeStruct((x.shape[1], 256), BF),
        cost_estimate=pl.CostEstimate(
            flops=2 * 512 * 768 * 256, bytes_accessed=2 * 2**20, transcendentals=0
        ),
        name="compact",
    )(slot, x)


def grad_kernel(slot_ref, weight_ref, y_ref, tap_ref, out_ref):
    n = y_ref.shape[0]
    cols = lax.broadcasted_iota(jnp.int32, (256, n), 1)
    sel = (cols == slot_ref[...]).astype(F32).astype(BF)
    predicted = jnp.dot(sel, y_ref[...], preferred_element_type=F32)
    out_ref[...] = ((predicted - tap_ref[...].astype(F32)) * weight_ref[...]).astype(BF)


def grad_pred(slot, weight, y, tap):
    return pl.pallas_call(
        grad_kernel,
        out_shape=jax.ShapeDtypeStruct(tap.shape, BF),
        compiler_params=pltpu.CompilerParams(vmem_limit_bytes=32 * 2**20),
        cost_estimate=pl.CostEstimate(
            flops=2 * 512 * 256 * tap.shape[1], bytes_accessed=3 * 2**20, transcendentals=0
        ),
        name="grad_pred",
    )(slot, weight, y, tap)


def outer_kernel(place, x0, xa, xb, xc, xd, g0, ga, gb, gc, gd, send_ref, keep_ref, xbuf, gbuf, sem):
    x, h, y = place[0], place[1], place[2]

    def put_x(ref, half, dx):
        at = pl.multiple_of(half * 768, 768)
        col = pl.multiple_of(((x + dx) % 4) * 256, 256)
        return pltpu.make_async_copy(ref, xbuf.at[pl.ds(at, 768), pl.ds(col, 256)], sem.at[0])

    def put_g(ref, dy, lo, n):
        at = pl.multiple_of(((y + dy) % 4) * 256 + lo, 128)
        return pltpu.make_async_copy(ref, gbuf.at[pl.ds(at, n)], sem.at[1])

    for copy in (
        put_x(x0.at[0], h, 0),
        put_x(x0.at[1], 1 - h, 0),
        put_x(xa.at[0], h, 3),
        put_x(xa.at[1], 1 - h, 3),
        put_x(xb.at[0], h, 1),
        put_x(xb.at[1], 1 - h, 1),
        put_x(xc, h, 2),
        put_x(xd, 1 - h, 2),
        put_g(g0, 0, 0, 256),
        put_g(ga, 3, 0, 256),
        put_g(gb, 1, 0, 256),
        put_g(gc, 2, 0, 128),
        put_g(gd, 2, 128, 128),
    ):
        copy.start()
    pltpu.make_async_copy(xbuf, xbuf, sem.at[0]).wait()
    pltpu.make_async_copy(gbuf, gbuf, sem.at[1]).wait()
    for col in range(0, gbuf.shape[1], 384):
        g = gbuf[:, col : col + 384]
        send_ref[:, col : col + 384] = jnp.dot(
            xbuf[:768, :], g, preferred_element_type=F32
        ).astype(BF)
        keep_ref[:, col : col + 384] = jnp.dot(xbuf[768:, :], g, preferred_element_type=F32)


def outer(place, xs, gs):
    m = gs[0].shape[1]
    return pl.pallas_call(
        outer_kernel,
        grid_spec=pltpu.PrefetchScalarGridSpec(
            num_scalar_prefetch=1,
            grid=(),
            in_specs=[pl.BlockSpec(memory_space=pl.ANY)] * 10,
            out_specs=[pl.BlockSpec(memory_space=pltpu.VMEM)] * 2,
            scratch_shapes=[
                pltpu.VMEM((1536, 1024), BF),
                pltpu.VMEM((1024, m), BF),
                pltpu.SemaphoreType.DMA((2,)),
            ],
        ),
        out_shape=[jax.ShapeDtypeStruct((768, m), BF), jax.ShapeDtypeStruct((768, m), F32)],
        compiler_params=pltpu.CompilerParams(vmem_limit_bytes=32 * 2**20),
        cost_estimate=pl.CostEstimate(
            flops=2 * 1536 * 1024 * m, bytes_accessed=12 * 2**20, transcendentals=0
        ),
        name="outer",
    )(place, *xs, *gs)


def slot_rows(route):
    same = route[:, None] == route[None, :]
    earlier = jnp.arange(16)[None, :] < jnp.arange(16)[:, None]
    rank = jnp.sum((same & earlier).astype(jnp.int32), axis=1)
    rows = (route * (MOST * LMAX) + rank * LMAX)[:, None] + jnp.arange(LMAX)[None, :]
    return rows.reshape(-1)


def body(queries, responses, cache_pool, page_table, lengths, routes, student_rows, projection):
    gi = lax.axis_index("grp")
    ti = lax.axis_index("tp")
    z, y, c = gi // 8, (gi // 2) % 4, gi % 2
    h, x = ti // 4, ti % 4
    place = jnp.stack([x, h, y]).astype(jnp.int32)
    route = routes[0, :, 0]
    all_routes = lax.all_gather(route, "grp", tiled=True)

    rows = student_rows[0].reshape(-1, student_rows.shape[-1])
    share = pick(rows, place)
    share = lax.all_to_all(share, "grp", split_axis=0, concat_axis=0, tiled=True)

    predicted = predict(rows, projection)
    predicted = lax.all_to_all(predicted, "grp", split_axis=0, concat_axis=0, tiled=True)

    tap = attention(
        queries[0].reshape(256, -1), responses[0].reshape(256, -1), cache_pool, page_table[0]
    )

    shared_prompt = z * 8 + x * 2 + c
    shared_route = lax.dynamic_slice_in_dim(all_routes, shared_prompt * 16, 16)
    mine = compact(slot_rows(shared_route)[None, :], share)
    other = lax.ppermute(mine, "tp", H_SWAP)
    x0 = jnp.stack([mine, other])
    xa = lax.ppermute(x0, "tp", x_shift(1))
    xb = lax.ppermute(x0, "tp", x_shift(-1))
    xc = lax.ppermute(xa[0], "tp", x_shift(1))
    xd = lax.ppermute(xb[1], "tp", x_shift(-1))

    my_lengths = lax.dynamic_index_in_dim(lengths, gi, 0, keepdims=False)
    hits = (route[:, None] == all_routes[None, :]).astype(F32)
    count = jnp.sum(hits * lengths.reshape(1, -1).astype(F32), axis=1)
    live = (jnp.arange(LMAX)[None, :] < my_lengths[:, None]).astype(F32)
    weight = (live * (1.0 / count)[:, None]).reshape(-1, 1)
    g0 = grad_pred(slot_rows(route)[:, None], weight, predicted, tap)
    ga = lax.ppermute(g0, "grp", y_shift(1))
    gb = lax.ppermute(g0, "grp", y_shift(-1))
    gc = lax.ppermute(ga[:128], "grp", y_shift(1))
    gd = lax.ppermute(gb[128:], "grp", y_shift(-1))

    send, keep = outer(place, (x0, xa, xb, xc, xd), (g0, ga, gb, gc, gd))
    total = keep + lax.ppermute(send, "grp", C_SWAP).astype(F32)
    got = lax.ppermute(total[:384].astype(BF), "grp", Z_SWAP)
    return (total[384:] + got.astype(F32)).astype(BF)


def solution(mesh):
    return jax.shard_map(
        body,
        mesh=mesh,
        in_specs=(
            P("grp", None, None, "tp"),
            P("grp", None, None, "tp"),
            P("grp", None, "tp"),
            P("grp", None),
            P(),
            P("grp", None, None),
            P("grp", None, None, None),
            P(None, "tp"),
        ),
        out_specs=P("grp", "tp"),
        check_vma=False,
    )
```

time: 306 us -> 184 us (0.60)
  waiting for transfers between devices: 184 us -> 57.2 us
  Pallas kernels: 0 us -> 61.4 us
  matrix products: 46.6 us -> 0 us
  local copies, waits for them, and re-layouts: 33.9 us -> 12.6 us
  starting transfers between devices: 13.1 us -> 32.7 us
  blocking collectives: 0 us -> 14.8 us
  between operations: 14.3 us -> 0.83 us
  other arithmetic: 12.4 us -> 4.08 us
    psum x1 -> x0, waiting for transfers between devices: 168 us -> none  [body(): lax.psum(partial_value.astype(jnp.bfloat16), 'grp').astype(jnp.float32)]
    pallas_call x0 -> x6, Pallas kernels: none -> 61.4 us  [the longest x1 25.7 us: pick(): pl.pallas_call(pick_kernel, grid_spec=pltpu.PrefetchScalarGridSpec(num_sc...]
    ppermute x0 -> x11, waiting for transfers between devices: none -> 57.2 us  [the longest x1 20.2 us: body(): got = lax.ppermute(total[:384].astype(BF), 'grp', Z_SWAP)]
    dot_general x7 -> x0, matrix products: 46.6 us -> none  [the longest x1 27.6 us: body(): lax.dot_general(full_rows, grad_pred, (((0,), (0,)), ((), ())), preferred...]
    ppermute x0 -> x11, starting transfers between devices: none -> 19.1 us  [the longest x1 3.48 us: body(): gd = lax.ppermute(gb[128:], 'grp', y_shift(-1))]
    gather x3 -> x0, local copies, waits for them, and re-layouts: 17 us -> none  [body(): jnp.take(cache_pool, page_table[0], axis=0)]
    all_to_all x2, waiting for transfers between devices: 15.8 us -> 0.01 us  [the longest x1 0.01 us: body(): lax.all_to_all(share, 'grp', split_axis=0, concat_axis=0, tiled=True)]
    unnamed x0 -> x1, blocking collectives: none -> 14.8 us
  transfers between devices with their start and end apart: 3 -> 13, of which waited for: 2 -> 6; matrix products, arithmetic and copies ran while one was open for 18% -> 3% of each run, Pallas kernels for 0% -> 16%
where the time goes in v1:
time: 184 us
  Pallas kernels  61.4 us (33%)
  waiting for transfers between devices  57.2 us (31%)
  starting transfers between devices  32.7 us (18%)
  blocking collectives  14.8 us (8%)
  local copies, waits for them, and re-layouts  12.6 us (7%)
  other arithmetic  4.08 us (2%)
    pallas_call x1, Pallas kernels, pick(): pl.pallas_call(pick_kernel, grid_spec=pltpu.PrefetchScalarGridSpec(num_sc...  25.7 us
    ppermute x1, waiting for transfers between devices, body(): got = lax.ppermute(total[:384].astype(BF), 'grp', Z_SWAP)  20.2 us
    ppermute x1, waiting for transfers between devices, body(): other = lax.ppermute(mine, 'tp', H_SWAP)  19.7 us
    unnamed x1, blocking collectives  14.8 us
    pallas_call x1, Pallas kernels, attention(): pl.pallas_call(functools.partial(attention_kernel, chunk=chunk), grid_spe...  12.9 us
    pallas_call x1, Pallas kernels, predict(): pl.pallas_call(predict_kernel, grid=(k // block,), in_specs=[pl.BlockSpec...  12.9 us
    unnamed x22, local copies, waits for them, and re-layouts  9.4 us
    all_to_all x1, starting transfers between devices, body(): lax.all_to_all(share, 'grp', split_axis=0, concat_axis=0, tiled=True)  7.35 us
  transfers between devices with their start and end apart: 13, of which 6 were waited for; matrix products, arithmetic and copies ran while one was open for 3% of the time, Pallas kernels for 16%

profile of v1, /device:TPU:1, one launch (start us, length us, event | category | flops | bytes accessed | tf_op | source)
XLA Modules:
  0.0 183.7 jit_solution(16635516427163684303)
XLA Ops:
  0.0 0.6 pad_add_fusion.place
  0.7 25.7 %pick.1 = bf16[512,768]{1,0:T(8,128)(2,1)} custom-call(s32[3]{0:T(128)} %pad_add_fusion.place, bf16[512,6144]{1,0:T(8,128)(2,1)} %bitcast.23), custom_call_target="tpu_custom_call" | custom-call | tf_op jit(solution)/shard_map/pick/pallas_call | solution.py:183
  26.4 7.4 %all-to-all-start = ((bf16[16,32,768]{2,1,0:T(8,128)(2,1)}), bf16[16,32,768]{2,1,0:T(8,128)(2,1)S(1)}, u32[]{:S(2)}, u32[]{:S(2)}) async-start(bf16[16,32,768]{2,1,0:T(8,128)(2,1)} %bitcast.29), calls=%async_computation | async-start | bytes 1572864 | tf_op jit(solution)/shard_map/all_to_all | solution.py:318
  33.7 0.0 copy-done.8
  33.8 0.2 convert_reduce_fusion
  33.9 0.0 copy-done.9
  33.9 0.6 dynamic-slice.1
  35.2 0.1 multiply_add_fusion
  35.3 14.8 %all-reduce = s32[256]{0:T(256)S(1)} all-reduce(s32[256]{0:T(256)S(1)} %get-tuple-element.10), channel_id=2, replica_groups=mesh['tp'=8,'grp'=16] {'grp'}, use_global_device_ids=true, to_apply=%add | all-reduce | flops 256 | bytes 2048
  50.1 0.1 dynamic-slice.2
  50.2 0.2 convert_reduce_fusion.1
  50.4 0.1 multiply_add_fusion.1
  50.5 0.1 iota_add_fusion.1
  50.5 0.7 add.93.slot_ref
  51.2 0.0 copy-done.7
  51.2 0.1 convert_element_type.32
  51.3 0.2 select_reduce_fusion
  51.5 0.0 copy-start
  51.5 2.8 %copy-done = bf16[1,32,16,6144]{3,2,1,0:T(8,128)(2,1)S(1)} copy-done((bf16[1,32,16,6144]{3,2,1,0:T(8,128)(2,1)S(1)}, bf16[1,32,16,6144]{3,2,1,0:T(8,128)(2,1)}, u32[]{:S(2)}) %copy-start) | copy-done | bytes 6291480
  54.3 5.0 %copy-done.2 = bf16[6144,1152]{1,0:T(8,128)(2,1)S(1)} copy-done((bf16[6144,1152]{1,0:T(8,128)(2,1)S(1)}, bf16[6144,1152]{1,0:T(8,128)(2,1)}, u32[]{:S(2)}) %copy-start.2) | copy-done | bytes 14155800
  59.3 12.9 %predict.1 = bf16[512,1152]{1,0:T(8,128)(2,1)} custom-call(bf16[512,6144]{1,0:T(8,128)(2,1)S(1)} %bitcast.24, bf16[6144,1152]{1,0:T(8,128)(2,1)S(1)} %copy-done.2), custom_call_target="tpu_custom_call" | custom-call | flops 7247757312 | bytes 21626880 | tf_op jit(solution)/shard_map/predict/pallas_call | solution.py:144
  72.2 0.0 all-to-all-done
  72.2 6.3 %all-to-all-start.1 = ((bf16[16,32,1152]{2,1,0:T(8,128)(2,1)}), bf16[16,32,1152]{2,1,0:T(8,128)(2,1)S(1)}, u32[]{:S(2)}, u32[]{:S(2)}) async-start(bf16[16,32,1152]{2,1,0:T(8,128)(2,1)} %bitcast.13), calls=%async_computation.1 | async-start | bytes 2359296 | tf_op jit(solution)/shard_map/all_to_all | solution.py:321
  78.5 0.0 copy-done.6
  78.5 2.3 %compact.1 = bf16[768,256]{1,0:T(8,128)(2,1)} custom-call(s32[1,256]{1,0:T(1,128)} %add.93.slot_ref, bf16[512,768]{1,0:T(8,128)(2,1)} %bitcast.30), custom_call_target="tpu_custom_call" | custom-call | flops 201326592 | bytes 2097152 | tf_op jit(solution)/shard_map/compact/pallas_call | solution.py:207
  80.8 3.3 %collective-permute-start = (bf16[768,256]{1,0:T(8,128)(2,1)}, bf16[768,256]{1,0:T(8,128)(2,1)S(1)}, u32[]{:S(2)}, u32[]{:S(2)}) collective-permute-start(bf16[768,256]{1,0:T(8,128)(2,1)} %compact.1), channel_id=1, source_target_pairs={{0,64},{16,80},{32,96},{48,112},{64,0},{80,16},{96,32},{112,48},{1... | collective-permute-start | bytes 1179656 | tf_op jit(solution)/shard_map/ppermute | solution.py:330
  84.2 0.1 fusion.3
  84.2 0.1 mul.59.weight_ref
  84.3 19.7 %collective-permute-done = bf16[768,256]{1,0:T(8,128)(2,1)S(1)} collective-permute-done((bf16[768,256]{1,0:T(8,128)(2,1)}, bf16[768,256]{1,0:T(8,128)(2,1)S(1)}, u32[]{:S(2)}, u32[]{:S(2)}) %collective-permute-start) | collective-permute-done | bytes 393248 | tf_op jit(solution)/shard_map/ppermute | solution.py:330
  104.0 1.1 pad_maximum_fusion.x0
  105.1 2.5 %collective-permute-start.2 = (bf16[2,768,256]{2,1,0:T(8,128)(2,1)S(1)}, bf16[2,768,256]{2,1,0:T(8,128)(2,1)}, u32[]{:S(2)}, u32[]{:S(2)}) collective-permute-start(bf16[2,768,256]{2,1,0:T(8,128)(2,1)S(1)} %pad_maximum_fusion.x0), channel_id=1, source_target_pairs={{0,48},{16,0},{32,16},{48,32},{64,112},{80,64},{96,80},{112,96},{1... | collective-permute-start | bytes 2359304 | tf_op jit(solution)/shard_map/ppermute | solution.py:333
  107.6 0.1 iota_add_fusion
  107.7 0.1 add.103.slot_ref
  107.8 0.1 collective-permute-start.1
  107.9 0.0 copy-done.3
  107.9 0.0 copy-start.4
  107.9 0.9 copy-done.4
  108.9 12.9 %attention.1.tap_ref = bf16[256,1152]{1,0:T(8,128)(2,1)S(1)} custom-call(s32[64]{0:T(128)S(1)} %bitcast.28, bf16[256,1152]{1,0:T(8,128)(2,1)S(1)} %bitcast.26, bf16[256,384]{1,0:T(8,128)(2,1)S(1)} %bitcast.27, bf16[128,64,384]{2,1,0:T(8,128)(2,1)} %pool_ref.1), custom_call_target="tpu_custom_call" | custom-call | flops 6845104128 | bytes 8388608 | tf_op jit(solution)/shard_map/attention/pallas_call | solution.py:94
  121.8 0.0 all-to-all-done.1
  121.8 0.6 grad_pred.1.g0
  122.3 2.5 %collective-permute-start.6 = (bf16[256,1152]{1,0:T(8,128)(2,1)S(1)}, bf16[256,1152]{1,0:T(8,128)(2,1)S(1)}, u32[]{:S(2)}, u32[]{:S(2)}) collective-permute-start(bf16[256,1152]{1,0:T(8,128)(2,1)S(1)} %grad_pred.1.g0), channel_id=1, source_target_pairs={{0,6},{1,7},{2,0},{3,1},{4,2},{5,3},{6,4},{7,5},{8,14},{9,15},{10,... | collective-permute-start | bytes 1769480 | tf_op jit(solution)/shard_map/ppermute | solution.py:344
  124.8 0.0 collective-permute-start.5
  124.9 0.0 collective-permute-done.2.xb
  124.9 1.0 slice_bitcast_fusion
  125.9 2.7 %collective-permute-start.4 = (bf16[768,256]{1,0:T(8,128)(2,1)S(1)}, bf16[768,256]{1,0:T(8,128)(2,1)S(1)}, u32[]{:S(2)}, u32[]{:S(2)}) collective-permute-start(bf16[768,256]{1,0:T(8,128)(2,1)S(1)} %slice_bitcast_fusion), channel_id=1, source_target_pairs={{0,48},{16,0},{32,16},{48,32},{64,112},{80,64},{96,80},{112,96},{1... | collective-permute-start | bytes 1179656 | tf_op jit(solution)/shard_map/ppermute | solution.py:335
  128.6 0.0 collective-permute-done.1.xa
  128.6 1.0 slice_bitcast_fusion.1
  129.6 0.1 collective-permute-start.3
  129.7 6.6 %collective-permute-done.6.gb = bf16[256,1152]{1,0:T(8,128)(2,1)S(1)} collective-permute-done((bf16[256,1152]{1,0:T(8,128)(2,1)S(1)}, bf16[256,1152]{1,0:T(8,128)(2,1)S(1)}, u32[]{:S(2)}, u32[]{:S(2)}) %collective-permute-start.6) | collective-permute-done | bytes 589856 | tf_op jit(solution)/shard_map/ppermute | solution.py:344
  136.3 3.5 %collective-permute-start.8 = (bf16[128,1152]{1,0:T(8,128)(2,1)S(1)}, bf16[128,1152]{1,0:T(8,128)(2,1)S(1)}, u32[]{:S(2)}, u32[]{:S(2)}) collective-permute-start(bf16[128,1152]{1,0:T(8,128)(2,1)S(1)} %slice.28), channel_id=1, source_target_pairs={{0,6},{1,7},{2,0},{3,1},{4,2},{5,3},{6,4},{7,5},{8,14},{9,15},{10,... | collective-permute-start | bytes 884744 | tf_op jit(solution)/shard_map/ppermute | solution.py:346
  139.8 0.0 collective-permute-done.5.ga
  139.8 0.3 collective-permute-start.7
  140.1 3.9 %collective-permute-done.8.gd = bf16[128,1152]{1,0:T(8,128)(2,1)S(1)} collective-permute-done((bf16[128,1152]{1,0:T(8,128)(2,1)S(1)}, bf16[128,1152]{1,0:T(8,128)(2,1)S(1)}, u32[]{:S(2)}, u32[]{:S(2)}) %collective-permute-start.8) | collective-permute-done | bytes 294944 | tf_op jit(solution)/shard_map/ppermute | solution.py:346
  144.0 3.4 %collective-permute-done.7.gc = bf16[128,1152]{1,0:T(8,128)(2,1)S(1)} collective-permute-done((bf16[128,1152]{1,0:T(8,128)(2,1)S(1)}, bf16[128,1152]{1,0:T(8,128)(2,1)S(1)}, u32[]{:S(2)}, u32[]{:S(2)}) %collective-permute-start.7) | collective-permute-done | bytes 294944 | tf_op jit(solution)/shard_map/ppermute | solution.py:345
  147.5 0.0 collective-permute-done.4.xd
  147.5 0.0 collective-permute-done.3.xc
  147.5 7.1 %outer.1 = (bf16[768,1152]{1,0:T(8,128)(2,1)S(1)}, f32[768,1152]{1,0:T(8,128)S(1)}) custom-call(s32[3]{0:T(128)S(1)} %copy-done.1, bf16[2,768,256]{2,1,0:T(8,128)(2,1)S(1)} %pad_maximum_fusion.x0, bf16[2,768,256]{2,1,0:T(8,128)(2,1)} %collective-permute-done.1.xa, bf16[2,768,256]{2,1,0:T(8,128)(2,1)} %collective-permute-done.2.xb, ...), custom_call_target="tpu_custom_call" | custom-call | flops 3623878656 | bytes 12582912 | tf_op jit(solution)/shard_map/outer/pallas_call | solution.py:277
  154.6 3.4 %collective-permute-start.9 = (bf16[768,1152]{1,0:T(8,128)(2,1)S(1)}, bf16[768,1152]{1,0:T(8,128)(2,1)S(1)}, u32[]{:S(2)}, u32[]{:S(2)}) collective-permute-start(bf16[768,1152]{1,0:T(8,128)(2,1)S(1)} %get-tuple-element.8), channel_id=1, source_target_pairs={{0,1},{1,0},{2,3},{3,2},{4,5},{5,4},{6,7},{7,6},{8,9},{9,8},{10,11... | collective-permute-start | bytes 5308424 | tf_op jit(solution)/shard_map/ppermute | solution.py:349
  157.9 3.3 %collective-permute-done.9 = bf16[768,1152]{1,0:T(8,128)(2,1)S(1)} collective-permute-done((bf16[768,1152]{1,0:T(8,128)(2,1)S(1)}, bf16[768,1152]{1,0:T(8,128)(2,1)S(1)}, u32[]{:S(2)}, u32[]{:S(2)}) %collective-permute-start.9) | collective-permute-done | bytes 1769504 | tf_op jit(solution)/shard_map/ppermute | solution.py:349
  161.2 0.3 convert_add_fusion
  161.5 0.1 slice.37
  161.6 0.7 collective-permute-start.10
  162.3 20.2 %collective-permute-done.10 = bf16[384,1152]{1,0:T(8,128)(2,1)S(1)} collective-permute-done((bf16[384,1152]{1,0:T(8,128)(2,1)S(1)}, bf16[384,1152]{1,0:T(8,128)(2,1)S(1)}, u32[]{:S(2)}, u32[]{:S(2)}) %collective-permute-start.10) | collective-permute-done | bytes 884768 | tf_op jit(solution)/shard_map/ppermute | solution.py:350
  182.6 1.1 fusion
  (16 shorter events, 0.1 us)
Async XLA Ops:
  0.6 33.1 %copy-start.8 = (s32[1,16,1]{1,2,0:T(1,128)S(1)}, s32[1,16,1]{1,2,0:T(1,128)}, u32[]{:S(2)}) copy-start(s32[1,16,1]{1,2,0:T(1,128)} %param.13) | copy-start | bytes 196
  0.6 33.3 %copy-start.9 = (u32[128]{0:T(128)S(1)}, u32[128]{0:T(128)}, u32[]{:S(2)}) copy-start(u32[128]{0:T(128)} %constant.92) | copy-start | bytes 1540
  0.6 50.6 %copy-start.7 = (s32[16,16]{1,0:T(8,128)S(1)}, s32[16,16]{1,0:T(8,128)}, u32[]{:S(2)}) copy-start(s32[16,16]{1,0:T(8,128)} %param.12) | copy-start | bytes 3076
  26.4 45.8 %all-to-all-start = ((bf16[16,32,768]{2,1,0:T(8,128)(2,1)}), bf16[16,32,768]{2,1,0:T(8,128)(2,1)S(1)}, u32[]{:S(2)}, u32[]{:S(2)}) async-start(bf16[16,32,768]{2,1,0:T(8,128)(2,1)} %bitcast.29), calls=%async_computation | async-start | bytes 1572864 | tf_op jit(solution)/shard_map/all_to_all | solution.py:318
  51.5 2.8 %copy-start = (bf16[1,32,16,6144]{3,2,1,0:T(8,128)(2,1)S(1)}, bf16[1,32,16,6144]{3,2,1,0:T(8,128)(2,1)}, u32[]{:S(2)}) copy-start(bf16[1,32,16,6144]{3,2,1,0:T(8,128)(2,1)} %param.14) | copy-start | bytes 18874372
  54.3 5.0 %copy-start.2 = (bf16[6144,1152]{1,0:T(8,128)(2,1)S(1)}, bf16[6144,1152]{1,0:T(8,128)(2,1)}, u32[]{:S(2)}) copy-start(bf16[6144,1152]{1,0:T(8,128)(2,1)} %p_ref.1) | copy-start | bytes 42467332
  72.2 35.7 %copy-start.3 = (bf16[1,16,16,1152]{3,2,1,0:T(8,128)(2,1)S(1)}, bf16[1,16,16,1152]{3,2,1,0:T(8,128)(2,1)}, u32[]{:S(2)}) copy-start(bf16[1,16,16,1152]{3,2,1,0:T(8,128)(2,1)} %param.8) | copy-start | bytes 1769476
  72.2 35.7 %copy-start.5 = (s32[1,64]{1,0:T(1,128)S(1)}, s32[1,64]{1,0:T(1,128)}, u32[]{:S(2)}) copy-start(s32[1,64]{1,0:T(1,128)} %param.11) | copy-start | bytes 772
  72.2 6.3 %copy-start.6 = (bf16[16,32,768]{2,1,0:T(8,128)(2,1)}, bf16[16,32,768]{2,1,0:T(8,128)(2,1)S(1)}, u32[]{:S(2)}) copy-start(bf16[16,32,768]{2,1,0:T(8,128)(2,1)S(1)} %all-to-all-done) | copy-start | bytes 2359300
  72.2 49.6 %all-to-all-start.1 = ((bf16[16,32,1152]{2,1,0:T(8,128)(2,1)}), bf16[16,32,1152]{2,1,0:T(8,128)(2,1)S(1)}, u32[]{:S(2)}, u32[]{:S(2)}) async-start(bf16[16,32,1152]{2,1,0:T(8,128)(2,1)} %bitcast.13), calls=%async_computation.1 | async-start | bytes 2359296 | tf_op jit(solution)/shard_map/all_to_all | solution.py:321
  80.8 23.2 %collective-permute-start = (bf16[768,256]{1,0:T(8,128)(2,1)}, bf16[768,256]{1,0:T(8,128)(2,1)S(1)}, u32[]{:S(2)}, u32[]{:S(2)}) collective-permute-start(bf16[768,256]{1,0:T(8,128)(2,1)} %compact.1), channel_id=1, source_target_pairs={{0,64},{16,80},{32,96},{48,112},{64,0},{80,16},{96,32},{112,48},{1... | collective-permute-start | bytes 1179656 | tf_op jit(solution)/shard_map/ppermute | solution.py:330
  105.1 19.8 %collective-permute-start.2 = (bf16[2,768,256]{2,1,0:T(8,128)(2,1)S(1)}, bf16[2,768,256]{2,1,0:T(8,128)(2,1)}, u32[]{:S(2)}, u32[]{:S(2)}) collective-permute-start(bf16[2,768,256]{2,1,0:T(8,128)(2,1)S(1)} %pad_maximum_fusion.x0), channel_id=1, source_target_pairs={{0,48},{16,0},{32,16},{48,32},{64,112},{80,64},{96,80},{112,96},{1... | collective-permute-start | bytes 2359304 | tf_op jit(solution)/shard_map/ppermute | solution.py:333
  107.8 20.8 %collective-permute-start.1 = (bf16[2,768,256]{2,1,0:T(8,128)(2,1)S(1)}, bf16[2,768,256]{2,1,0:T(8,128)(2,1)}, u32[]{:S(2)}, u32[]{:S(2)}) collective-permute-start(bf16[2,768,256]{2,1,0:T(8,128)(2,1)S(1)} %pad_maximum_fusion.x0), channel_id=1, source_target_pairs={{0,16},{16,32},{32,48},{48,0},{64,80},{80,96},{96,112},{112,64},{1... | collective-permute-start | bytes 2359304 | tf_op jit(solution)/shard_map/ppermute | solution.py:332
  107.9 0.9 copy-start.4
  121.7 25.7 %copy-start.1 = (s32[3]{0:T(128)S(1)}, s32[3]{0:T(128)}, u32[]{:S(2)}) copy-start(s32[3]{0:T(128)} %pad_add_fusion.place) | copy-start | bytes 40
  122.3 14.0 %collective-permute-start.6 = (bf16[256,1152]{1,0:T(8,128)(2,1)S(1)}, bf16[256,1152]{1,0:T(8,128)(2,1)S(1)}, u32[]{:S(2)}, u32[]{:S(2)}) collective-permute-start(bf16[256,1152]{1,0:T(8,128)(2,1)S(1)} %grad_pred.1.g0), channel_id=1, source_target_pairs={{0,6},{1,7},{2,0},{3,1},{4,2},{5,3},{6,4},{7,5},{8,14},{9,15},{10,... | collective-permute-start | bytes 1769480 | tf_op jit(solution)/shard_map/ppermute | solution.py:344
  124.8 15.0 %collective-permute-start.5 = (bf16[256,1152]{1,0:T(8,128)(2,1)S(1)}, bf16[256,1152]{1,0:T(8,128)(2,1)S(1)}, u32[]{:S(2)}, u32[]{:S(2)}) collective-permute-start(bf16[256,1152]{1,0:T(8,128)(2,1)S(1)} %grad_pred.1.g0), channel_id=1, source_target_pairs={{0,2},{1,3},{2,4},{3,5},{4,6},{5,7},{6,0},{7,1},{8,10},{9,11},{10,... | collective-permute-start | bytes 1769480 | tf_op jit(solution)/shard_map/ppermute | solution.py:343
  125.9 21.6 %collective-permute-start.4 = (bf16[768,256]{1,0:T(8,128)(2,1)S(1)}, bf16[768,256]{1,0:T(8,128)(2,1)S(1)}, u32[]{:S(2)}, u32[]{:S(2)}) collective-permute-start(bf16[768,256]{1,0:T(8,128)(2,1)S(1)} %slice_bitcast_fusion), channel_id=1, source_target_pairs={{0,48},{16,0},{32,16},{48,32},{64,112},{80,64},{96,80},{112,96},{1... | collective-permute-start | bytes 1179656 | tf_op jit(solution)/shard_map/ppermute | solution.py:335
  129.6 17.8 %collective-permute-start.3 = (bf16[768,256]{1,0:T(8,128)(2,1)S(1)}, bf16[768,256]{1,0:T(8,128)(2,1)S(1)}, u32[]{:S(2)}, u32[]{:S(2)}) collective-permute-start(bf16[768,256]{1,0:T(8,128)(2,1)S(1)} %slice_bitcast_fusion.1), channel_id=1, source_target_pairs={{0,16},{16,32},{32,48},{48,0},{64,80},{80,96},{96,112},{112,64},{1... | collective-permute-start | bytes 1179656 | tf_op jit(solution)/shard_map/ppermute | solution.py:334
  136.3 7.7 %collective-permute-start.8 = (bf16[128,1152]{1,0:T(8,128)(2,1)S(1)}, bf16[128,1152]{1,0:T(8,128)(2,1)S(1)}, u32[]{:S(2)}, u32[]{:S(2)}) collective-permute-start(bf16[128,1152]{1,0:T(8,128)(2,1)S(1)} %slice.28), channel_id=1, source_target_pairs={{0,6},{1,7},{2,0},{3,1},{4,2},{5,3},{6,4},{7,5},{8,14},{9,15},{10,... | collective-permute-start | bytes 884744 | tf_op jit(solution)/shard_map/ppermute | solution.py:346
  139.8 7.6 %collective-permute-start.7 = (bf16[128,1152]{1,0:T(8,128)(2,1)S(1)}, bf16[128,1152]{1,0:T(8,128)(2,1)S(1)}, u32[]{:S(2)}, u32[]{:S(2)}) collective-permute-start(bf16[128,1152]{1,0:T(8,128)(2,1)S(1)} %slice.27), channel_id=1, source_target_pairs={{0,2},{1,3},{2,4},{3,5},{4,6},{5,7},{6,0},{7,1},{8,10},{9,11},{10,... | collective-permute-start | bytes 884744 | tf_op jit(solution)/shard_map/ppermute | solution.py:345
  154.6 6.7 %collective-permute-start.9 = (bf16[768,1152]{1,0:T(8,128)(2,1)S(1)}, bf16[768,1152]{1,0:T(8,128)(2,1)S(1)}, u32[]{:S(2)}, u32[]{:S(2)}) collective-permute-start(bf16[768,1152]{1,0:T(8,128)(2,1)S(1)} %get-tuple-element.8), channel_id=1, source_target_pairs={{0,1},{1,0},{2,3},{3,2},{4,5},{5,4},{6,7},{7,6},{8,9},{9,8},{10,11... | collective-permute-start | bytes 5308424 | tf_op jit(solution)/shard_map/ppermute | solution.py:349
  161.6 20.9 %collective-permute-start.10 = (bf16[384,1152]{1,0:T(8,128)(2,1)S(1)}, bf16[384,1152]{1,0:T(8,128)(2,1)S(1)}, u32[]{:S(2)}, u32[]{:S(2)}) collective-permute-start(bf16[384,1152]{1,0:T(8,128)(2,1)S(1)} %slice.37), channel_id=1, source_target_pairs={{0,8},{1,9},{2,10},{3,11},{4,12},{5,13},{6,14},{7,15},{8,0},{9,1},... | collective-permute-start | bytes 2654216 | tf_op jit(solution)/shard_map/ppermute | solution.py:350

commit v2 on v1

v2 whole, which is shorter than its diff:
```python
import functools

import jax
import jax.numpy as jnp
from jax import lax
from jax.experimental import pallas as pl
from jax.experimental.pallas import tpu as pltpu
from jax.sharding import PartitionSpec as P

HD = 192
MOST = 2
GQA = 6
PAGE = 64
LMAX = 16
LOG2E = 1.4426950408889634
BF = jnp.bfloat16
F32 = jnp.float32
ROUTE, LENGTH = 8, 24
MIB = 2**20

GRID = [(z, y, c) for z in range(2) for y in range(4) for c in range(2)]
TPGRID = [(h, x) for h in range(2) for x in range(4)]


def grp_at(z, y, c):
    return z * 8 + (y % 4) * 2 + c


def y_shift(step):
    return [(grp_at(z, y, c), grp_at(z, y + step, c)) for z, y, c in GRID]


Z_SWAP = [(grp_at(z, y, c), grp_at(1 - z, y, c)) for z, y, c in GRID]
C_SWAP = [(grp_at(z, y, c), grp_at(z, y, 1 - c)) for z, y, c in GRID]
H_SWAP = [(h * 4 + x, (1 - h) * 4 + x) for h, x in TPGRID]


def x_shift(step):
    return [(h * 4 + x, h * 4 + (x + step) % 4) for h, x in TPGRID]


def attention_kernel(table, q_ref, resp_ref, pool_ref, out_ref, kv, q2, acc, tops, *, chunk, mb):
    pages = table.shape[0]
    n = q_ref.shape[0]
    heads = q_ref.shape[1] // HD
    scale = LOG2E * float(HD) ** -0.5
    pad = jnp.zeros((n, 256 - HD), BF)
    for i in range(heads):
        q2[i * n : (i + 1) * n, :] = jnp.concatenate([q_ref[:, i * HD : (i + 1) * HD], pad], 1)

    def fold(rows, first):
        kt = rows[:, 0:256].T
        values = rows[:, 128:384]
        lane = lax.broadcasted_iota(jnp.int32, values.shape, 1)
        vx = jnp.where(lane < 64, jnp.where(lane == 0, 1.0, 0.0).astype(BF), values)
        for lo in range(0, heads * n, mb):
            here = slice(lo, lo + mb)
            s = jnp.dot(q2[here, :], kt, preferred_element_type=F32)
            if first:
                row = lax.broadcasted_iota(jnp.int32, s.shape, 0) % n
                col = lax.broadcasted_iota(jnp.int32, s.shape, 1)
                s = jnp.where((row // LMAX == col // LMAX) & (col <= row), s, -1e30)
            new = jnp.max(s, axis=1, keepdims=True) * scale
            if not first:
                old = tops[here, 0:1]
                new = jnp.maximum(old, new)
            p = jnp.exp2(s * scale - new).astype(BF)
            o = jnp.dot(p, vx, preferred_element_type=F32)
            acc[here, :] = o if first else acc[here, :] * jnp.exp2(old - new) + o
            tops[here, :] = jnp.broadcast_to(new, (mb, 128))

    fold(resp_ref[...], True)
    for lo in range(0, pages * PAGE, chunk):
        for j in range(lo // PAGE, (lo + chunk) // PAGE):
            kv[j * PAGE : (j + 1) * PAGE, :] = pool_ref[table[j]]
        fold(kv[lo : lo + chunk, :], False)
    for i in range(0, heads, 2):
        ratios = []
        for j in (i, i + 1):
            total = acc[j * n : (j + 1) * n, :]
            ratios.append(total[:, 64:] / total[:, 0:1])
        out_ref[:, i * HD : (i + 2) * HD] = jnp.concatenate(ratios, 1).astype(BF)


def attention(q, resp, pool, table, chunk=2048, mb=256):
    n, width = q.shape
    keys = table.shape[0] * PAGE
    heads = width // HD
    return pl.pallas_call(
        functools.partial(attention_kernel, chunk=chunk, mb=mb),
        grid_spec=pltpu.PrefetchScalarGridSpec(
            num_scalar_prefetch=1,
            grid=(),
            in_specs=[pl.BlockSpec(memory_space=pltpu.VMEM)] * 3,
            out_specs=pl.BlockSpec(memory_space=pltpu.VMEM),
            scratch_shapes=[
                pltpu.VMEM((keys, 2 * HD), BF),
                pltpu.VMEM((heads * n, 256), BF),
                pltpu.VMEM((heads * n, 256), F32),
                pltpu.VMEM((heads * n, 128), F32),
            ],
        ),
        out_shape=jax.ShapeDtypeStruct((n, width), BF),
        compiler_params=pltpu.CompilerParams(vmem_limit_bytes=24 * MIB),
        cost_estimate=pl.CostEstimate(
            flops=4 * heads * n * (keys + n) * 256,
            bytes_accessed=8 * 2**20,
            transcendentals=heads * n * (keys + n),
        ),
        name="attention",
    )(table, q, resp, pool)


def predict_kernel(x_ref, p_ref, out_ref, acc):
    k = pl.program_id(0)
    part = jnp.dot(x_ref[...], p_ref[...], preferred_element_type=F32)

    @pl.when(k == 0)
    def _():
        acc[...] = part

    @pl.when(k > 0)
    def _():
        acc[...] += part

    @pl.when(k == pl.num_programs(0) - 1)
    def _():
        out_ref[...] = acc[...].astype(BF)


def predict(x, p, block=1536):
    n, k = x.shape
    m = p.shape[1]
    return pl.pallas_call(
        predict_kernel,
        grid=(k // block,),
        in_specs=[
            pl.BlockSpec((n, block), lambda i: (0, i)),
            pl.BlockSpec((block, m), lambda i: (i, 0)),
        ],
        out_specs=pl.BlockSpec((n, m), lambda i: (0, 0)),
        out_shape=jax.ShapeDtypeStruct((n, m), BF),
        scratch_shapes=[pltpu.VMEM((n, m), F32)],
        compiler_params=pltpu.CompilerParams(vmem_limit_bytes=52 * MIB),
        cost_estimate=pl.CostEstimate(
            flops=2 * n * m * k, bytes_accessed=2 * (n * k + k * m + n * m), transcendentals=0
        ),
        name="predict",
    )(x, p)


def pick_kernel(info, x_hbm, out_ref, x_ref, sem):
    x, h = info[0], info[1]
    for z, c in ((0, 0), (0, 1), (1, 0), (1, 1)):
        row = pl.multiple_of((z * 8 + x * 2 + c) * 32, 32)
        there = x_ref.at[pl.ds((z * 2 + c) * 32, 32)]
        pltpu.make_async_copy(x_hbm.at[pl.ds(row, 32)], there, sem).start()
    token = lax.broadcasted_iota(jnp.int32, (32, 128), 0) * 128
    token += lax.broadcasted_iota(jnp.int32, (32, 128), 1)
    mark = jnp.full((32, 128), 127, jnp.int32)
    for r in range(16):
        route = info[ROUTE + r]
        rank = jnp.int32(0)
        for earlier in range(r):
            rank += (info[ROUTE + earlier] == route).astype(jnp.int32)
        dead = jnp.where(token % LMAX < info[LENGTH + r], 0, 64)
        mark = jnp.where(token // LMAX == r, route * MOST + rank + dead, mark)
    mark = mark.astype(F32).astype(BF)
    pltpu.make_async_copy(x_ref, x_ref, sem).wait()

    for z, y, c in GRID:
        at = grp_at(z, y, c) * 32
        row = (z * 2 + c) * 32
        for i, zf in enumerate((1 - z, z)):
            block = zf * 8 + y * 2 + jnp.where(h == 0, 1 - c, c)
            col = pl.multiple_of(block * 384, 384)
            out_ref[at : at + 32, i * 384 : (i + 1) * 384] = x_ref[row : row + 32, pl.ds(col, 384)]
        out_ref[at : at + 32, 768:] = mark


def pick(info, x):
    return pl.pallas_call(
        pick_kernel,
        grid_spec=pltpu.PrefetchScalarGridSpec(
            num_scalar_prefetch=1,
            grid=(),
            in_specs=[pl.BlockSpec(memory_space=pl.ANY)],
            out_specs=pl.BlockSpec(memory_space=pltpu.VMEM),
            scratch_shapes=[pltpu.VMEM((128, x.shape[1]), BF), pltpu.SemaphoreType.DMA(())],
        ),
        out_shape=jax.ShapeDtypeStruct((512, 896), BF),
        compiler_params=pltpu.CompilerParams(vmem_limit_bytes=58 * MIB),
        cost_estimate=pl.CostEstimate(flops=0, bytes_accessed=3 * 2**20, transcendentals=0),
        name="pick",
    )(info, x)


def slot_of(mark):
    lane = lax.broadcasted_iota(jnp.int32, mark.shape, 1)
    return jnp.where(mark < 64, mark, mark - 64) * LMAX + lane % LMAX


def compact_kernel(info, x_ref, out_ref, meta_ref):
    def marks_of(prompt):
        at = pl.multiple_of(prompt * 32, 32)
        rows = x_ref[pl.ds(at, 32), 768:].astype(F32)
        return jnp.concatenate([rows[0:1], rows[1:2]], 1).astype(jnp.int32)

    slot = slot_of(marks_of(info[3]))
    rows = lax.broadcasted_iota(jnp.int32, (512, 256), 0)
    sel = (rows == slot).astype(F32).astype(BF)
    out_ref[...] = lax.dot_general(
        x_ref[:, :768], sel, (((0,), (0,)), ((), ())), preferred_element_type=F32
    ).astype(BF)

    every = x_ref[:, 768:].astype(F32)
    own = marks_of(info[4])
    weight = jnp.zeros(own.shape, F32)
    for s in range(16):
        hit = (every == 2.0 * s) | (every == 2.0 * s + 1.0)
        count = jnp.sum(jnp.sum(hit.astype(F32), axis=0, keepdims=True), axis=1, keepdims=True)
        weight = jnp.where((own == 2 * s) | (own == 2 * s + 1), 1.0 / count, weight)
    meta_ref[...] = jnp.concatenate(
        [slot_of(own).astype(F32), weight, jnp.zeros((6, 256), F32)], 0
    )


def compact(info, x):
    return pl.pallas_call(
        compact_kernel,
        grid_spec=pltpu.PrefetchScalarGridSpec(
            num_scalar_prefetch=1,
            grid=(),
            in_specs=[pl.BlockSpec(memory_space=pltpu.VMEM)],
            out_specs=[pl.BlockSpec(memory_space=pltpu.VMEM)] * 2,
        ),
        out_shape=[
            jax.ShapeDtypeStruct((768, 256), BF),
            jax.ShapeDtypeStruct((8, 256), F32),
        ],
        compiler_params=pltpu.CompilerParams(vmem_limit_bytes=12 * MIB),
        cost_estimate=pl.CostEstimate(
            flops=2 * 512 * 768 * 256, bytes_accessed=2 * 2**20, transcendentals=0
        ),
        name="compact",
    )(info, x)


def grad_kernel(meta_ref, y_ref, tap_ref, out_ref):
    n = y_ref.shape[0]
    meta = meta_ref[...].T
    cols = lax.broadcasted_iota(jnp.int32, (256, n), 1)
    sel = (cols == meta[:, 0:1].astype(jnp.int32)).astype(F32).astype(BF)
    predicted = jnp.dot(sel, y_ref[...], preferred_element_type=F32)
    out_ref[...] = ((predicted - tap_ref[...].astype(F32)) * meta[:, 1:2]).astype(BF)


def grad_pred(meta, y, tap):
    return pl.pallas_call(
        grad_kernel,
        in_specs=[pl.BlockSpec(memory_space=pltpu.VMEM)] * 3,
        out_specs=pl.BlockSpec(memory_space=pltpu.VMEM),
        out_shape=jax.ShapeDtypeStruct(tap.shape, BF),
        compiler_params=pltpu.CompilerParams(vmem_limit_bytes=16 * MIB),
        cost_estimate=pl.CostEstimate(
            flops=2 * 512 * 256 * tap.shape[1], bytes_accessed=3 * 2**20, transcendentals=0
        ),
        name="grad_pred",
    )(meta, y, tap)


def send_kernel(info, *refs):
    xs, gs, (out_ref, keep_ref, gbuf_ref, xbuf) = refs[:8], refs[8:13], refs[13:]
    x, h, y = info[0], info[1], info[2]
    for ref, dy, lo in zip(gs, (0, 1, 3, 2, 2), (0, 0, 0, 0, 128)):
        at = pl.multiple_of(((y + dy + 4 - x) % 4) * 256 + lo, 128)
        gbuf_ref[pl.ds(at, ref.shape[0]), :] = ref[...]
    for i in range(4):
        here = slice(i * 256, (i + 1) * 256)

        @pl.when(h == 0)
        def _():
            xbuf[:, here] = xs[i][...]
            keep_ref[:, here] = xs[4 + i][...]

        @pl.when(h == 1)
        def _():
            xbuf[:, here] = xs[4 + i][...]
            keep_ref[:, here] = xs[i][...]

    out_ref[...] = jnp.dot(xbuf[...], gbuf_ref[...], preferred_element_type=F32).astype(BF)


def outer_send(info, xs, gs):
    m = gs[0].shape[1]
    return pl.pallas_call(
        send_kernel,
        grid_spec=pltpu.PrefetchScalarGridSpec(
            num_scalar_prefetch=1,
            grid=(),
            in_specs=[pl.BlockSpec(memory_space=pltpu.VMEM)] * 13,
            out_specs=[pl.BlockSpec(memory_space=pltpu.VMEM)] * 3,
            scratch_shapes=[pltpu.VMEM((768, 1024), BF)],
        ),
        out_shape=[
            jax.ShapeDtypeStruct((768, m), BF),
            jax.ShapeDtypeStruct((768, 1024), BF),
            jax.ShapeDtypeStruct((1024, m), BF),
        ],
        compiler_params=pltpu.CompilerParams(vmem_limit_bytes=16 * MIB),
        cost_estimate=pl.CostEstimate(
            flops=2 * 768 * 1024 * m, bytes_accessed=8 * 2**20, transcendentals=0
        ),
        name="outer_send",
    )(info, *xs, *gs)


def keep_kernel(x_ref, g_ref, out_ref, *, lo):
    rows = out_ref.shape[0]
    out_ref[...] = jnp.dot(x_ref[lo : lo + rows, :], g_ref[...], preferred_element_type=F32)


def outer_keep(x, g, lo):
    m = g.shape[1]
    return pl.pallas_call(
        functools.partial(keep_kernel, lo=lo),
        in_specs=[pl.BlockSpec(memory_space=pltpu.VMEM)] * 2,
        out_specs=pl.BlockSpec(memory_space=pltpu.VMEM),
        out_shape=jax.ShapeDtypeStruct((384, m), F32),
        compiler_params=pltpu.CompilerParams(vmem_limit_bytes=16 * MIB),
        cost_estimate=pl.CostEstimate(
            flops=2 * 384 * 1024 * m, bytes_accessed=4 * 2**20, transcendentals=0
        ),
        name="outer_keep",
    )(x, g)


def body(queries, responses, cache_pool, page_table, lengths, routes, student_rows, projection):
    gi = lax.axis_index("grp")
    ti = lax.axis_index("tp")
    z, y, c = gi // 8, (gi // 2) % 4, gi % 2
    h, x = ti // 4, ti % 4
    my_lengths = lax.dynamic_index_in_dim(lengths, gi, 0, keepdims=False)
    own = jnp.stack([x, h, y, z * 8 + x * 2 + c, gi, gi, gi, gi]).astype(jnp.int32)
    info = jnp.concatenate([own, routes[0, :, 0], my_lengths])

    rows = student_rows[0].reshape(-1, student_rows.shape[-1])
    share = pick(info, rows)
    share = lax.all_to_all(share, "grp", split_axis=0, concat_axis=0, tiled=True)

    predicted = predict(rows, projection)
    mine, meta = compact(info, share)
    predicted, mine = lax.optimization_barrier((predicted, mine))
    predicted = lax.all_to_all(predicted, "grp", split_axis=0, concat_axis=0, tiled=True)

    other = lax.ppermute(mine, "tp", H_SWAP)
    ma = lax.ppermute(mine, "tp", x_shift(1))
    mb = lax.ppermute(mine, "tp", x_shift(-1))

    q = queries[0].reshape(256, -1)
    q, meta = lax.optimization_barrier((q, meta))
    tap = attention(q, responses[0].reshape(256, -1), cache_pool, page_table[0])
    other, ma, mb, tap = lax.optimization_barrier((other, ma, mb, tap))
    oa = lax.ppermute(other, "tp", x_shift(1))
    ob = lax.ppermute(other, "tp", x_shift(-1))
    mc = lax.ppermute(ma, "tp", x_shift(1))

    g = grad_pred(meta, predicted, tap)
    ga = lax.ppermute(g, "grp", y_shift(1))
    gb = lax.ppermute(g, "grp", y_shift(-1))
    ga, gb, ob = lax.optimization_barrier((ga, gb, ob))
    gc = lax.ppermute(ga[:128], "grp", y_shift(1))
    gd = lax.ppermute(gb[128:], "grp", y_shift(-1))
    oc = lax.ppermute(ob, "tp", x_shift(-1))
    xs = (mine, mb, mc, ma, other, ob, oc, oa)

    send, kept, grads = outer_send(info, xs, (g, gb, ga, gc, gd))
    got = lax.ppermute(send, "grp", C_SWAP)
    to_z = outer_keep(kept, grads, 0) + got[:384].astype(F32)
    to_z = to_z.astype(BF)
    kept, to_z = lax.optimization_barrier((kept, to_z))
    stay = outer_keep(kept, grads, 384) + got[384:].astype(F32)
    return (stay + lax.ppermute(to_z, "grp", Z_SWAP).astype(F32)).astype(BF)


def solution(mesh):
    return jax.shard_map(
        body,
        mesh=mesh,
        in_specs=(
            P("grp", None, None, "tp"),
            P("grp", None, None, "tp"),
            P("grp", None, "tp"),
            P("grp", None),
            P(),
            P("grp", None, None),
            P("grp", None, None, None),
            P(None, "tp"),
        ),
        out_specs=P("grp", "tp"),
        check_vma=False,
    )
```

time: 184 us -> 120 us (0.65)
  Pallas kernels: 61.4 us -> 35.3 us
  blocking collectives: 14.8 us -> 0 us
  waiting for transfers between devices: 57.2 us -> 45.5 us
  local copies, waits for them, and re-layouts: 12.6 us -> 5.57 us
  other arithmetic: 4.08 us -> 1.45 us
    pallas_call x1, Pallas kernels: 25.7 us -> 3.03 us  [pick(): pl.pallas_call(pick_kernel, grid_spec=pltpu.PrefetchScalarGridSpec(num_sc...]
    unnamed x1 -> x0, blocking collectives: 14.8 us -> none
    ppermute x1, waiting for transfers between devices: 19.7 us -> 6.27 us  [body(): other = lax.ppermute(mine, 'tp', H_SWAP)]
    unnamed x22 -> x16, local copies, waits for them, and re-layouts: 9.4 us -> 4.24 us
    ppermute x8 -> x10, waiting for transfers between devices: 30.2 us -> 34.8 us  [the longest x1 19.1 us: body(): return (stay + lax.ppermute(to_z, 'grp', Z_SWAP).astype(F32)).astype(BF)]
    ppermute x1, waiting for transfers between devices: 3.93 us -> 0.01 us  [body(): gd = lax.ppermute(gb[128:], 'grp', y_shift(-1))]
    pallas_call x4 -> x6, Pallas kernels: 22.8 us -> 18.9 us  [the longest x1 10.1 us: attention(): pl.pallas_call(functools.partial(attention_kernel, chunk=chunk, mb=mb), g...]
    squeeze x2 -> x1, local copies, waits for them, and re-layouts: 2.04 us -> 0.01 us  [body(): my_lengths = lax.dynamic_index_in_dim(lengths, gi, 0, keepdims=False)]
  transfers between devices with their start and end apart: 13 -> 15, of which waited for: 6 -> 9; matrix products, arithmetic and copies ran while one was open for 3% -> 0% of each run, Pallas kernels for 16% -> 21%
where the time goes in v2:
time: 120 us
  waiting for transfers between devices  45.5 us (38%)
  Pallas kernels  35.3 us (29%)
  starting transfers between devices  32 us (27%)
  local copies, waits for them, and re-layouts  5.57 us (5%)
  other arithmetic  1.45 us (1%)
    ppermute x1, waiting for transfers between devices, body(): return (stay + lax.ppermute(to_z, 'grp', Z_SWAP).astype(F32)).astype(BF)  19.1 us
    pallas_call x1, Pallas kernels, predict(): pl.pallas_call(predict_kernel, grid=(k // block,), in_specs=[pl.BlockSpec...  13.3 us
    pallas_call x1, Pallas kernels, attention(): pl.pallas_call(functools.partial(attention_kernel, chunk=chunk, mb=mb), g...  10.1 us
    ppermute x1, waiting for transfers between devices, body(): ob = lax.ppermute(other, 'tp', x_shift(-1))  7.37 us
    all_to_all x1, starting transfers between devices, body(): lax.all_to_all(share, 'grp', split_axis=0, concat_axis=0, tiled=True)  7.35 us
    ppermute x1, waiting for transfers between devices, body(): other = lax.ppermute(mine, 'tp', H_SWAP)  6.27 us
    all_to_all x1, starting transfers between devices, body(): lax.all_to_all(predicted, 'grp', split_axis=0, concat_axis=0, tiled=True)  4.63 us
    pallas_call x1, Pallas kernels, outer_send(): pl.pallas_call(send_kernel, grid_spec=pltpu.PrefetchScalarGridSpec(num_sc...  4.36 us
  transfers between devices with their start and end apart: 15, of which 9 were waited for; matrix products, arithmetic and copies ran while one was open for 0% of the time, Pallas kernels for 21%

profile of v2, /device:TPU:1, one launch (start us, length us, event | category | flops | bytes accessed | tf_op | source)
XLA Modules:
  0.0 120.0 jit_solution(636460119651072667)
XLA Ops:
  0.0 0.0 copy-start
  0.0 0.7 copy-done
  0.7 1.3 %concatenate.3.info = s32[40]{0:T(128)} concatenate(s32[1]{0:T(128)} %bitcast, s32[1]{0:T(128)} %bitcast.1, s32[1]{0:T(128)} %bitcast.2, s32[1]{0:T(128)} %bitcast.3, s32[1]{0:T(128)} %bitcast.4, s32[1]{0:T(128)} %bitcast.4, s32[1]{0:T(128)} %bitcast.4, s32[1]{0:T(128)} %bitcast.4, s32[16]{0:T(128)} %bitcast.24, s32[16]{0:T(128)S(1)} %dynamic-slice_bitcast_fusion), dimensions={0} | concatenate | bytes 320 | tf_op jit(solution)/shard_map/concatenate | solution.py:345
  2.0 3.0 %pick.1 = bf16[512,896]{1,0:T(8,128)(2,1)} custom-call(s32[40]{0:T(128)} %concatenate.3.info, bf16[512,6144]{1,0:T(8,128)(2,1)} %bitcast.21), custom_call_target="tpu_custom_call" | custom-call | bytes 3145728 | tf_op jit(solution)/shard_map/pick/pallas_call | solution.py:182
  5.0 7.4 %all-to-all-start = ((bf16[16,32,896]{2,1,0:T(8,128)(2,1)}), bf16[16,32,896]{2,1,0:T(8,128)(2,1)S(1)}, u32[]{:S(2)}, u32[]{:S(2)}) async-start(bf16[16,32,896]{2,1,0:T(8,128)(2,1)} %bitcast.23), calls=%async_computation | async-start | bytes 1835008 | tf_op jit(solution)/shard_map/all_to_all | solution.py:349
  12.4 0.0 copy-start.1
  12.4 13.3 %predict.1 = bf16[512,1152]{1,0:T(8,128)(2,1)} custom-call(bf16[512,6144]{1,0:T(8,128)(2,1)} %bitcast.22, bf16[6144,1152]{1,0:T(8,128)(2,1)} %p_ref.1), custom_call_target="tpu_custom_call" | custom-call | flops 7247757312 | bytes 21626880 | tf_op jit(solution)/shard_map/predict/pallas_call | solution.py:134
  25.7 0.0 copy-start.3
  25.7 0.0 copy-start.6
  25.7 0.0 copy-start.7
  25.7 1.1 all-to-all-done
  26.8 0.0 copy-done.1
  26.8 1.4 %compact.1 = (bf16[768,256]{1,0:T(8,128)(2,1)S(1)}, f32[8,256]{1,0:T(8,128)S(1)}) custom-call(s32[40]{0:T(128)S(1)} %copy-done.1, bf16[512,896]{1,0:T(8,128)(2,1)S(1)} %bitcast.17), custom_call_target="tpu_custom_call" | custom-call | flops 201326592 | bytes 2097152 | tf_op jit(solution)/shard_map/compact/pallas_call | solution.py:229
  28.2 4.6 %all-to-all-start.1 = ((bf16[16,32,1152]{2,1,0:T(8,128)(2,1)}), bf16[16,32,1152]{2,1,0:T(8,128)(2,1)S(1)}, u32[]{:S(2)}, u32[]{:S(2)}) async-start(bf16[16,32,1152]{2,1,0:T(8,128)(2,1)} %bitcast.13), calls=%async_computation.1 | async-start | bytes 2359296 | tf_op jit(solution)/shard_map/all_to_all | solution.py:354
  32.9 2.5 %collective-permute-start.2 = (bf16[768,256]{1,0:T(8,128)(2,1)S(1)}, bf16[768,256]{1,0:T(8,128)(2,1)S(1)}, u32[]{:S(2)}, u32[]{:S(2)}) collective-permute-start(bf16[768,256]{1,0:T(8,128)(2,1)S(1)} %get-tuple-element.24.refs_0_), channel_id=1, source_target_pairs={{0,48},{16,0},{32,16},{48,32},{64,112},{80,64},{96,80},{112,96},{1... | collective-permute-start | bytes 1179656 | tf_op jit(solution)/shard_map/ppermute | solution.py:358
  35.4 0.0 collective-permute-start.1
  35.4 3.3 %collective-permute-start = (bf16[768,256]{1,0:T(8,128)(2,1)S(1)}, bf16[768,256]{1,0:T(8,128)(2,1)}, u32[]{:S(2)}, u32[]{:S(2)}) collective-permute-start(bf16[768,256]{1,0:T(8,128)(2,1)S(1)} %get-tuple-element.24.refs_0_), channel_id=1, source_target_pairs={{0,64},{16,80},{32,96},{48,112},{64,0},{80,16},{96,32},{112,48},{1... | collective-permute-start | bytes 1179656 | tf_op jit(solution)/shard_map/ppermute | solution.py:356
  38.7 0.0 copy-done.3
  38.7 0.0 copy-done.6
  38.7 0.0 copy-done.7
  38.7 0.0 copy-start.2
  38.7 2.8 %copy-done.2 = bf16[128,64,384]{2,1,0:T(8,128)(2,1)S(1)} copy-done((bf16[128,64,384]{2,1,0:T(8,128)(2,1)S(1)}, bf16[128,64,384]{2,1,0:T(8,128)(2,1)}, u32[]{:S(2)}) %copy-start.2) | copy-done | bytes 6291480
  41.4 10.1 %attention.1.tap_ref = bf16[256,1152]{1,0:T(8,128)(2,1)S(1)} custom-call(s32[64]{0:T(128)S(1)} %bitcast.20, bf16[256,1152]{1,0:T(8,128)(2,1)S(1)} %bitcast.18, bf16[256,384]{1,0:T(8,128)(2,1)S(1)} %bitcast.19, bf16[128,64,384]{2,1,0:T(8,128)(2,1)S(1)} %copy-done.2), custom_call_target="tpu_custom_call" | custom-call | flops 6845104128 | bytes 8388608 | tf_op jit(solution)/shard_map/attention/pallas_call | solution.py:89
  51.6 0.0 collective-permute-done.2.refs_1_
  51.6 0.0 collective-permute-done.1.refs_3_
  51.6 0.0 copy-start.4
  51.6 0.7 copy-done.4
  52.3 6.3 %collective-permute-done.refs_4_ = bf16[768,256]{1,0:T(8,128)(2,1)} collective-permute-done((bf16[768,256]{1,0:T(8,128)(2,1)S(1)}, bf16[768,256]{1,0:T(8,128)(2,1)}, u32[]{:S(2)}, u32[]{:S(2)}) %collective-permute-start) | collective-permute-done | bytes 393248 | tf_op jit(solution)/shard_map/ppermute | solution.py:356
  58.6 0.0 copy-start.5
  58.6 0.0 all-to-all-done.1
  58.6 0.7 grad_pred.1.refs_8_
  59.3 2.4 %collective-permute-start.5 = (bf16[256,1152]{1,0:T(8,128)(2,1)S(1)}, bf16[256,1152]{1,0:T(8,128)(2,1)S(1)}, u32[]{:S(2)}, u32[]{:S(2)}) collective-permute-start(bf16[256,1152]{1,0:T(8,128)(2,1)S(1)} %grad_pred.1.refs_8_), channel_id=1, source_target_pairs={{0,6},{1,7},{2,0},{3,1},{4,2},{5,3},{6,4},{7,5},{8,14},{9,15},{10,... | collective-permute-start | bytes 1769480 | tf_op jit(solution)/shard_map/ppermute | solution.py:370
  61.7 0.0 collective-permute-start.4
  61.7 2.5 %collective-permute-start.6 = (bf16[768,256]{1,0:T(8,128)(2,1)}, bf16[768,256]{1,0:T(8,128)(2,1)S(1)}, u32[]{:S(2)}, u32[]{:S(2)}) collective-permute-start(bf16[768,256]{1,0:T(8,128)(2,1)} %collective-permute-done.refs_4_), channel_id=1, source_target_pairs={{0,48},{16,0},{32,16},{48,32},{64,112},{80,64},{96,80},{112,96},{1... | collective-permute-start | bytes 1179656 | tf_op jit(solution)/shard_map/ppermute | solution.py:365
  64.2 0.0 collective-permute-start.8
  64.2 0.0 copy-done.5
  64.2 0.2 collective-permute-start.3
  64.4 7.4 %collective-permute-done.6.refs_5_ = bf16[768,256]{1,0:T(8,128)(2,1)S(1)} collective-permute-done((bf16[768,256]{1,0:T(8,128)(2,1)}, bf16[768,256]{1,0:T(8,128)(2,1)S(1)}, u32[]{:S(2)}, u32[]{:S(2)}) %collective-permute-start.6) | collective-permute-done | bytes 393248 | tf_op jit(solution)/shard_map/ppermute | solution.py:365
  71.7 1.9 %collective-permute-done.5.refs_9_ = bf16[256,1152]{1,0:T(8,128)(2,1)S(1)} collective-permute-done((bf16[256,1152]{1,0:T(8,128)(2,1)S(1)}, bf16[256,1152]{1,0:T(8,128)(2,1)S(1)}, u32[]{:S(2)}, u32[]{:S(2)}) %collective-permute-start.5) | collective-permute-done | bytes 589856 | tf_op jit(solution)/shard_map/ppermute | solution.py:370
  73.7 2.9 %collective-permute-done.4.refs_10_ = bf16[256,1152]{1,0:T(8,128)(2,1)S(1)} collective-permute-done((bf16[256,1152]{1,0:T(8,128)(2,1)S(1)}, bf16[256,1152]{1,0:T(8,128)(2,1)S(1)}, u32[]{:S(2)}, u32[]{:S(2)}) %collective-permute-start.4) | collective-permute-done | bytes 589856 | tf_op jit(solution)/shard_map/ppermute | solution.py:369
  76.6 2.5 %collective-permute-start.7 = (bf16[768,256]{1,0:T(8,128)(2,1)S(1)}, bf16[768,256]{1,0:T(8,128)(2,1)S(1)}, u32[]{:S(2)}, u32[]{:S(2)}) collective-permute-start(bf16[768,256]{1,0:T(8,128)(2,1)S(1)} %collective-permute-done.6.refs_5_), channel_id=1, source_target_pairs={{0,48},{16,0},{32,16},{48,32},{64,112},{80,64},{96,80},{112,96},{1... | collective-permute-start | bytes 1179656 | tf_op jit(solution)/shard_map/ppermute | solution.py:374
  79.1 0.1 collective-permute-start.9
  79.2 2.7 %collective-permute-start.10 = (bf16[128,1152]{1,0:T(8,128)(2,1)S(1)}, bf16[128,1152]{1,0:T(8,128)(2,1)S(1)}, u32[]{:S(2)}, u32[]{:S(2)}) collective-permute-start(bf16[128,1152]{1,0:T(8,128)(2,1)S(1)} %slice.13), channel_id=1, source_target_pairs={{0,6},{1,7},{2,0},{3,1},{4,2},{5,3},{6,4},{7,5},{8,14},{9,15},{10,... | collective-permute-start | bytes 884744 | tf_op jit(solution)/shard_map/ppermute | solution.py:373
  81.8 1.3 %collective-permute-done.3.refs_2_ = bf16[768,256]{1,0:T(8,128)(2,1)S(1)} collective-permute-done((bf16[768,256]{1,0:T(8,128)(2,1)S(1)}, bf16[768,256]{1,0:T(8,128)(2,1)S(1)}, u32[]{:S(2)}, u32[]{:S(2)}) %collective-permute-start.3) | collective-permute-done | bytes 393248 | tf_op jit(solution)/shard_map/ppermute | solution.py:366
  83.2 0.0 collective-permute-done.8.refs_7_
  83.2 3.3 %collective-permute-done.9.refs_11_ = bf16[128,1152]{1,0:T(8,128)(2,1)S(1)} collective-permute-done((bf16[128,1152]{1,0:T(8,128)(2,1)S(1)}, bf16[128,1152]{1,0:T(8,128)(2,1)S(1)}, u32[]{:S(2)}, u32[]{:S(2)}) %collective-permute-start.9) | collective-permute-done | bytes 294944 | tf_op jit(solution)/shard_map/ppermute | solution.py:372
  86.5 0.0 collective-permute-done.10.refs_12_
  86.5 0.0 collective-permute-done.7.refs_6_
  86.5 4.4 %outer_send.1 = (bf16[768,1152]{1,0:T(8,128)(2,1)S(1)}, bf16[768,1024]{1,0:T(8,128)(2,1)S(1)}, bf16[1024,1152]{1,0:T(8,128)(2,1)S(1)}) custom-call(s32[40]{0:T(128)S(1)} %copy-done.1, bf16[768,256]{1,0:T(8,128)(2,1)S(1)} %get-tuple-element.24.refs_0_, bf16[768,256]{1,0:T(8,128)(2,1)S(1)} %collective-permute-done.2.refs_1_, ...), custom_call_target="tpu_custom_call" | custom-call | flops 1811939328 | bytes 8388608 | tf_op jit(solution)/shard_map/outer_send/pallas_call | solution.py:296
  90.9 3.4 %collective-permute-start.11 = (bf16[768,1152]{1,0:T(8,128)(2,1)S(1)}, bf16[768,1152]{1,0:T(8,128)(2,1)S(1)}, u32[]{:S(2)}, u32[]{:S(2)}) collective-permute-start(bf16[768,1152]{1,0:T(8,128)(2,1)S(1)} %get-tuple-element.38), channel_id=1, source_target_pairs={{0,1},{1,0},{2,3},{3,2},{4,5},{5,4},{6,7},{7,6},{8,9},{9,8},{10,11... | collective-permute-start | bytes 5308424 | tf_op jit(solution)/shard_map/ppermute | solution.py:378
  94.3 1.2 outer_keep.2
  95.4 2.1 %collective-permute-done.11 = bf16[768,1152]{1,0:T(8,128)(2,1)S(1)} collective-permute-done((bf16[768,1152]{1,0:T(8,128)(2,1)S(1)}, bf16[768,1152]{1,0:T(8,128)(2,1)S(1)}, u32[]{:S(2)}, u32[]{:S(2)}) %collective-permute-start.11) | collective-permute-done | bytes 1769504 | tf_op jit(solution)/shard_map/ppermute | solution.py:378
  97.6 0.2 add_convert_fusion.1
  97.8 0.7 collective-permute-start.12
  98.5 1.2 outer_keep.3
  99.7 19.1 %collective-permute-done.12 = bf16[384,1152]{1,0:T(8,128)(2,1)S(1)} collective-permute-done((bf16[384,1152]{1,0:T(8,128)(2,1)S(1)}, bf16[384,1152]{1,0:T(8,128)(2,1)S(1)}, u32[]{:S(2)}, u32[]{:S(2)}) %collective-permute-start.12) | collective-permute-done | bytes 884768 | tf_op jit(solution)/shard_map/ppermute | solution.py:383
  118.7 1.2 %add_convert_fusion = bf16[384,1152]{1,0:T(8,128)(2,1)} fusion(bf16[384,1152]{1,0:T(8,128)(2,1)S(1)} %collective-permute-done.12, f32[384,1152]{1,0:T(8,128)S(1)} %outer_keep.3, bf16[768,1152]{1,0:T(8,128)(2,1)S(1)} %collective-permute-done.11), kind=kLoop, calls=%fused_computation | loop fusion | flops 2211840 | bytes 4423680 | tf_op jit(solution)/shard_map/convert_element_type | solution.py:383
  (3 shorter events, 0.1 us)
Async XLA Ops:
  0.0 0.7 copy-start
  5.0 21.8 %all-to-all-start = ((bf16[16,32,896]{2,1,0:T(8,128)(2,1)}), bf16[16,32,896]{2,1,0:T(8,128)(2,1)S(1)}, u32[]{:S(2)}, u32[]{:S(2)}) async-start(bf16[16,32,896]{2,1,0:T(8,128)(2,1)} %bitcast.23), calls=%async_computation | async-start | bytes 1835008 | tf_op jit(solution)/shard_map/all_to_all | solution.py:349
  12.4 14.5 %copy-start.1 = (s32[40]{0:T(128)S(1)}, s32[40]{0:T(128)}, u32[]{:S(2)}) copy-start(s32[40]{0:T(128)} %concatenate.3.info) | copy-start | bytes 484
  25.7 13.0 %copy-start.3 = (bf16[1,16,16,1152]{3,2,1,0:T(8,128)(2,1)S(1)}, bf16[1,16,16,1152]{3,2,1,0:T(8,128)(2,1)}, u32[]{:S(2)}) copy-start(bf16[1,16,16,1152]{3,2,1,0:T(8,128)(2,1)} %param.8) | copy-start | bytes 1769476
  25.7 13.0 %copy-start.6 = (bf16[1,16,16,384]{3,2,1,0:T(8,128)(2,1)S(1)}, bf16[1,16,16,384]{3,2,1,0:T(8,128)(2,1)}, u32[]{:S(2)}) copy-start(bf16[1,16,16,384]{3,2,1,0:T(8,128)(2,1)} %param.9) | copy-start | bytes 589828
  25.7 13.0 %copy-start.7 = (s32[1,64]{1,0:T(1,128)S(1)}, s32[1,64]{1,0:T(1,128)}, u32[]{:S(2)}) copy-start(s32[1,64]{1,0:T(1,128)} %param.11) | copy-start | bytes 772
  28.2 30.4 %all-to-all-start.1 = ((bf16[16,32,1152]{2,1,0:T(8,128)(2,1)}), bf16[16,32,1152]{2,1,0:T(8,128)(2,1)S(1)}, u32[]{:S(2)}, u32[]{:S(2)}) async-start(bf16[16,32,1152]{2,1,0:T(8,128)(2,1)} %bitcast.13), calls=%async_computation.1 | async-start | bytes 2359296 | tf_op jit(solution)/shard_map/all_to_all | solution.py:354
  32.9 18.7 %collective-permute-start.2 = (bf16[768,256]{1,0:T(8,128)(2,1)S(1)}, bf16[768,256]{1,0:T(8,128)(2,1)S(1)}, u32[]{:S(2)}, u32[]{:S(2)}) collective-permute-start(bf16[768,256]{1,0:T(8,128)(2,1)S(1)} %get-tuple-element.24.refs_0_), channel_id=1, source_target_pairs={{0,48},{16,0},{32,16},{48,32},{64,112},{80,64},{96,80},{112,96},{1... | collective-permute-start | bytes 1179656 | tf_op jit(solution)/shard_map/ppermute | solution.py:358
  35.4 16.2 %collective-permute-start.1 = (bf16[768,256]{1,0:T(8,128)(2,1)S(1)}, bf16[768,256]{1,0:T(8,128)(2,1)S(1)}, u32[]{:S(2)}, u32[]{:S(2)}) collective-permute-start(bf16[768,256]{1,0:T(8,128)(2,1)S(1)} %get-tuple-element.24.refs_0_), channel_id=1, source_target_pairs={{0,16},{16,32},{32,48},{48,0},{64,80},{80,96},{96,112},{112,64},{1... | collective-permute-start | bytes 1179656 | tf_op jit(solution)/shard_map/ppermute | solution.py:357
  35.4 23.2 %collective-permute-start = (bf16[768,256]{1,0:T(8,128)(2,1)S(1)}, bf16[768,256]{1,0:T(8,128)(2,1)}, u32[]{:S(2)}, u32[]{:S(2)}) collective-permute-start(bf16[768,256]{1,0:T(8,128)(2,1)S(1)} %get-tuple-element.24.refs_0_), channel_id=1, source_target_pairs={{0,64},{16,80},{32,96},{48,112},{64,0},{80,16},{96,32},{112,48},{1... | collective-permute-start | bytes 1179656 | tf_op jit(solution)/shard_map/ppermute | solution.py:356
  38.7 2.8 %copy-start.2 = (bf16[128,64,384]{2,1,0:T(8,128)(2,1)S(1)}, bf16[128,64,384]{2,1,0:T(8,128)(2,1)}, u32[]{:S(2)}) copy-start(bf16[128,64,384]{2,1,0:T(8,128)(2,1)} %pool_ref.1) | copy-start | bytes 18874372
  51.6 0.7 copy-start.4
  58.6 5.6 %copy-start.5 = (bf16[768,256]{1,0:T(8,128)(2,1)S(1)}, bf16[768,256]{1,0:T(8,128)(2,1)}, u32[]{:S(2)}) copy-start(bf16[768,256]{1,0:T(8,128)(2,1)} %copy-done.4) | copy-start | bytes 1179652
  59.3 14.4 %collective-permute-start.5 = (bf16[256,1152]{1,0:T(8,128)(2,1)S(1)}, bf16[256,1152]{1,0:T(8,128)(2,1)S(1)}, u32[]{:S(2)}, u32[]{:S(2)}) collective-permute-start(bf16[256,1152]{1,0:T(8,128)(2,1)S(1)} %grad_pred.1.refs_8_), channel_id=1, source_target_pairs={{0,6},{1,7},{2,0},{3,1},{4,2},{5,3},{6,4},{7,5},{8,14},{9,15},{10,... | collective-permute-start | bytes 1769480 | tf_op jit(solution)/shard_map/ppermute | solution.py:370
  61.7 14.9 %collective-permute-start.4 = (bf16[256,1152]{1,0:T(8,128)(2,1)S(1)}, bf16[256,1152]{1,0:T(8,128)(2,1)S(1)}, u32[]{:S(2)}, u32[]{:S(2)}) collective-permute-start(bf16[256,1152]{1,0:T(8,128)(2,1)S(1)} %grad_pred.1.refs_8_), channel_id=1, source_target_pairs={{0,2},{1,3},{2,4},{3,5},{4,6},{5,7},{6,0},{7,1},{8,10},{9,11},{10,... | collective-permute-start | bytes 1769480 | tf_op jit(solution)/shard_map/ppermute | solution.py:369
  61.7 10.1 %collective-permute-start.6 = (bf16[768,256]{1,0:T(8,128)(2,1)}, bf16[768,256]{1,0:T(8,128)(2,1)S(1)}, u32[]{:S(2)}, u32[]{:S(2)}) collective-permute-start(bf16[768,256]{1,0:T(8,128)(2,1)} %collective-permute-done.refs_4_), channel_id=1, source_target_pairs={{0,48},{16,0},{32,16},{48,32},{64,112},{80,64},{96,80},{112,96},{1... | collective-permute-start | bytes 1179656 | tf_op jit(solution)/shard_map/ppermute | solution.py:365
  64.2 19.0 %collective-permute-start.8 = (bf16[768,256]{1,0:T(8,128)(2,1)}, bf16[768,256]{1,0:T(8,128)(2,1)S(1)}, u32[]{:S(2)}, u32[]{:S(2)}) collective-permute-start(bf16[768,256]{1,0:T(8,128)(2,1)} %collective-permute-done.refs_4_), channel_id=1, source_target_pairs={{0,16},{16,32},{32,48},{48,0},{64,80},{80,96},{96,112},{112,64},{1... | collective-permute-start | bytes 1179656 | tf_op jit(solution)/shard_map/ppermute | solution.py:364
  64.2 19.0 %collective-permute-start.3 = (bf16[768,256]{1,0:T(8,128)(2,1)S(1)}, bf16[768,256]{1,0:T(8,128)(2,1)S(1)}, u32[]{:S(2)}, u32[]{:S(2)}) collective-permute-start(bf16[768,256]{1,0:T(8,128)(2,1)S(1)} %copy-done.5), channel_id=1, source_target_pairs={{0,16},{16,32},{32,48},{48,0},{64,80},{80,96},{96,112},{112,64},{1... | collective-permute-start | bytes 1179656 | tf_op jit(solution)/shard_map/ppermute | solution.py:366
  76.6 10.0 %collective-permute-start.7 = (bf16[768,256]{1,0:T(8,128)(2,1)S(1)}, bf16[768,256]{1,0:T(8,128)(2,1)S(1)}, u32[]{:S(2)}, u32[]{:S(2)}) collective-permute-start(bf16[768,256]{1,0:T(8,128)(2,1)S(1)} %collective-permute-done.6.refs_5_), channel_id=1, source_target_pairs={{0,48},{16,0},{32,16},{48,32},{64,112},{80,64},{96,80},{112,96},{1... | collective-permute-start | bytes 1179656 | tf_op jit(solution)/shard_map/ppermute | solution.py:374
  79.1 7.4 %collective-permute-start.9 = (bf16[128,1152]{1,0:T(8,128)(2,1)S(1)}, bf16[128,1152]{1,0:T(8,128)(2,1)S(1)}, u32[]{:S(2)}, u32[]{:S(2)}) collective-permute-start(bf16[128,1152]{1,0:T(8,128)(2,1)S(1)} %slice.12), channel_id=1, source_target_pairs={{0,2},{1,3},{2,4},{3,5},{4,6},{5,7},{6,0},{7,1},{8,10},{9,11},{10,... | collective-permute-start | bytes 884744 | tf_op jit(solution)/shard_map/ppermute | solution.py:372
  79.2 7.3 %collective-permute-start.10 = (bf16[128,1152]{1,0:T(8,128)(2,1)S(1)}, bf16[128,1152]{1,0:T(8,128)(2,1)S(1)}, u32[]{:S(2)}, u32[]{:S(2)}) collective-permute-start(bf16[128,1152]{1,0:T(8,128)(2,1)S(1)} %slice.13), channel_id=1, source_target_pairs={{0,6},{1,7},{2,0},{3,1},{4,2},{5,3},{6,4},{7,5},{8,14},{9,15},{10,... | collective-permute-start | bytes 884744 | tf_op jit(solution)/shard_map/ppermute | solution.py:373
  90.9 6.7 %collective-permute-start.11 = (bf16[768,1152]{1,0:T(8,128)(2,1)S(1)}, bf16[768,1152]{1,0:T(8,128)(2,1)S(1)}, u32[]{:S(2)}, u32[]{:S(2)}) collective-permute-start(bf16[768,1152]{1,0:T(8,128)(2,1)S(1)} %get-tuple-element.38), channel_id=1, source_target_pairs={{0,1},{1,0},{2,3},{3,2},{4,5},{5,4},{6,7},{7,6},{8,9},{9,8},{10,11... | collective-permute-start | bytes 5308424 | tf_op jit(solution)/shard_map/ppermute | solution.py:378
  97.8 20.9 %collective-permute-start.12 = (bf16[384,1152]{1,0:T(8,128)(2,1)S(1)}, bf16[384,1152]{1,0:T(8,128)(2,1)S(1)}, u32[]{:S(2)}, u32[]{:S(2)}) collective-permute-start(bf16[384,1152]{1,0:T(8,128)(2,1)S(1)} %add_convert_fusion.1), channel_id=1, source_target_pairs={{0,8},{1,9},{2,10},{3,11},{4,12},{5,13},{6,14},{7,15},{8,0},{9,1},... | collective-permute-start | bytes 2654216 | tf_op jit(solution)/shard_map/ppermute | solution.py:383

commit v3 on v2

--- a/solution.py
+++ b/solution.py
@@ -15,7 +15,6 @@
 LOG2E = 1.4426950408889634
 BF = jnp.bfloat16
 F32 = jnp.float32
-ROUTE, LENGTH = 8, 24
 MIB = 2**20
 
 GRID = [(z, y, c) for z in range(2) for y in range(4) for c in range(2)]
@@ -37,6 +36,11 @@
 
 def x_shift(step):
     return [(h * 4 + x, h * 4 + (x + step) % 4) for h, x in TPGRID]
+
+
+def coordinates():
+    g, t = lax.axis_index("grp"), lax.axis_index("tp")
+    return g // 8, (g // 2) % 4, g % 2, t // 4, t % 4
 
 
 def attention_kernel(table, q_ref, resp_ref, pool_ref, out_ref, kv, q2, acc, tops, *, chunk, mb):
@@ -149,8 +153,9 @@
     )(x, p)
 
 
-def pick_kernel(info, x_hbm, out_ref, x_ref, sem):
-    x, h = info[0], info[1]
+def pick_kernel(routes, lengths, x_hbm, out_ref, x_ref, sem):
+    mine = lax.axis_index("grp")
+    _, _, _, h, x = coordinates()
     for z, c in ((0, 0), (0, 1), (1, 0), (1, 1)):
         row = pl.multiple_of((z * 8 + x * 2 + c) * 32, 32)
         there = x_ref.at[pl.ds((z * 2 + c) * 32, 32)]
@@ -159,11 +164,11 @@
     token += lax.broadcasted_iota(jnp.int32, (32, 128), 1)
     mark = jnp.full((32, 128), 127, jnp.int32)
     for r in range(16):
-        route = info[ROUTE + r]
+        route = routes[r]
         rank = jnp.int32(0)
         for earlier in range(r):
-            rank += (info[ROUTE + earlier] == route).astype(jnp.int32)
-        dead = jnp.where(token % LMAX < info[LENGTH + r], 0, 64)
+            rank += (routes[earlier] == route).astype(jnp.int32)
+        dead = jnp.where(token % LMAX < lengths[mine, r], 0, 64)
         mark = jnp.where(token // LMAX == r, route * MOST + rank + dead, mark)
     mark = mark.astype(F32).astype(BF)
     pltpu.make_async_copy(x_ref, x_ref, sem).wait()
@@ -178,11 +183,11 @@
         out_ref[at : at + 32, 768:] = mark
 
 
-def pick(info, x):
+def pick(routes, lengths, x):
     return pl.pallas_call(
         pick_kernel,
         grid_spec=pltpu.PrefetchScalarGridSpec(
-            num_scalar_prefetch=1,
+            num_scalar_prefetch=2,
             grid=(),
             in_specs=[pl.BlockSpec(memory_space=pl.ANY)],
             out_specs=pl.BlockSpec(memory_space=pltpu.VMEM),
@@ -192,7 +197,7 @@
         compiler_params=pltpu.CompilerParams(vmem_limit_bytes=58 * MIB),
         cost_estimate=pl.CostEstimate(flops=0, bytes_accessed=3 * 2**20, transcendentals=0),
         name="pick",
-    )(info, x)
+    )(routes, lengths, x)
 
 
 def slot_of(mark):
@@ -200,13 +205,15 @@
     return jnp.where(mark < 64, mark, mark - 64) * LMAX + lane % LMAX
 
 
-def compact_kernel(info, x_ref, out_ref, meta_ref):
+def compact_kernel(x_ref, out_ref, meta_ref):
+    z, _, c, _, x = coordinates()
+
     def marks_of(prompt):
         at = pl.multiple_of(prompt * 32, 32)
         rows = x_ref[pl.ds(at, 32), 768:].astype(F32)
         return jnp.concatenate([rows[0:1], rows[1:2]], 1).astype(jnp.int32)
 
-    slot = slot_of(marks_of(info[3]))
+    slot = slot_of(marks_of(z * 8 + x * 2 + c))
     rows = lax.broadcasted_iota(jnp.int32, (512, 256), 0)
     sel = (rows == slot).astype(F32).astype(BF)
     out_ref[...] = lax.dot_general(
@@ -214,7 +221,7 @@
     ).astype(BF)
 
     every = x_ref[:, 768:].astype(F32)
-    own = marks_of(info[4])
+    own = marks_of(lax.axis_index("grp"))
     weight = jnp.zeros(own.shape, F32)
     for s in range(16):
         hit = (every == 2.0 * s) | (every == 2.0 * s + 1.0)
@@ -225,15 +232,11 @@
     )
 
 
-def compact(info, x):
+def compact(x):
     return pl.pallas_call(
         compact_kernel,
-        grid_spec=pltpu.PrefetchScalarGridSpec(
-            num_scalar_prefetch=1,
-            grid=(),
-            in_specs=[pl.BlockSpec(memory_space=pltpu.VMEM)],
-            out_specs=[pl.BlockSpec(memory_space=pltpu.VMEM)] * 2,
-        ),
+        in_specs=[pl.BlockSpec(memory_space=pltpu.VMEM)],
+        out_specs=[pl.BlockSpec(memory_space=pltpu.VMEM)] * 2,
         out_shape=[
             jax.ShapeDtypeStruct((768, 256), BF),
             jax.ShapeDtypeStruct((8, 256), F32),
@@ -243,7 +246,7 @@
             flops=2 * 512 * 768 * 256, bytes_accessed=2 * 2**20, transcendentals=0
         ),
         name="compact",
-    )(info, x)
+    )(x)
 
 
 def grad_kernel(meta_ref, y_ref, tap_ref, out_ref):
@@ -261,7 +264,7 @@
         in_specs=[pl.BlockSpec(memory_space=pltpu.VMEM)] * 3,
         out_specs=pl.BlockSpec(memory_space=pltpu.VMEM),
         out_shape=jax.ShapeDtypeStruct(tap.shape, BF),
-        compiler_params=pltpu.CompilerParams(vmem_limit_bytes=16 * MIB),
+        compiler_params=pltpu.CompilerParams(vmem_limit_bytes=10 * MIB),
         cost_estimate=pl.CostEstimate(
             flops=2 * 512 * 256 * tap.shape[1], bytes_accessed=3 * 2**20, transcendentals=0
         ),
@@ -269,9 +272,9 @@
     )(meta, y, tap)
 
 
-def send_kernel(info, *refs):
+def send_kernel(*refs):
     xs, gs, (out_ref, keep_ref, gbuf_ref, xbuf) = refs[:8], refs[8:13], refs[13:]
-    x, h, y = info[0], info[1], info[2]
+    _, y, _, h, x = coordinates()
     for ref, dy, lo in zip(gs, (0, 1, 3, 2, 2), (0, 0, 0, 0, 128)):
         at = pl.multiple_of(((y + dy + 4 - x) % 4) * 256 + lo, 128)
         gbuf_ref[pl.ds(at, ref.shape[0]), :] = ref[...]
@@ -291,28 +294,24 @@
     out_ref[...] = jnp.dot(xbuf[...], gbuf_ref[...], preferred_element_type=F32).astype(BF)
 
 
-def outer_send(info, xs, gs):
+def outer_send(xs, gs):
     m = gs[0].shape[1]
     return pl.pallas_call(
         send_kernel,
-        grid_spec=pltpu.PrefetchScalarGridSpec(
-            num_scalar_prefetch=1,
-            grid=(),
-            in_specs=[pl.BlockSpec(memory_space=pltpu.VMEM)] * 13,
-            out_specs=[pl.BlockSpec(memory_space=pltpu.VMEM)] * 3,
-            scratch_shapes=[pltpu.VMEM((768, 1024), BF)],
-        ),
+        in_specs=[pl.BlockSpec(memory_space=pltpu.VMEM)] * 13,
+        out_specs=[pl.BlockSpec(memory_space=pltpu.VMEM)] * 3,
+        scratch_shapes=[pltpu.VMEM((768, 1024), BF)],
         out_shape=[
             jax.ShapeDtypeStruct((768, m), BF),
             jax.ShapeDtypeStruct((768, 1024), BF),
             jax.ShapeDtypeStruct((1024, m), BF),
         ],
-        compiler_params=pltpu.CompilerParams(vmem_limit_bytes=16 * MIB),
+        compiler_params=pltpu.CompilerParams(vmem_limit_bytes=10 * MIB),
         cost_estimate=pl.CostEstimate(
             flops=2 * 768 * 1024 * m, bytes_accessed=8 * 2**20, transcendentals=0
         ),
         name="outer_send",
-    )(info, *xs, *gs)
+    )(*xs, *gs)
 
 
 def keep_kernel(x_ref, g_ref, out_ref, *, lo):
@@ -327,7 +326,7 @@
         in_specs=[pl.BlockSpec(memory_space=pltpu.VMEM)] * 2,
         out_specs=pl.BlockSpec(memory_space=pltpu.VMEM),
         out_shape=jax.ShapeDtypeStruct((384, m), F32),
-        compiler_params=pltpu.CompilerParams(vmem_limit_bytes=16 * MIB),
+        compiler_params=pltpu.CompilerParams(vmem_limit_bytes=10 * MIB),
         cost_estimate=pl.CostEstimate(
             flops=2 * 384 * 1024 * m, bytes_accessed=4 * 2**20, transcendentals=0
         ),
@@ -336,45 +335,36 @@
 
 
 def body(queries, responses, cache_pool, page_table, lengths, routes, student_rows, projection):
-    gi = lax.axis_index("grp")
-    ti = lax.axis_index("tp")
-    z, y, c = gi // 8, (gi // 2) % 4, gi % 2
-    h, x = ti // 4, ti % 4
-    my_lengths = lax.dynamic_index_in_dim(lengths, gi, 0, keepdims=False)
-    own = jnp.stack([x, h, y, z * 8 + x * 2 + c, gi, gi, gi, gi]).astype(jnp.int32)
-    info = jnp.concatenate([own, routes[0, :, 0], my_lengths])
-
     rows = student_rows[0].reshape(-1, student_rows.shape[-1])
-    share = pick(info, rows)
+    share = pick(routes.reshape(-1), lengths, rows)
     share = lax.all_to_all(share, "grp", split_axis=0, concat_axis=0, tiled=True)
 
     predicted = predict(rows, projection)
-    mine, meta = compact(info, share)
+    mine, meta = compact(share)
     predicted, mine = lax.optimization_barrier((predicted, mine))
     predicted = lax.all_to_all(predicted, "grp", split_axis=0, concat_axis=0, tiled=True)
 
     other = lax.ppermute(mine, "tp", H_SWAP)
     ma = lax.ppermute(mine, "tp", x_shift(1))
     mb = lax.ppermute(mine, "tp", x_shift(-1))
+    mc = lax.ppermute(mine, "tp", x_shift(2))
 
     q = queries[0].reshape(256, -1)
     q, meta = lax.optimization_barrier((q, meta))
     tap = attention(q, responses[0].reshape(256, -1), cache_pool, page_table[0])
-    other, ma, mb, tap = lax.optimization_barrier((other, ma, mb, tap))
-    oa = lax.ppermute(other, "tp", x_shift(1))
-    ob = lax.ppermute(other, "tp", x_shift(-1))
-    mc = lax.ppermute(ma, "tp", x_shift(1))
-
     g = grad_pred(meta, predicted, tap)
     ga = lax.ppermute(g, "grp", y_shift(1))
     gb = lax.ppermute(g, "grp", y_shift(-1))
-    ga, gb, ob = lax.optimization_barrier((ga, gb, ob))
+    other, ma, mb, mc, g = lax.optimization_barrier((other, ma, mb, mc, g))
+    oa = lax.ppermute(other, "tp", x_shift(1))
+    ob = lax.ppermute(other, "tp", x_shift(-1))
+    oc = lax.ppermute(other, "tp", x_shift(2))
+    ga, gb, oa = lax.optimization_barrier((ga, gb, oa))
     gc = lax.ppermute(ga[:128], "grp", y_shift(1))
     gd = lax.ppermute(gb[128:], "grp", y_shift(-1))
-    oc = lax.ppermute(ob, "tp", x_shift(-1))
     xs = (mine, mb, mc, ma, other, ob, oc, oa)
 
-    send, kept, grads = outer_send(info, xs, (g, gb, ga, gc, gd))
+    send, kept, grads = outer_send(xs, (g, gb, ga, gc, gd))
     got = lax.ppermute(send, "grp", C_SWAP)
     to_z = outer_keep(kept, grads, 0) + got[:384].astype(F32)
     to_z = to_z.astype(BF)

time: 120 us -> 111 us (0.925)
  waiting for transfers between devices: 45.5 us -> 36.5 us
  starting transfers between devices: 32 us -> 33.9 us
  local copies, waits for them, and re-layouts: 5.57 us -> 3.77 us
    ppermute x1, waiting for transfers between devices: 7.37 us -> 0.01 us  [body(): ob = lax.ppermute(other, 'tp', x_shift(-1))]
    ppermute x1, waiting for transfers between devices: 0.01 us -> 6.37 us  [body(): oa = lax.ppermute(other, 'tp', x_shift(1))]
    ppermute x1, waiting for transfers between devices: 6.27 us -> 0.98 us  [body(): other = lax.ppermute(mine, 'tp', H_SWAP)]
    ppermute x1, waiting for transfers between devices: 3.34 us -> 0.01 us  [body(): gc = lax.ppermute(ga[:128], 'grp', y_shift(1))]
    ppermute x2, waiting for transfers between devices: 1.34 us -> 4.63 us  [the longest x1 4.62 us: body(): oc = lax.ppermute(other, 'tp', x_shift(2))]
    ppermute x2, starting transfers between devices: 2.67 us -> 5.2 us  [the longest x1 2.74 us: body(): mc = lax.ppermute(mine, 'tp', x_shift(2))]
    ppermute x1, waiting for transfers between devices: 1.92 us -> 0.01 us  [body(): gb = lax.ppermute(g, 'grp', y_shift(-1))]
    ppermute x1, starting transfers between devices: 2.48 us -> 0.86 us  [body(): mb = lax.ppermute(mine, 'tp', x_shift(-1))]
  transfers between devices with their start and end apart: 15 -> 15, of which waited for: 9 -> 7; matrix products, arithmetic and copies ran while one was open for 0% -> 0% of each run, Pallas kernels for 21% -> 24%
where the time goes in v3:
time: 111 us; the launch traced here: 110 us
  waiting for transfers between devices  36.5 us (33%)
  Pallas kernels  34.5 us (31%)
  starting transfers between devices  33.9 us (31%)
  local copies, waits for them, and re-layouts  3.77 us (3%)
  other arithmetic  1.33 us (1%)
    ppermute x1, waiting for transfers between devices, body(): return (stay + lax.ppermute(to_z, 'grp', Z_SWAP).astype(F32)).astype(BF)  19.1 us
    pallas_call x1, Pallas kernels, predict(): pl.pallas_call(predict_kernel, grid=(k // block,), in_specs=[pl.BlockSpec...  13.3 us
    pallas_call x1, Pallas kernels, attention(): pl.pallas_call(functools.partial(attention_kernel, chunk=chunk, mb=mb), g...  10.1 us
    all_to_all x1, starting transfers between devices, body(): lax.all_to_all(share, 'grp', split_axis=0, concat_axis=0, tiled=True)  7.35 us
    ppermute x1, waiting for transfers between devices, body(): oa = lax.ppermute(other, 'tp', x_shift(1))  6.37 us
    ppermute x1, waiting for transfers between devices, body(): oc = lax.ppermute(other, 'tp', x_shift(2))  4.62 us
    all_to_all x1, starting transfers between devices, body(): lax.all_to_all(predicted, 'grp', split_axis=0, concat_axis=0, tiled=True)  4.58 us
    pallas_call x1, Pallas kernels, outer_send(): pl.pallas_call(send_kernel, in_specs=[pl.BlockSpec(memory_space=pltpu.VME...  3.95 us
  transfers between devices with their start and end apart: 15, of which 7 were waited for; matrix products, arithmetic and copies ran while one was open for 0% of the time, Pallas kernels for 24%

profile of v3, /device:TPU:1, one launch (start us, length us, event | category | flops | bytes accessed | tf_op | source)
XLA Modules:
  0.0 110.2 jit_solution(6189883246502645070)
XLA Ops:
  0.0 3.3 %pick.1 = bf16[512,896]{1,0:T(8,128)(2,1)} custom-call(s32[16]{0:T(128)} %bitcast.17, s32[16,16]{1,0:T(8,128)} %lengths.1, bf16[512,6144]{1,0:T(8,128)(2,1)} %bitcast.14), custom_call_target="tpu_custom_call" | custom-call | bytes 3145728 | tf_op jit(solution)/shard_map/pick/pallas_call | solution.py:187
  3.3 7.4 %all-to-all-start = ((bf16[16,32,896]{2,1,0:T(8,128)(2,1)}), bf16[16,32,896]{2,1,0:T(8,128)(2,1)S(1)}, u32[]{:S(2)}, u32[]{:S(2)}) async-start(bf16[16,32,896]{2,1,0:T(8,128)(2,1)} %bitcast.16), calls=%async_computation | async-start | bytes 1835008 | tf_op jit(solution)/shard_map/all_to_all | solution.py:340
  10.6 13.3 %predict.1 = bf16[512,1152]{1,0:T(8,128)(2,1)} custom-call(bf16[512,6144]{1,0:T(8,128)(2,1)} %bitcast.15, bf16[6144,1152]{1,0:T(8,128)(2,1)} %p_ref.1), custom_call_target="tpu_custom_call" | custom-call | flops 7247757312 | bytes 21626880 | tf_op jit(solution)/shard_map/predict/pallas_call | solution.py:138
  23.9 0.0 copy-start.1
  23.9 0.0 copy-start.3
  23.9 1.2 %all-to-all-done = bf16[16,32,896]{2,1,0:T(8,128)(2,1)S(1)} async-done(((bf16[16,32,896]{2,1,0:T(8,128)(2,1)}), bf16[16,32,896]{2,1,0:T(8,128)(2,1)S(1)}, u32[]{:S(2)}, u32[]{:S(2)}) %all-to-all-start) | async-done | bytes 917536 | tf_op jit(solution)/shard_map/all_to_all | solution.py:340
  25.1 0.9 compact.1
  26.0 4.6 %all-to-all-start.1 = ((bf16[16,32,1152]{2,1,0:T(8,128)(2,1)}), bf16[16,32,1152]{2,1,0:T(8,128)(2,1)S(1)}, u32[]{:S(2)}, u32[]{:S(2)}) async-start(bf16[16,32,1152]{2,1,0:T(8,128)(2,1)} %bitcast.5), calls=%async_computation.1 | async-start | bytes 2359296 | tf_op jit(solution)/shard_map/all_to_all | solution.py:345
  30.6 2.7 %collective-permute-start.3 = (bf16[768,256]{1,0:T(8,128)(2,1)S(1)}, bf16[768,256]{1,0:T(8,128)(2,1)S(1)}, u32[]{:S(2)}, u32[]{:S(2)}) collective-permute-start(bf16[768,256]{1,0:T(8,128)(2,1)S(1)} %get-tuple-element.25.refs_0_), channel_id=1, source_target_pairs={{0,32},{16,48},{32,0},{48,16},{64,96},{80,112},{96,64},{112,80},{1... | collective-permute-start | bytes 1179656 | tf_op jit(solution)/shard_map/ppermute | solution.py:350
  33.3 0.9 collective-permute-start.2
  34.2 0.6 collective-permute-start.1
  34.8 3.3 %collective-permute-start = (bf16[768,256]{1,0:T(8,128)(2,1)S(1)}, bf16[768,256]{1,0:T(8,128)(2,1)}, u32[]{:S(2)}, u32[]{:S(2)}) collective-permute-start(bf16[768,256]{1,0:T(8,128)(2,1)S(1)} %get-tuple-element.25.refs_0_), channel_id=1, source_target_pairs={{0,64},{16,80},{32,96},{48,112},{64,0},{80,16},{96,32},{112,48},{1... | collective-permute-start | bytes 1179656 | tf_op jit(solution)/shard_map/ppermute | solution.py:347
  38.1 0.0 copy-done.1
  38.1 0.0 copy-done.3
  38.1 0.0 copy-start
  38.1 2.8 %copy-done = bf16[128,64,384]{2,1,0:T(8,128)(2,1)S(1)} copy-done((bf16[128,64,384]{2,1,0:T(8,128)(2,1)S(1)}, bf16[128,64,384]{2,1,0:T(8,128)(2,1)}, u32[]{:S(2)}) %copy-start) | copy-done | bytes 6291480
  40.9 0.0 copy-start.2
  40.9 0.9 copy-done.2
  41.8 10.1 %attention.1.tap_ref = bf16[256,1152]{1,0:T(8,128)(2,1)S(1)} custom-call(s32[64]{0:T(128)S(1)} %bitcast.13, bf16[256,1152]{1,0:T(8,128)(2,1)S(1)} %bitcast.11, bf16[256,384]{1,0:T(8,128)(2,1)S(1)} %bitcast.12, bf16[128,64,384]{2,1,0:T(8,128)(2,1)S(1)} %copy-done), custom_call_target="tpu_custom_call" | custom-call | flops 6845104128 | bytes 8388608 | tf_op jit(solution)/shard_map/attention/pallas_call | solution.py:93
  51.9 0.0 all-to-all-done.1
  51.9 0.7 grad_pred.1.refs_8_
  52.6 2.7 %collective-permute-start.7 = (bf16[256,1152]{1,0:T(8,128)(2,1)S(1)}, bf16[256,1152]{1,0:T(8,128)(2,1)S(1)}, u32[]{:S(2)}, u32[]{:S(2)}) collective-permute-start(bf16[256,1152]{1,0:T(8,128)(2,1)S(1)} %grad_pred.1.refs_8_), channel_id=1, source_target_pairs={{0,6},{1,7},{2,0},{3,1},{4,2},{5,3},{6,4},{7,5},{8,14},{9,15},{10,... | collective-permute-start | bytes 1769480 | tf_op jit(solution)/shard_map/ppermute | solution.py:357
  55.3 0.0 collective-permute-done.3.refs_2_
  55.3 0.0 collective-permute-start.6
  55.3 0.0 collective-permute-done.2.refs_1_
  55.3 0.0 collective-permute-done.1.refs_3_
  55.3 1.0 collective-permute-done.refs_4_
  56.3 1.2 %collective-permute-start.8 = (bf16[768,256]{1,0:T(8,128)(2,1)}, bf16[768,256]{1,0:T(8,128)(2,1)S(1)}, u32[]{:S(2)}, u32[]{:S(2)}) collective-permute-start(bf16[768,256]{1,0:T(8,128)(2,1)} %collective-permute-done.refs_4_), channel_id=1, source_target_pairs={{0,16},{16,32},{32,48},{48,0},{64,80},{80,96},{96,112},{112,64},{1... | collective-permute-start | bytes 1179656 | tf_op jit(solution)/shard_map/ppermute | solution.py:359
  57.5 2.5 %collective-permute-start.5 = (bf16[768,256]{1,0:T(8,128)(2,1)}, bf16[768,256]{1,0:T(8,128)(2,1)S(1)}, u32[]{:S(2)}, u32[]{:S(2)}) collective-permute-start(bf16[768,256]{1,0:T(8,128)(2,1)} %collective-permute-done.refs_4_), channel_id=1, source_target_pairs={{0,32},{16,48},{32,0},{48,16},{64,96},{80,112},{96,64},{112,80},{1... | collective-permute-start | bytes 1179656 | tf_op jit(solution)/shard_map/ppermute | solution.py:361
  59.9 1.2 %collective-permute-start.4 = (bf16[768,256]{1,0:T(8,128)(2,1)}, bf16[768,256]{1,0:T(8,128)(2,1)S(1)}, u32[]{:S(2)}, u32[]{:S(2)}) collective-permute-start(bf16[768,256]{1,0:T(8,128)(2,1)} %collective-permute-done.refs_4_), channel_id=1, source_target_pairs={{0,48},{16,0},{32,16},{48,32},{64,112},{80,64},{96,80},{112,96},{1... | collective-permute-start | bytes 1179656 | tf_op jit(solution)/shard_map/ppermute | solution.py:360
  61.1 6.4 %collective-permute-done.8.refs_7_ = bf16[768,256]{1,0:T(8,128)(2,1)S(1)} collective-permute-done((bf16[768,256]{1,0:T(8,128)(2,1)}, bf16[768,256]{1,0:T(8,128)(2,1)S(1)}, u32[]{:S(2)}, u32[]{:S(2)}) %collective-permute-start.8) | collective-permute-done | bytes 393248 | tf_op jit(solution)/shard_map/ppermute | solution.py:359
  67.5 0.0 collective-permute-done.7.refs_9_
  67.5 2.1 %collective-permute-done.6.refs_10_ = bf16[256,1152]{1,0:T(8,128)(2,1)S(1)} collective-permute-done((bf16[256,1152]{1,0:T(8,128)(2,1)S(1)}, bf16[256,1152]{1,0:T(8,128)(2,1)S(1)}, u32[]{:S(2)}, u32[]{:S(2)}) %collective-permute-start.6) | collective-permute-done | bytes 589856 | tf_op jit(solution)/shard_map/ppermute | solution.py:356
  69.6 0.3 collective-permute-start.9
  69.9 2.7 %collective-permute-start.10 = (bf16[128,1152]{1,0:T(8,128)(2,1)S(1)}, bf16[128,1152]{1,0:T(8,128)(2,1)S(1)}, u32[]{:S(2)}, u32[]{:S(2)}) collective-permute-start(bf16[128,1152]{1,0:T(8,128)(2,1)S(1)} %slice.13), channel_id=1, source_target_pairs={{0,6},{1,7},{2,0},{3,1},{4,2},{5,3},{6,4},{7,5},{8,14},{9,15},{10,... | collective-permute-start | bytes 884744 | tf_op jit(solution)/shard_map/ppermute | solution.py:364
  72.6 4.6 %collective-permute-done.5.refs_6_ = bf16[768,256]{1,0:T(8,128)(2,1)S(1)} collective-permute-done((bf16[768,256]{1,0:T(8,128)(2,1)}, bf16[768,256]{1,0:T(8,128)(2,1)S(1)}, u32[]{:S(2)}, u32[]{:S(2)}) %collective-permute-start.5) | collective-permute-done | bytes 393248 | tf_op jit(solution)/shard_map/ppermute | solution.py:361
  77.2 0.0 collective-permute-done.4.refs_5_
  77.2 0.0 collective-permute-done.9.refs_11_
  77.2 0.0 collective-permute-done.10.refs_12_
  77.2 4.0 %outer_send.1 = (bf16[768,1152]{1,0:T(8,128)(2,1)S(1)}, bf16[768,1024]{1,0:T(8,128)(2,1)S(1)}, bf16[1024,1152]{1,0:T(8,128)(2,1)S(1)}) custom-call(bf16[768,256]{1,0:T(8,128)(2,1)S(1)} %get-tuple-element.25.refs_0_, bf16[768,256]{1,0:T(8,128)(2,1)S(1)} %collective-permute-done.2.refs_1_, bf16[768,256]{1,0:T(8,128)(2,1)S(1)} %collective-permute-done.3.refs_2_, ...), custom_call_target="tpu_custom_call" | custom-call | flops 1811939328 | bytes 8388608 | tf_op jit(solution)/shard_map/outer_send/pallas_call | solution.py:299
  81.2 3.4 %collective-permute-start.11 = (bf16[768,1152]{1,0:T(8,128)(2,1)S(1)}, bf16[768,1152]{1,0:T(8,128)(2,1)S(1)}, u32[]{:S(2)}, u32[]{:S(2)}) collective-permute-start(bf16[768,1152]{1,0:T(8,128)(2,1)S(1)} %get-tuple-element.40), channel_id=1, source_target_pairs={{0,1},{1,0},{2,3},{3,2},{4,5},{5,4},{6,7},{7,6},{8,9},{9,8},{10,11... | collective-permute-start | bytes 5308424 | tf_op jit(solution)/shard_map/ppermute | solution.py:368
  84.6 1.2 %outer_keep.2 = f32[384,1152]{1,0:T(8,128)S(1)} custom-call(bf16[768,1024]{1,0:T(8,128)(2,1)S(1)} %get-tuple-element.41.x_ref, bf16[1024,1152]{1,0:T(8,128)(2,1)S(1)} %get-tuple-element.39.g_ref), custom_call_target="tpu_custom_call" | custom-call | flops 905969664 | bytes 4194304 | tf_op jit(solution)/shard_map/outer_keep/pallas_call | solution.py:324
  85.7 2.1 %collective-permute-done.11 = bf16[768,1152]{1,0:T(8,128)(2,1)S(1)} collective-permute-done((bf16[768,1152]{1,0:T(8,128)(2,1)S(1)}, bf16[768,1152]{1,0:T(8,128)(2,1)S(1)}, u32[]{:S(2)}, u32[]{:S(2)}) %collective-permute-start.11) | collective-permute-done | bytes 1769504 | tf_op jit(solution)/shard_map/ppermute | solution.py:368
  87.9 0.2 add_convert_fusion.1
  88.0 0.7 collective-permute-start.12
  88.7 1.2 %outer_keep.3 = f32[384,1152]{1,0:T(8,128)S(1)} custom-call(bf16[768,1024]{1,0:T(8,128)(2,1)S(1)} %get-tuple-element.41.x_ref, bf16[1024,1152]{1,0:T(8,128)(2,1)S(1)} %get-tuple-element.39.g_ref), custom_call_target="tpu_custom_call" | custom-call | flops 905969664 | bytes 4194304 | tf_op jit(solution)/shard_map/outer_keep/pallas_call | solution.py:324
  89.9 19.1 %collective-permute-done.12 = bf16[384,1152]{1,0:T(8,128)(2,1)S(1)} collective-permute-done((bf16[384,1152]{1,0:T(8,128)(2,1)S(1)}, bf16[384,1152]{1,0:T(8,128)(2,1)S(1)}, u32[]{:S(2)}, u32[]{:S(2)}) %collective-permute-start.12) | collective-permute-done | bytes 884768 | tf_op jit(solution)/shard_map/ppermute | solution.py:373
  109.0 1.2 %add_convert_fusion = bf16[384,1152]{1,0:T(8,128)(2,1)} fusion(bf16[384,1152]{1,0:T(8,128)(2,1)S(1)} %collective-permute-done.12, f32[384,1152]{1,0:T(8,128)S(1)} %outer_keep.3, bf16[768,1152]{1,0:T(8,128)(2,1)S(1)} %collective-permute-done.11), kind=kLoop, calls=%fused_computation | loop fusion | flops 2211840 | bytes 4423680 | tf_op jit(solution)/shard_map/convert_element_type | solution.py:373
  (2 shorter events, 0.0 us)
Async XLA Ops:
  3.3 21.8 %all-to-all-start = ((bf16[16,32,896]{2,1,0:T(8,128)(2,1)}), bf16[16,32,896]{2,1,0:T(8,128)(2,1)S(1)}, u32[]{:S(2)}, u32[]{:S(2)}) async-start(bf16[16,32,896]{2,1,0:T(8,128)(2,1)} %bitcast.16), calls=%async_computation | async-start | bytes 1835008 | tf_op jit(solution)/shard_map/all_to_all | solution.py:340
  23.9 14.1 %copy-start.1 = (bf16[1,16,16,1152]{3,2,1,0:T(8,128)(2,1)S(1)}, bf16[1,16,16,1152]{3,2,1,0:T(8,128)(2,1)}, u32[]{:S(2)}) copy-start(bf16[1,16,16,1152]{3,2,1,0:T(8,128)(2,1)} %param.8) | copy-start | bytes 1769476
  23.9 14.1 %copy-start.3 = (s32[1,64]{1,0:T(1,128)S(1)}, s32[1,64]{1,0:T(1,128)}, u32[]{:S(2)}) copy-start(s32[1,64]{1,0:T(1,128)} %param.11) | copy-start | bytes 772
  26.0 25.9 %all-to-all-start.1 = ((bf16[16,32,1152]{2,1,0:T(8,128)(2,1)}), bf16[16,32,1152]{2,1,0:T(8,128)(2,1)S(1)}, u32[]{:S(2)}, u32[]{:S(2)}) async-start(bf16[16,32,1152]{2,1,0:T(8,128)(2,1)} %bitcast.5), calls=%async_computation.1 | async-start | bytes 2359296 | tf_op jit(solution)/shard_map/all_to_all | solution.py:345
  30.6 24.7 %collective-permute-start.3 = (bf16[768,256]{1,0:T(8,128)(2,1)S(1)}, bf16[768,256]{1,0:T(8,128)(2,1)S(1)}, u32[]{:S(2)}, u32[]{:S(2)}) collective-permute-start(bf16[768,256]{1,0:T(8,128)(2,1)S(1)} %get-tuple-element.25.refs_0_), channel_id=1, source_target_pairs={{0,32},{16,48},{32,0},{48,16},{64,96},{80,112},{96,64},{112,80},{1... | collective-permute-start | bytes 1179656 | tf_op jit(solution)/shard_map/ppermute | solution.py:350
  33.3 22.0 %collective-permute-start.2 = (bf16[768,256]{1,0:T(8,128)(2,1)S(1)}, bf16[768,256]{1,0:T(8,128)(2,1)S(1)}, u32[]{:S(2)}, u32[]{:S(2)}) collective-permute-start(bf16[768,256]{1,0:T(8,128)(2,1)S(1)} %get-tuple-element.25.refs_0_), channel_id=1, source_target_pairs={{0,48},{16,0},{32,16},{48,32},{64,112},{80,64},{96,80},{112,96},{1... | collective-permute-start | bytes 1179656 | tf_op jit(solution)/shard_map/ppermute | solution.py:349
  34.2 21.1 %collective-permute-start.1 = (bf16[768,256]{1,0:T(8,128)(2,1)S(1)}, bf16[768,256]{1,0:T(8,128)(2,1)}, u32[]{:S(2)}, u32[]{:S(2)}) collective-permute-start(bf16[768,256]{1,0:T(8,128)(2,1)S(1)} %get-tuple-element.25.refs_0_), channel_id=1, source_target_pairs={{0,16},{16,32},{32,48},{48,0},{64,80},{80,96},{96,112},{112,64},{1... | collective-permute-start | bytes 1179656 | tf_op jit(solution)/shard_map/ppermute | solution.py:348
  34.8 21.5 %collective-permute-start = (bf16[768,256]{1,0:T(8,128)(2,1)S(1)}, bf16[768,256]{1,0:T(8,128)(2,1)}, u32[]{:S(2)}, u32[]{:S(2)}) collective-permute-start(bf16[768,256]{1,0:T(8,128)(2,1)S(1)} %get-tuple-element.25.refs_0_), channel_id=1, source_target_pairs={{0,64},{16,80},{32,96},{48,112},{64,0},{80,16},{96,32},{112,48},{1... | collective-permute-start | bytes 1179656 | tf_op jit(solution)/shard_map/ppermute | solution.py:347
  38.1 2.8 %copy-start = (bf16[128,64,384]{2,1,0:T(8,128)(2,1)S(1)}, bf16[128,64,384]{2,1,0:T(8,128)(2,1)}, u32[]{:S(2)}) copy-start(bf16[128,64,384]{2,1,0:T(8,128)(2,1)} %pool_ref.1) | copy-start | bytes 18874372
  40.9 0.9 copy-start.2
  52.6 14.9 %collective-permute-start.7 = (bf16[256,1152]{1,0:T(8,128)(2,1)S(1)}, bf16[256,1152]{1,0:T(8,128)(2,1)S(1)}, u32[]{:S(2)}, u32[]{:S(2)}) collective-permute-start(bf16[256,1152]{1,0:T(8,128)(2,1)S(1)} %grad_pred.1.refs_8_), channel_id=1, source_target_pairs={{0,6},{1,7},{2,0},{3,1},{4,2},{5,3},{6,4},{7,5},{8,14},{9,15},{10,... | collective-permute-start | bytes 1769480 | tf_op jit(solution)/shard_map/ppermute | solution.py:357
  55.3 14.3 %collective-permute-start.6 = (bf16[256,1152]{1,0:T(8,128)(2,1)S(1)}, bf16[256,1152]{1,0:T(8,128)(2,1)S(1)}, u32[]{:S(2)}, u32[]{:S(2)}) collective-permute-start(bf16[256,1152]{1,0:T(8,128)(2,1)S(1)} %grad_pred.1.refs_8_), channel_id=1, source_target_pairs={{0,2},{1,3},{2,4},{3,5},{4,6},{5,7},{6,0},{7,1},{8,10},{9,11},{10,... | collective-permute-start | bytes 1769480 | tf_op jit(solution)/shard_map/ppermute | solution.py:356
  56.3 11.2 %collective-permute-start.8 = (bf16[768,256]{1,0:T(8,128)(2,1)}, bf16[768,256]{1,0:T(8,128)(2,1)S(1)}, u32[]{:S(2)}, u32[]{:S(2)}) collective-permute-start(bf16[768,256]{1,0:T(8,128)(2,1)} %collective-permute-done.refs_4_), channel_id=1, source_target_pairs={{0,16},{16,32},{32,48},{48,0},{64,80},{80,96},{96,112},{112,64},{1... | collective-permute-start | bytes 1179656 | tf_op jit(solution)/shard_map/ppermute | solution.py:359
  57.5 19.7 %collective-permute-start.5 = (bf16[768,256]{1,0:T(8,128)(2,1)}, bf16[768,256]{1,0:T(8,128)(2,1)S(1)}, u32[]{:S(2)}, u32[]{:S(2)}) collective-permute-start(bf16[768,256]{1,0:T(8,128)(2,1)} %collective-permute-done.refs_4_), channel_id=1, source_target_pairs={{0,32},{16,48},{32,0},{48,16},{64,96},{80,112},{96,64},{112,80},{1... | collective-permute-start | bytes 1179656 | tf_op jit(solution)/shard_map/ppermute | solution.py:361
  59.9 17.3 %collective-permute-start.4 = (bf16[768,256]{1,0:T(8,128)(2,1)}, bf16[768,256]{1,0:T(8,128)(2,1)S(1)}, u32[]{:S(2)}, u32[]{:S(2)}) collective-permute-start(bf16[768,256]{1,0:T(8,128)(2,1)} %collective-permute-done.refs_4_), channel_id=1, source_target_pairs={{0,48},{16,0},{32,16},{48,32},{64,112},{80,64},{96,80},{112,96},{1... | collective-permute-start | bytes 1179656 | tf_op jit(solution)/shard_map/ppermute | solution.py:360
  69.6 7.6 %collective-permute-start.9 = (bf16[128,1152]{1,0:T(8,128)(2,1)S(1)}, bf16[128,1152]{1,0:T(8,128)(2,1)S(1)}, u32[]{:S(2)}, u32[]{:S(2)}) collective-permute-start(bf16[128,1152]{1,0:T(8,128)(2,1)S(1)} %slice.12), channel_id=1, source_target_pairs={{0,2},{1,3},{2,4},{3,5},{4,6},{5,7},{6,0},{7,1},{8,10},{9,11},{10,... | collective-permute-start | bytes 884744 | tf_op jit(solution)/shard_map/ppermute | solution.py:363
  69.9 7.3 %collective-permute-start.10 = (bf16[128,1152]{1,0:T(8,128)(2,1)S(1)}, bf16[128,1152]{1,0:T(8,128)(2,1)S(1)}, u32[]{:S(2)}, u32[]{:S(2)}) collective-permute-start(bf16[128,1152]{1,0:T(8,128)(2,1)S(1)} %slice.13), channel_id=1, source_target_pairs={{0,6},{1,7},{2,0},{3,1},{4,2},{5,3},{6,4},{7,5},{8,14},{9,15},{10,... | collective-permute-start | bytes 884744 | tf_op jit(solution)/shard_map/ppermute | solution.py:364
  81.2 6.7 %collective-permute-start.11 = (bf16[768,1152]{1,0:T(8,128)(2,1)S(1)}, bf16[768,1152]{1,0:T(8,128)(2,1)S(1)}, u32[]{:S(2)}, u32[]{:S(2)}) collective-permute-start(bf16[768,1152]{1,0:T(8,128)(2,1)S(1)} %get-tuple-element.40), channel_id=1, source_target_pairs={{0,1},{1,0},{2,3},{3,2},{4,5},{5,4},{6,7},{7,6},{8,9},{9,8},{10,11... | collective-permute-start | bytes 5308424 | tf_op jit(solution)/shard_map/ppermute | solution.py:368
  88.0 20.9 %collective-permute-start.12 = (bf16[384,1152]{1,0:T(8,128)(2,1)S(1)}, bf16[384,1152]{1,0:T(8,128)(2,1)S(1)}, u32[]{:S(2)}, u32[]{:S(2)}) collective-permute-start(bf16[384,1152]{1,0:T(8,128)(2,1)S(1)} %add_convert_fusion.1), channel_id=1, source_target_pairs={{0,8},{1,9},{2,10},{3,11},{4,12},{5,13},{6,14},{7,15},{8,0},{9,1},... | collective-permute-start | bytes 2654216 | tf_op jit(solution)/shard_map/ppermute | solution.py:373

commit v4 on v3

--- a/solution.py
+++ b/solution.py
@@ -272,8 +272,8 @@
     )(meta, y, tap)
 
 
-def send_kernel(*refs):
-    xs, gs, (out_ref, keep_ref, gbuf_ref, xbuf) = refs[:8], refs[8:13], refs[13:]
+def first_kernel(*refs):
+    xs, gs, (out_ref, send_ref, keep_ref, gbuf_ref) = refs[:8], refs[8:13], refs[13:]
     _, y, _, h, x = coordinates()
     for ref, dy, lo in zip(gs, (0, 1, 3, 2, 2), (0, 0, 0, 0, 128)):
         at = pl.multiple_of(((y + dy + 4 - x) % 4) * 256 + lo, 128)
@@ -283,26 +283,28 @@
 
         @pl.when(h == 0)
         def _():
-            xbuf[:, here] = xs[i][...]
+            send_ref[:, here] = xs[i][...]
             keep_ref[:, here] = xs[4 + i][...]
 
         @pl.when(h == 1)
         def _():
-            xbuf[:, here] = xs[4 + i][...]
+            send_ref[:, here] = xs[4 + i][...]
             keep_ref[:, here] = xs[i][...]
 
-    out_ref[...] = jnp.dot(xbuf[...], gbuf_ref[...], preferred_element_type=F32).astype(BF)
-
-
-def outer_send(xs, gs):
+    out_ref[...] = jnp.dot(
+        send_ref[:384, :], gbuf_ref[...], preferred_element_type=F32
+    ).astype(BF)
+
+
+def outer_first(xs, gs):
     m = gs[0].shape[1]
     return pl.pallas_call(
-        send_kernel,
+        first_kernel,
         in_specs=[pl.BlockSpec(memory_space=pltpu.VMEM)] * 13,
-        out_specs=[pl.BlockSpec(memory_space=pltpu.VMEM)] * 3,
-        scratch_shapes=[pltpu.VMEM((768, 1024), BF)],
+        out_specs=[pl.BlockSpec(memory_space=pltpu.VMEM)] * 4,
         out_shape=[
-            jax.ShapeDtypeStruct((768, m), BF),
+            jax.ShapeDtypeStruct((384, m), BF),
+            jax.ShapeDtypeStruct((768, 1024), BF),
             jax.ShapeDtypeStruct((768, 1024), BF),
             jax.ShapeDtypeStruct((1024, m), BF),
         ],
@@ -310,28 +312,32 @@
         cost_estimate=pl.CostEstimate(
             flops=2 * 768 * 1024 * m, bytes_accessed=8 * 2**20, transcendentals=0
         ),
-        name="outer_send",
+        name="outer_first",
     )(*xs, *gs)
 
 
-def keep_kernel(x_ref, g_ref, out_ref, *, lo):
+def rows_kernel(x_ref, g_ref, *refs, lo):
+    added, out_ref = refs[:-1], refs[-1]
     rows = out_ref.shape[0]
-    out_ref[...] = jnp.dot(x_ref[lo : lo + rows, :], g_ref[...], preferred_element_type=F32)
-
-
-def outer_keep(x, g, lo):
+    total = jnp.dot(x_ref[lo : lo + rows, :], g_ref[...], preferred_element_type=F32)
+    for ref in added:
+        total += ref[...].astype(F32)
+    out_ref[...] = total.astype(out_ref.dtype)
+
+
+def outer_rows(x, g, lo, dtype, *added):
     m = g.shape[1]
     return pl.pallas_call(
-        functools.partial(keep_kernel, lo=lo),
-        in_specs=[pl.BlockSpec(memory_space=pltpu.VMEM)] * 2,
+        functools.partial(rows_kernel, lo=lo),
+        in_specs=[pl.BlockSpec(memory_space=pltpu.VMEM)] * (2 + len(added)),
         out_specs=pl.BlockSpec(memory_space=pltpu.VMEM),
-        out_shape=jax.ShapeDtypeStruct((384, m), F32),
+        out_shape=jax.ShapeDtypeStruct((384, m), dtype),
         compiler_params=pltpu.CompilerParams(vmem_limit_bytes=10 * MIB),
         cost_estimate=pl.CostEstimate(
             flops=2 * 384 * 1024 * m, bytes_accessed=4 * 2**20, transcendentals=0
         ),
-        name="outer_keep",
-    )(x, g)
+        name="outer_rows",
+    )(x, g, *added)
 
 
 def body(queries, responses, cache_pool, page_table, lengths, routes, student_rows, projection):
@@ -364,12 +370,12 @@
     gd = lax.ppermute(gb[128:], "grp", y_shift(-1))
     xs = (mine, mb, mc, ma, other, ob, oc, oa)
 
-    send, kept, grads = outer_send(xs, (g, gb, ga, gc, gd))
+    send, sent_x, kept_x, grads = outer_first(xs, (g, gb, ga, gc, gd))
     got = lax.ppermute(send, "grp", C_SWAP)
-    to_z = outer_keep(kept, grads, 0) + got[:384].astype(F32)
-    to_z = to_z.astype(BF)
-    kept, to_z = lax.optimization_barrier((kept, to_z))
-    stay = outer_keep(kept, grads, 384) + got[384:].astype(F32)
+    send = outer_rows(sent_x, grads, 384, BF)
+    got_own = lax.ppermute(send, "grp", C_SWAP)
+    to_z = outer_rows(kept_x, grads, 0, BF, got)
+    stay = outer_rows(kept_x, grads, 384, F32, got_own)
     return (stay + lax.ppermute(to_z, "grp", Z_SWAP).astype(F32)).astype(BF)
 
 

time: 111 us -> 109 us (0.982)
  waiting for transfers between devices: 36.5 us -> 35.2 us
    ppermute x1, waiting for transfers between devices: 2.14 us -> 0.77 us  [body(): got = lax.ppermute(send, 'grp', C_SWAP)]
    pallas_call x3 -> x4, Pallas kernels: 6.3 us -> 6.52 us  [the longest x3 3.59 us: outer_rows(): pl.pallas_call(functools.partial(rows_kernel, lo=lo), in_specs=[pl.BlockS...]
  transfers between devices with their start and end apart: 15 -> 16, of which waited for: 7 -> 7; matrix products, arithmetic and copies ran while one was open for 0% -> 0% of each run, Pallas kernels for 24% -> 25%
where the time goes in v4:
time: 109 us
  waiting for transfers between devices  35.2 us (32%)
  Pallas kernels  34.6 us (32%)
  starting transfers between devices  33.9 us (31%)
  local copies, waits for them, and re-layouts  3.77 us (3%)
  other arithmetic  1.09 us (1%)
    ppermute x1, waiting for transfers between devices, body(): return (stay + lax.ppermute(to_z, 'grp', Z_SWAP).astype(F32)).astype(BF)  19.1 us
    pallas_call x1, Pallas kernels, predict(): pl.pallas_call(predict_kernel, grid=(k // block,), in_specs=[pl.BlockSpec...  13.3 us
    pallas_call x1, Pallas kernels, attention(): pl.pallas_call(functools.partial(attention_kernel, chunk=chunk, mb=mb), g...  9.95 us
    all_to_all x1, starting transfers between devices, body(): lax.all_to_all(share, 'grp', split_axis=0, concat_axis=0, tiled=True)  7.35 us
    ppermute x1, waiting for transfers between devices, body(): oa = lax.ppermute(other, 'tp', x_shift(1))  6.58 us
    ppermute x1, waiting for transfers between devices, body(): oc = lax.ppermute(other, 'tp', x_shift(2))  4.78 us
    all_to_all x1, starting transfers between devices, body(): lax.all_to_all(predicted, 'grp', split_axis=0, concat_axis=0, tiled=True)  4.58 us
    unnamed x8, local copies, waits for them, and re-layouts  3.72 us
  transfers between devices with their start and end apart: 16, of which 7 were waited for; matrix products, arithmetic and copies ran while one was open for 0% of the time, Pallas kernels for 25%

profile of v4, /device:TPU:1, one launch (start us, length us, event | category | flops | bytes accessed | tf_op | source)
XLA Modules:
  0.0 108.7 jit_solution(13154264780368154069)
XLA Ops:
  0.0 3.3 %pick.1 = bf16[512,896]{1,0:T(8,128)(2,1)} custom-call(s32[16]{0:T(128)} %bitcast.17, s32[16,16]{1,0:T(8,128)} %lengths.1, bf16[512,6144]{1,0:T(8,128)(2,1)} %bitcast.14), custom_call_target="tpu_custom_call" | custom-call | bytes 3145728 | tf_op jit(solution)/shard_map/pick/pallas_call | solution.py:187
  3.3 7.4 %all-to-all-start = ((bf16[16,32,896]{2,1,0:T(8,128)(2,1)}), bf16[16,32,896]{2,1,0:T(8,128)(2,1)S(1)}, u32[]{:S(2)}, u32[]{:S(2)}) async-start(bf16[16,32,896]{2,1,0:T(8,128)(2,1)} %bitcast.16), calls=%async_computation | async-start | bytes 1835008 | tf_op jit(solution)/shard_map/all_to_all | solution.py:346
  10.6 13.3 %predict.1 = bf16[512,1152]{1,0:T(8,128)(2,1)} custom-call(bf16[512,6144]{1,0:T(8,128)(2,1)} %bitcast.15, bf16[6144,1152]{1,0:T(8,128)(2,1)} %p_ref.1), custom_call_target="tpu_custom_call" | custom-call | flops 7247757312 | bytes 21626880 | tf_op jit(solution)/shard_map/predict/pallas_call | solution.py:138
  23.9 0.0 copy-start.1
  23.9 0.0 copy-start.3
  23.9 1.2 %all-to-all-done = bf16[16,32,896]{2,1,0:T(8,128)(2,1)S(1)} async-done(((bf16[16,32,896]{2,1,0:T(8,128)(2,1)}), bf16[16,32,896]{2,1,0:T(8,128)(2,1)S(1)}, u32[]{:S(2)}, u32[]{:S(2)}) %all-to-all-start) | async-done | bytes 917536 | tf_op jit(solution)/shard_map/all_to_all | solution.py:346
  25.1 0.9 compact.1
  26.0 4.6 %all-to-all-start.1 = ((bf16[16,32,1152]{2,1,0:T(8,128)(2,1)}), bf16[16,32,1152]{2,1,0:T(8,128)(2,1)S(1)}, u32[]{:S(2)}, u32[]{:S(2)}) async-start(bf16[16,32,1152]{2,1,0:T(8,128)(2,1)} %bitcast.5), calls=%async_computation.1 | async-start | bytes 2359296 | tf_op jit(solution)/shard_map/all_to_all | solution.py:351
  30.5 2.7 %collective-permute-start.3 = (bf16[768,256]{1,0:T(8,128)(2,1)S(1)}, bf16[768,256]{1,0:T(8,128)(2,1)S(1)}, u32[]{:S(2)}, u32[]{:S(2)}) collective-permute-start(bf16[768,256]{1,0:T(8,128)(2,1)S(1)} %get-tuple-element.24.refs_0_), channel_id=1, source_target_pairs={{0,32},{16,48},{32,0},{48,16},{64,96},{80,112},{96,64},{112,80},{1... | collective-permute-start | bytes 1179656 | tf_op jit(solution)/shard_map/ppermute | solution.py:356
  33.3 0.9 collective-permute-start.2
  34.1 0.6 collective-permute-start.1
  34.8 3.3 %collective-permute-start = (bf16[768,256]{1,0:T(8,128)(2,1)S(1)}, bf16[768,256]{1,0:T(8,128)(2,1)}, u32[]{:S(2)}, u32[]{:S(2)}) collective-permute-start(bf16[768,256]{1,0:T(8,128)(2,1)S(1)} %get-tuple-element.24.refs_0_), channel_id=1, source_target_pairs={{0,64},{16,80},{32,96},{48,112},{64,0},{80,16},{96,32},{112,48},{1... | collective-permute-start | bytes 1179656 | tf_op jit(solution)/shard_map/ppermute | solution.py:353
  38.0 0.0 copy-done.1
  38.0 0.0 copy-done.3
  38.1 0.0 copy-start
  38.1 2.8 %copy-done = bf16[128,64,384]{2,1,0:T(8,128)(2,1)S(1)} copy-done((bf16[128,64,384]{2,1,0:T(8,128)(2,1)S(1)}, bf16[128,64,384]{2,1,0:T(8,128)(2,1)}, u32[]{:S(2)}) %copy-start) | copy-done | bytes 6291480
  40.8 0.0 copy-start.2
  40.8 0.9 copy-done.2
  41.8 9.9 %attention.1.tap_ref = bf16[256,1152]{1,0:T(8,128)(2,1)S(1)} custom-call(s32[64]{0:T(128)S(1)} %bitcast.13, bf16[256,1152]{1,0:T(8,128)(2,1)S(1)} %bitcast.11, bf16[256,384]{1,0:T(8,128)(2,1)S(1)} %bitcast.12, bf16[128,64,384]{2,1,0:T(8,128)(2,1)S(1)} %copy-done), custom_call_target="tpu_custom_call" | custom-call | flops 6845104128 | bytes 8388608 | tf_op jit(solution)/shard_map/attention/pallas_call | solution.py:93
  51.7 0.0 all-to-all-done.1
  51.7 0.7 grad_pred.1.refs_8_
  52.4 2.7 %collective-permute-start.7 = (bf16[256,1152]{1,0:T(8,128)(2,1)S(1)}, bf16[256,1152]{1,0:T(8,128)(2,1)S(1)}, u32[]{:S(2)}, u32[]{:S(2)}) collective-permute-start(bf16[256,1152]{1,0:T(8,128)(2,1)S(1)} %grad_pred.1.refs_8_), channel_id=1, source_target_pairs={{0,6},{1,7},{2,0},{3,1},{4,2},{5,3},{6,4},{7,5},{8,14},{9,15},{10,... | collective-permute-start | bytes 1769480 | tf_op jit(solution)/shard_map/ppermute | solution.py:363
  55.1 0.0 collective-permute-done.3.refs_2_
  55.1 0.0 collective-permute-start.6
  55.1 0.0 collective-permute-done.2.refs_1_
  55.1 0.0 collective-permute-done.1.refs_3_
  55.1 1.1 %collective-permute-done.refs_4_ = bf16[768,256]{1,0:T(8,128)(2,1)} collective-permute-done((bf16[768,256]{1,0:T(8,128)(2,1)S(1)}, bf16[768,256]{1,0:T(8,128)(2,1)}, u32[]{:S(2)}, u32[]{:S(2)}) %collective-permute-start) | collective-permute-done | bytes 393248 | tf_op jit(solution)/shard_map/ppermute | solution.py:353
  56.3 1.2 %collective-permute-start.8 = (bf16[768,256]{1,0:T(8,128)(2,1)}, bf16[768,256]{1,0:T(8,128)(2,1)S(1)}, u32[]{:S(2)}, u32[]{:S(2)}) collective-permute-start(bf16[768,256]{1,0:T(8,128)(2,1)} %collective-permute-done.refs_4_), channel_id=1, source_target_pairs={{0,16},{16,32},{32,48},{48,0},{64,80},{80,96},{96,112},{112,64},{1... | collective-permute-start | bytes 1179656 | tf_op jit(solution)/shard_map/ppermute | solution.py:365
  57.5 2.5 %collective-permute-start.5 = (bf16[768,256]{1,0:T(8,128)(2,1)}, bf16[768,256]{1,0:T(8,128)(2,1)S(1)}, u32[]{:S(2)}, u32[]{:S(2)}) collective-permute-start(bf16[768,256]{1,0:T(8,128)(2,1)} %collective-permute-done.refs_4_), channel_id=1, source_target_pairs={{0,32},{16,48},{32,0},{48,16},{64,96},{80,112},{96,64},{112,80},{1... | collective-permute-start | bytes 1179656 | tf_op jit(solution)/shard_map/ppermute | solution.py:367
  59.9 1.2 %collective-permute-start.4 = (bf16[768,256]{1,0:T(8,128)(2,1)}, bf16[768,256]{1,0:T(8,128)(2,1)S(1)}, u32[]{:S(2)}, u32[]{:S(2)}) collective-permute-start(bf16[768,256]{1,0:T(8,128)(2,1)} %collective-permute-done.refs_4_), channel_id=1, source_target_pairs={{0,48},{16,0},{32,16},{48,32},{64,112},{80,64},{96,80},{112,96},{1... | collective-permute-start | bytes 1179656 | tf_op jit(solution)/shard_map/ppermute | solution.py:366
  61.1 6.6 %collective-permute-done.8.refs_7_ = bf16[768,256]{1,0:T(8,128)(2,1)S(1)} collective-permute-done((bf16[768,256]{1,0:T(8,128)(2,1)}, bf16[768,256]{1,0:T(8,128)(2,1)S(1)}, u32[]{:S(2)}, u32[]{:S(2)}) %collective-permute-start.8) | collective-permute-done | bytes 393248 | tf_op jit(solution)/shard_map/ppermute | solution.py:365
  67.7 0.0 collective-permute-done.7.refs_9_
  67.7 1.7 %collective-permute-done.6.refs_10_ = bf16[256,1152]{1,0:T(8,128)(2,1)S(1)} collective-permute-done((bf16[256,1152]{1,0:T(8,128)(2,1)S(1)}, bf16[256,1152]{1,0:T(8,128)(2,1)S(1)}, u32[]{:S(2)}, u32[]{:S(2)}) %collective-permute-start.6) | collective-permute-done | bytes 589856 | tf_op jit(solution)/shard_map/ppermute | solution.py:362
  69.4 0.3 collective-permute-start.9
  69.7 2.7 %collective-permute-start.10 = (bf16[128,1152]{1,0:T(8,128)(2,1)S(1)}, bf16[128,1152]{1,0:T(8,128)(2,1)S(1)}, u32[]{:S(2)}, u32[]{:S(2)}) collective-permute-start(bf16[128,1152]{1,0:T(8,128)(2,1)S(1)} %slice.7), channel_id=1, source_target_pairs={{0,6},{1,7},{2,0},{3,1},{4,2},{5,3},{6,4},{7,5},{8,14},{9,15},{10,... | collective-permute-start | bytes 884744 | tf_op jit(solution)/shard_map/ppermute | solution.py:370
  72.4 4.8 %collective-permute-done.5.refs_6_ = bf16[768,256]{1,0:T(8,128)(2,1)S(1)} collective-permute-done((bf16[768,256]{1,0:T(8,128)(2,1)}, bf16[768,256]{1,0:T(8,128)(2,1)S(1)}, u32[]{:S(2)}, u32[]{:S(2)}) %collective-permute-start.5) | collective-permute-done | bytes 393248 | tf_op jit(solution)/shard_map/ppermute | solution.py:367
  77.2 0.0 collective-permute-done.4.refs_5_
  77.2 0.0 collective-permute-done.9.refs_11_
  77.2 0.0 collective-permute-done.10.refs_12_
  77.2 2.9 %outer_first.1 = (bf16[384,1152]{1,0:T(8,128)(2,1)S(1)}, bf16[768,1024]{1,0:T(8,128)(2,1)S(1)}, bf16[768,1024]{1,0:T(8,128)(2,1)S(1)}, bf16[1024,1152]{1,0:T(8,128)(2,1)S(1)}) custom-call(bf16[768,256]{1,0:T(8,128)(2,1)S(1)} %get-tuple-element.24.refs_0_, bf16[768,256]{1,0:T(8,128)(2,1)S(1)} %collective-permute-done.2.refs_1_, ...), custom_call_target="tpu_custom_call" | custom-call | flops 1811939328 | bytes 8388608 | tf_op jit(solution)/shard_map/outer_first/pallas_call | solution.py:301
  80.1 3.2 %collective-permute-start.12 = (bf16[384,1152]{1,0:T(8,128)(2,1)S(1)}, bf16[384,1152]{1,0:T(8,128)(2,1)S(1)}, u32[]{:S(2)}, u32[]{:S(2)}) collective-permute-start(bf16[384,1152]{1,0:T(8,128)(2,1)S(1)} %get-tuple-element.40), channel_id=1, source_target_pairs={{0,1},{1,0},{2,3},{3,2},{4,5},{5,4},{6,7},{7,6},{8,9},{9,8},{10,11... | collective-permute-start | bytes 2654216 | tf_op jit(solution)/shard_map/ppermute | solution.py:374
  83.4 1.2 %outer_rows.3 = bf16[384,1152]{1,0:T(8,128)(2,1)S(1)} custom-call(bf16[768,1024]{1,0:T(8,128)(2,1)S(1)} %get-tuple-element.39.x_ref, bf16[1024,1152]{1,0:T(8,128)(2,1)S(1)} %get-tuple-element.38.g_ref), custom_call_target="tpu_custom_call" | custom-call | flops 905969664 | bytes 4194304 | tf_op jit(solution)/shard_map/outer_rows/pallas_call | solution.py:330
  84.6 0.1 collective-permute-start.11
  84.7 0.8 collective-permute-done.12.refs_0_
  85.4 1.2 %outer_rows.5 = bf16[384,1152]{1,0:T(8,128)(2,1)S(1)} custom-call(bf16[768,1024]{1,0:T(8,128)(2,1)S(1)} %get-tuple-element.37.x_ref, bf16[1024,1152]{1,0:T(8,128)(2,1)S(1)} %get-tuple-element.38.g_ref, bf16[384,1152]{1,0:T(8,128)(2,1)S(1)} %collective-permute-done.12.refs_0_), custom_call_target="tpu_custom_call" | custom-call | flops 905969664 | bytes 4194304 | tf_op jit(solution)/shard_map/outer_rows/pallas_call | solution.py:330
  86.6 0.7 collective-permute-start.13
  87.3 0.0 collective-permute-done.11.refs_0_
  87.3 1.2 %outer_rows.4 = f32[384,1152]{1,0:T(8,128)S(1)} custom-call(bf16[768,1024]{1,0:T(8,128)(2,1)S(1)} %get-tuple-element.37.x_ref, bf16[1024,1152]{1,0:T(8,128)(2,1)S(1)} %get-tuple-element.38.g_ref, bf16[384,1152]{1,0:T(8,128)(2,1)S(1)} %collective-permute-done.11.refs_0_), custom_call_target="tpu_custom_call" | custom-call | flops 905969664 | bytes 4194304 | tf_op jit(solution)/shard_map/outer_rows/pallas_call | solution.py:330
  88.5 19.1 %collective-permute-done.13 = bf16[384,1152]{1,0:T(8,128)(2,1)S(1)} collective-permute-done((bf16[384,1152]{1,0:T(8,128)(2,1)S(1)}, bf16[384,1152]{1,0:T(8,128)(2,1)S(1)}, u32[]{:S(2)}, u32[]{:S(2)}) %collective-permute-start.13) | collective-permute-done | bytes 884768 | tf_op jit(solution)/shard_map/ppermute | solution.py:379
  107.6 1.1 %add_convert_fusion = bf16[384,1152]{1,0:T(8,128)(2,1)} fusion(f32[384,1152]{1,0:T(8,128)S(1)} %outer_rows.4, bf16[384,1152]{1,0:T(8,128)(2,1)S(1)} %collective-permute-done.13), kind=kLoop, calls=%fused_computation | loop fusion | flops 1327104 | bytes 3538944 | tf_op jit(solution)/shard_map/convert_element_type | solution.py:379
  (2 shorter events, 0.0 us)
Async XLA Ops:
  3.3 21.8 %all-to-all-start = ((bf16[16,32,896]{2,1,0:T(8,128)(2,1)}), bf16[16,32,896]{2,1,0:T(8,128)(2,1)S(1)}, u32[]{:S(2)}, u32[]{:S(2)}) async-start(bf16[16,32,896]{2,1,0:T(8,128)(2,1)} %bitcast.16), calls=%async_computation | async-start | bytes 1835008 | tf_op jit(solution)/shard_map/all_to_all | solution.py:346
  23.9 14.1 %copy-start.1 = (bf16[1,16,16,1152]{3,2,1,0:T(8,128)(2,1)S(1)}, bf16[1,16,16,1152]{3,2,1,0:T(8,128)(2,1)}, u32[]{:S(2)}) copy-start(bf16[1,16,16,1152]{3,2,1,0:T(8,128)(2,1)} %param.8) | copy-start | bytes 1769476
  23.9 14.1 %copy-start.3 = (s32[1,64]{1,0:T(1,128)S(1)}, s32[1,64]{1,0:T(1,128)}, u32[]{:S(2)}) copy-start(s32[1,64]{1,0:T(1,128)} %param.11) | copy-start | bytes 772
  26.0 25.8 %all-to-all-start.1 = ((bf16[16,32,1152]{2,1,0:T(8,128)(2,1)}), bf16[16,32,1152]{2,1,0:T(8,128)(2,1)S(1)}, u32[]{:S(2)}, u32[]{:S(2)}) async-start(bf16[16,32,1152]{2,1,0:T(8,128)(2,1)} %bitcast.5), calls=%async_computation.1 | async-start | bytes 2359296 | tf_op jit(solution)/shard_map/all_to_all | solution.py:351
  30.5 24.6 %collective-permute-start.3 = (bf16[768,256]{1,0:T(8,128)(2,1)S(1)}, bf16[768,256]{1,0:T(8,128)(2,1)S(1)}, u32[]{:S(2)}, u32[]{:S(2)}) collective-permute-start(bf16[768,256]{1,0:T(8,128)(2,1)S(1)} %get-tuple-element.24.refs_0_), channel_id=1, source_target_pairs={{0,32},{16,48},{32,0},{48,16},{64,96},{80,112},{96,64},{112,80},{1... | collective-permute-start | bytes 1179656 | tf_op jit(solution)/shard_map/ppermute | solution.py:356
  33.3 21.8 %collective-permute-start.2 = (bf16[768,256]{1,0:T(8,128)(2,1)S(1)}, bf16[768,256]{1,0:T(8,128)(2,1)S(1)}, u32[]{:S(2)}, u32[]{:S(2)}) collective-permute-start(bf16[768,256]{1,0:T(8,128)(2,1)S(1)} %get-tuple-element.24.refs_0_), channel_id=1, source_target_pairs={{0,48},{16,0},{32,16},{48,32},{64,112},{80,64},{96,80},{112,96},{1... | collective-permute-start | bytes 1179656 | tf_op jit(solution)/shard_map/ppermute | solution.py:355
  34.1 21.0 %collective-permute-start.1 = (bf16[768,256]{1,0:T(8,128)(2,1)S(1)}, bf16[768,256]{1,0:T(8,128)(2,1)}, u32[]{:S(2)}, u32[]{:S(2)}) collective-permute-start(bf16[768,256]{1,0:T(8,128)(2,1)S(1)} %get-tuple-element.24.refs_0_), channel_id=1, source_target_pairs={{0,16},{16,32},{32,48},{48,0},{64,80},{80,96},{96,112},{112,64},{1... | collective-permute-start | bytes 1179656 | tf_op jit(solution)/shard_map/ppermute | solution.py:354
  34.8 21.5 %collective-permute-start = (bf16[768,256]{1,0:T(8,128)(2,1)S(1)}, bf16[768,256]{1,0:T(8,128)(2,1)}, u32[]{:S(2)}, u32[]{:S(2)}) collective-permute-start(bf16[768,256]{1,0:T(8,128)(2,1)S(1)} %get-tuple-element.24.refs_0_), channel_id=1, source_target_pairs={{0,64},{16,80},{32,96},{48,112},{64,0},{80,16},{96,32},{112,48},{1... | collective-permute-start | bytes 1179656 | tf_op jit(solution)/shard_map/ppermute | solution.py:353
  38.1 2.8 %copy-start = (bf16[128,64,384]{2,1,0:T(8,128)(2,1)S(1)}, bf16[128,64,384]{2,1,0:T(8,128)(2,1)}, u32[]{:S(2)}) copy-start(bf16[128,64,384]{2,1,0:T(8,128)(2,1)} %pool_ref.1) | copy-start | bytes 18874372
  40.8 0.9 copy-start.2
  52.4 15.2 %collective-permute-start.7 = (bf16[256,1152]{1,0:T(8,128)(2,1)S(1)}, bf16[256,1152]{1,0:T(8,128)(2,1)S(1)}, u32[]{:S(2)}, u32[]{:S(2)}) collective-permute-start(bf16[256,1152]{1,0:T(8,128)(2,1)S(1)} %grad_pred.1.refs_8_), channel_id=1, source_target_pairs={{0,6},{1,7},{2,0},{3,1},{4,2},{5,3},{6,4},{7,5},{8,14},{9,15},{10,... | collective-permute-start | bytes 1769480 | tf_op jit(solution)/shard_map/ppermute | solution.py:363
  55.1 14.3 %collective-permute-start.6 = (bf16[256,1152]{1,0:T(8,128)(2,1)S(1)}, bf16[256,1152]{1,0:T(8,128)(2,1)S(1)}, u32[]{:S(2)}, u32[]{:S(2)}) collective-permute-start(bf16[256,1152]{1,0:T(8,128)(2,1)S(1)} %grad_pred.1.refs_8_), channel_id=1, source_target_pairs={{0,2},{1,3},{2,4},{3,5},{4,6},{5,7},{6,0},{7,1},{8,10},{9,11},{10,... | collective-permute-start | bytes 1769480 | tf_op jit(solution)/shard_map/ppermute | solution.py:362
  56.3 11.4 %collective-permute-start.8 = (bf16[768,256]{1,0:T(8,128)(2,1)}, bf16[768,256]{1,0:T(8,128)(2,1)S(1)}, u32[]{:S(2)}, u32[]{:S(2)}) collective-permute-start(bf16[768,256]{1,0:T(8,128)(2,1)} %collective-permute-done.refs_4_), channel_id=1, source_target_pairs={{0,16},{16,32},{32,48},{48,0},{64,80},{80,96},{96,112},{112,64},{1... | collective-permute-start | bytes 1179656 | tf_op jit(solution)/shard_map/ppermute | solution.py:365
  57.5 19.7 %collective-permute-start.5 = (bf16[768,256]{1,0:T(8,128)(2,1)}, bf16[768,256]{1,0:T(8,128)(2,1)S(1)}, u32[]{:S(2)}, u32[]{:S(2)}) collective-permute-start(bf16[768,256]{1,0:T(8,128)(2,1)} %collective-permute-done.refs_4_), channel_id=1, source_target_pairs={{0,32},{16,48},{32,0},{48,16},{64,96},{80,112},{96,64},{112,80},{1... | collective-permute-start | bytes 1179656 | tf_op jit(solution)/shard_map/ppermute | solution.py:367
  59.9 17.3 %collective-permute-start.4 = (bf16[768,256]{1,0:T(8,128)(2,1)}, bf16[768,256]{1,0:T(8,128)(2,1)S(1)}, u32[]{:S(2)}, u32[]{:S(2)}) collective-permute-start(bf16[768,256]{1,0:T(8,128)(2,1)} %collective-permute-done.refs_4_), channel_id=1, source_target_pairs={{0,48},{16,0},{32,16},{48,32},{64,112},{80,64},{96,80},{112,96},{1... | collective-permute-start | bytes 1179656 | tf_op jit(solution)/shard_map/ppermute | solution.py:366
  69.4 7.8 %collective-permute-start.9 = (bf16[128,1152]{1,0:T(8,128)(2,1)S(1)}, bf16[128,1152]{1,0:T(8,128)(2,1)S(1)}, u32[]{:S(2)}, u32[]{:S(2)}) collective-permute-start(bf16[128,1152]{1,0:T(8,128)(2,1)S(1)} %slice.6), channel_id=1, source_target_pairs={{0,2},{1,3},{2,4},{3,5},{4,6},{5,7},{6,0},{7,1},{8,10},{9,11},{10,... | collective-permute-start | bytes 884744 | tf_op jit(solution)/shard_map/ppermute | solution.py:369
  69.7 7.5 %collective-permute-start.10 = (bf16[128,1152]{1,0:T(8,128)(2,1)S(1)}, bf16[128,1152]{1,0:T(8,128)(2,1)S(1)}, u32[]{:S(2)}, u32[]{:S(2)}) collective-permute-start(bf16[128,1152]{1,0:T(8,128)(2,1)S(1)} %slice.7), channel_id=1, source_target_pairs={{0,6},{1,7},{2,0},{3,1},{4,2},{5,3},{6,4},{7,5},{8,14},{9,15},{10,... | collective-permute-start | bytes 884744 | tf_op jit(solution)/shard_map/ppermute | solution.py:370
  80.1 5.3 %collective-permute-start.12 = (bf16[384,1152]{1,0:T(8,128)(2,1)S(1)}, bf16[384,1152]{1,0:T(8,128)(2,1)S(1)}, u32[]{:S(2)}, u32[]{:S(2)}) collective-permute-start(bf16[384,1152]{1,0:T(8,128)(2,1)S(1)} %get-tuple-element.40), channel_id=1, source_target_pairs={{0,1},{1,0},{2,3},{3,2},{4,5},{5,4},{6,7},{7,6},{8,9},{9,8},{10,11... | collective-permute-start | bytes 2654216 | tf_op jit(solution)/shard_map/ppermute | solution.py:374
  84.6 2.7 %collective-permute-start.11 = (bf16[384,1152]{1,0:T(8,128)(2,1)S(1)}, bf16[384,1152]{1,0:T(8,128)(2,1)S(1)}, u32[]{:S(2)}, u32[]{:S(2)}) collective-permute-start(bf16[384,1152]{1,0:T(8,128)(2,1)S(1)} %outer_rows.3), channel_id=1, source_target_pairs={{0,1},{1,0},{2,3},{3,2},{4,5},{5,4},{6,7},{7,6},{8,9},{9,8},{10,11... | collective-permute-start | bytes 2654216 | tf_op jit(solution)/shard_map/ppermute | solution.py:376
  86.6 20.9 %collective-permute-start.13 = (bf16[384,1152]{1,0:T(8,128)(2,1)S(1)}, bf16[384,1152]{1,0:T(8,128)(2,1)S(1)}, u32[]{:S(2)}, u32[]{:S(2)}) collective-permute-start(bf16[384,1152]{1,0:T(8,128)(2,1)S(1)} %outer_rows.5), channel_id=1, source_target_pairs={{0,8},{1,9},{2,10},{3,11},{4,12},{5,13},{6,14},{7,15},{8,0},{9,1},... | collective-permute-start | bytes 2654216 | tf_op jit(solution)/shard_map/ppermute | solution.py:379

commit v5 on v4

--- a/solution.py
+++ b/solution.py
@@ -43,7 +43,11 @@
     return g // 8, (g // 2) % 4, g % 2, t // 4, t % 4
 
 
-def attention_kernel(table, q_ref, resp_ref, pool_ref, out_ref, kv, q2, acc, tops, *, chunk, mb):
+def attention_kernel(
+    table, q_ref, resp_hbm, pool_ref, out_ref, resp_ref, kv, q2, acc, tops, sem, *, chunk, mb
+):
+    resp_copy = pltpu.make_async_copy(resp_hbm, resp_ref, sem)
+    resp_copy.start()
     pages = table.shape[0]
     n = q_ref.shape[0]
     heads = q_ref.shape[1] // HD
@@ -73,6 +77,7 @@
             acc[here, :] = o if first else acc[here, :] * jnp.exp2(old - new) + o
             tops[here, :] = jnp.broadcast_to(new, (mb, 128))
 
+    resp_copy.wait()
     fold(resp_ref[...], True)
     for lo in range(0, pages * PAGE, chunk):
         for j in range(lo // PAGE, (lo + chunk) // PAGE):
@@ -95,13 +100,15 @@
         grid_spec=pltpu.PrefetchScalarGridSpec(
             num_scalar_prefetch=1,
             grid=(),
-            in_specs=[pl.BlockSpec(memory_space=pltpu.VMEM)] * 3,
+            in_specs=[pl.BlockSpec(memory_space=m) for m in (pltpu.VMEM, pl.ANY, pltpu.VMEM)],
             out_specs=pl.BlockSpec(memory_space=pltpu.VMEM),
             scratch_shapes=[
+                pltpu.VMEM(resp.shape, BF),
                 pltpu.VMEM((keys, 2 * HD), BF),
                 pltpu.VMEM((heads * n, 256), BF),
                 pltpu.VMEM((heads * n, 256), F32),
                 pltpu.VMEM((heads * n, 128), F32),
+                pltpu.SemaphoreType.DMA(()),
             ],
         ),
         out_shape=jax.ShapeDtypeStruct((n, width), BF),

time: 109 us -> 109 us (level)
  transfers between devices with their start and end apart: 16 -> 16, of which waited for: 7 -> 7; matrix products, arithmetic and copies ran while one was open for 0% -> 0% of each run, Pallas kernels for 25% -> 26%
where the time goes in v5:
time: 109 us
  Pallas kernels  34.9 us (32%)
  waiting for transfers between devices  34.9 us (32%)
  starting transfers between devices  34.3 us (31%)
  local copies, waits for them, and re-layouts  3.77 us (3%)
  other arithmetic  1.09 us (1%)
    ppermute x1, waiting for transfers between devices, body(): return (stay + lax.ppermute(to_z, 'grp', Z_SWAP).astype(F32)).astype(BF)  19.1 us
    pallas_call x1, Pallas kernels, predict(): pl.pallas_call(predict_kernel, grid=(k // block,), in_specs=[pl.BlockSpec...  13.3 us
    pallas_call x1, Pallas kernels, attention(): pl.pallas_call(functools.partial(attention_kernel, chunk=chunk, mb=mb), g...  10.3 us
    all_to_all x1, starting transfers between devices, body(): lax.all_to_all(share, 'grp', split_axis=0, concat_axis=0, tiled=True)  7.35 us
    ppermute x1, waiting for transfers between devices, body(): oa = lax.ppermute(other, 'tp', x_shift(1))  6.17 us
    all_to_all x1, starting transfers between devices, body(): lax.all_to_all(predicted, 'grp', split_axis=0, concat_axis=0, tiled=True)  4.58 us
    ppermute x1, waiting for transfers between devices, body(): oc = lax.ppermute(other, 'tp', x_shift(2))  4.39 us
    unnamed x8, local copies, waits for them, and re-layouts  3.72 us
  transfers between devices with their start and end apart: 16, of which 7 were waited for; matrix products, arithmetic and copies ran while one was open for 0% of the time, Pallas kernels for 26%

profile of v5, /device:TPU:1, one launch (start us, length us, event | category | flops | bytes accessed | tf_op | source)
XLA Modules:
  0.0 109.0 jit_solution(1431037543702161019)
XLA Ops:
  0.0 3.3 %pick.1 = bf16[512,896]{1,0:T(8,128)(2,1)} custom-call(s32[16]{0:T(128)} %bitcast.17, s32[16,16]{1,0:T(8,128)} %lengths.1, bf16[512,6144]{1,0:T(8,128)(2,1)} %bitcast.14), custom_call_target="tpu_custom_call" | custom-call | bytes 3145728 | tf_op jit(solution)/shard_map/pick/pallas_call | solution.py:194
  3.3 7.4 %all-to-all-start = ((bf16[16,32,896]{2,1,0:T(8,128)(2,1)}), bf16[16,32,896]{2,1,0:T(8,128)(2,1)S(1)}, u32[]{:S(2)}, u32[]{:S(2)}) async-start(bf16[16,32,896]{2,1,0:T(8,128)(2,1)} %bitcast.16), calls=%async_computation | async-start | bytes 1835008 | tf_op jit(solution)/shard_map/all_to_all | solution.py:353
  10.6 13.3 %predict.1 = bf16[512,1152]{1,0:T(8,128)(2,1)} custom-call(bf16[512,6144]{1,0:T(8,128)(2,1)} %bitcast.15, bf16[6144,1152]{1,0:T(8,128)(2,1)} %p_ref.1), custom_call_target="tpu_custom_call" | custom-call | flops 7247757312 | bytes 21626880 | tf_op jit(solution)/shard_map/predict/pallas_call | solution.py:145
  23.9 0.0 copy-start.1
  23.9 0.0 copy-start.3
  23.9 1.2 %all-to-all-done = bf16[16,32,896]{2,1,0:T(8,128)(2,1)S(1)} async-done(((bf16[16,32,896]{2,1,0:T(8,128)(2,1)}), bf16[16,32,896]{2,1,0:T(8,128)(2,1)S(1)}, u32[]{:S(2)}, u32[]{:S(2)}) %all-to-all-start) | async-done | bytes 917536 | tf_op jit(solution)/shard_map/all_to_all | solution.py:353
  25.1 0.9 compact.1
  26.0 4.6 %all-to-all-start.1 = ((bf16[16,32,1152]{2,1,0:T(8,128)(2,1)}), bf16[16,32,1152]{2,1,0:T(8,128)(2,1)S(1)}, u32[]{:S(2)}, u32[]{:S(2)}) async-start(bf16[16,32,1152]{2,1,0:T(8,128)(2,1)} %bitcast.5), calls=%async_computation.1 | async-start | bytes 2359296 | tf_op jit(solution)/shard_map/all_to_all | solution.py:358
  30.5 2.7 %collective-permute-start.3 = (bf16[768,256]{1,0:T(8,128)(2,1)S(1)}, bf16[768,256]{1,0:T(8,128)(2,1)S(1)}, u32[]{:S(2)}, u32[]{:S(2)}) collective-permute-start(bf16[768,256]{1,0:T(8,128)(2,1)S(1)} %get-tuple-element.24.refs_0_), channel_id=1, source_target_pairs={{0,32},{16,48},{32,0},{48,16},{64,96},{80,112},{96,64},{112,80},{1... | collective-permute-start | bytes 1179656 | tf_op jit(solution)/shard_map/ppermute | solution.py:363
  33.3 0.9 collective-permute-start.2
  34.1 0.6 collective-permute-start.1
  34.8 3.3 %collective-permute-start = (bf16[768,256]{1,0:T(8,128)(2,1)S(1)}, bf16[768,256]{1,0:T(8,128)(2,1)}, u32[]{:S(2)}, u32[]{:S(2)}) collective-permute-start(bf16[768,256]{1,0:T(8,128)(2,1)S(1)} %get-tuple-element.24.refs_0_), channel_id=1, source_target_pairs={{0,64},{16,80},{32,96},{48,112},{64,0},{80,16},{96,32},{112,48},{1... | collective-permute-start | bytes 1179656 | tf_op jit(solution)/shard_map/ppermute | solution.py:360
  38.0 0.0 copy-done.1
  38.0 0.0 copy-done.3
  38.1 0.0 copy-start
  38.1 2.8 %copy-done = bf16[128,64,384]{2,1,0:T(8,128)(2,1)S(1)} copy-done((bf16[128,64,384]{2,1,0:T(8,128)(2,1)S(1)}, bf16[128,64,384]{2,1,0:T(8,128)(2,1)}, u32[]{:S(2)}) %copy-start) | copy-done | bytes 6291480
  40.8 0.0 copy-start.2
  40.8 0.9 copy-done.2
  41.8 10.3 %attention.1.tap_ref = bf16[256,1152]{1,0:T(8,128)(2,1)S(1)} custom-call(s32[64]{0:T(128)S(1)} %bitcast.13, bf16[256,1152]{1,0:T(8,128)(2,1)S(1)} %bitcast.11, bf16[256,384]{1,0:T(8,128)(2,1)S(1)} %bitcast.12, bf16[128,64,384]{2,1,0:T(8,128)(2,1)S(1)} %copy-done), custom_call_target="tpu_custom_call" | custom-call | flops 6845104128 | bytes 8388608 | tf_op jit(solution)/shard_map/attention/pallas_call | solution.py:98
  52.1 0.0 all-to-all-done.1
  52.1 0.7 grad_pred.1.refs_8_
  52.8 2.7 %collective-permute-start.7 = (bf16[256,1152]{1,0:T(8,128)(2,1)S(1)}, bf16[256,1152]{1,0:T(8,128)(2,1)S(1)}, u32[]{:S(2)}, u32[]{:S(2)}) collective-permute-start(bf16[256,1152]{1,0:T(8,128)(2,1)S(1)} %grad_pred.1.refs_8_), channel_id=1, source_target_pairs={{0,6},{1,7},{2,0},{3,1},{4,2},{5,3},{6,4},{7,5},{8,14},{9,15},{10,... | collective-permute-start | bytes 1769480 | tf_op jit(solution)/shard_map/ppermute | solution.py:370
  55.4 0.0 collective-permute-done.3.refs_2_
  55.4 0.0 collective-permute-start.6
  55.4 0.0 collective-permute-done.2.refs_1_
  55.5 0.0 collective-permute-done.1.refs_3_
  55.5 0.8 collective-permute-done.refs_4_
  56.3 1.2 %collective-permute-start.8 = (bf16[768,256]{1,0:T(8,128)(2,1)}, bf16[768,256]{1,0:T(8,128)(2,1)S(1)}, u32[]{:S(2)}, u32[]{:S(2)}) collective-permute-start(bf16[768,256]{1,0:T(8,128)(2,1)} %collective-permute-done.refs_4_), channel_id=1, source_target_pairs={{0,16},{16,32},{32,48},{48,0},{64,80},{80,96},{96,112},{112,64},{1... | collective-permute-start | bytes 1179656 | tf_op jit(solution)/shard_map/ppermute | solution.py:372
  57.5 2.5 %collective-permute-start.5 = (bf16[768,256]{1,0:T(8,128)(2,1)}, bf16[768,256]{1,0:T(8,128)(2,1)S(1)}, u32[]{:S(2)}, u32[]{:S(2)}) collective-permute-start(bf16[768,256]{1,0:T(8,128)(2,1)} %collective-permute-done.refs_4_), channel_id=1, source_target_pairs={{0,32},{16,48},{32,0},{48,16},{64,96},{80,112},{96,64},{112,80},{1... | collective-permute-start | bytes 1179656 | tf_op jit(solution)/shard_map/ppermute | solution.py:374
  59.9 1.2 %collective-permute-start.4 = (bf16[768,256]{1,0:T(8,128)(2,1)}, bf16[768,256]{1,0:T(8,128)(2,1)S(1)}, u32[]{:S(2)}, u32[]{:S(2)}) collective-permute-start(bf16[768,256]{1,0:T(8,128)(2,1)} %collective-permute-done.refs_4_), channel_id=1, source_target_pairs={{0,48},{16,0},{32,16},{48,32},{64,112},{80,64},{96,80},{112,96},{1... | collective-permute-start | bytes 1179656 | tf_op jit(solution)/shard_map/ppermute | solution.py:373
  61.1 6.2 %collective-permute-done.8.refs_7_ = bf16[768,256]{1,0:T(8,128)(2,1)S(1)} collective-permute-done((bf16[768,256]{1,0:T(8,128)(2,1)}, bf16[768,256]{1,0:T(8,128)(2,1)S(1)}, u32[]{:S(2)}, u32[]{:S(2)}) %collective-permute-start.8) | collective-permute-done | bytes 393248 | tf_op jit(solution)/shard_map/ppermute | solution.py:372
  67.3 0.0 collective-permute-done.7.refs_9_
  67.3 2.5 %collective-permute-done.6.refs_10_ = bf16[256,1152]{1,0:T(8,128)(2,1)S(1)} collective-permute-done((bf16[256,1152]{1,0:T(8,128)(2,1)S(1)}, bf16[256,1152]{1,0:T(8,128)(2,1)S(1)}, u32[]{:S(2)}, u32[]{:S(2)}) %collective-permute-start.6) | collective-permute-done | bytes 589856 | tf_op jit(solution)/shard_map/ppermute | solution.py:369
  69.8 0.3 collective-permute-start.9
  70.1 2.7 %collective-permute-start.10 = (bf16[128,1152]{1,0:T(8,128)(2,1)S(1)}, bf16[128,1152]{1,0:T(8,128)(2,1)S(1)}, u32[]{:S(2)}, u32[]{:S(2)}) collective-permute-start(bf16[128,1152]{1,0:T(8,128)(2,1)S(1)} %slice.7), channel_id=1, source_target_pairs={{0,6},{1,7},{2,0},{3,1},{4,2},{5,3},{6,4},{7,5},{8,14},{9,15},{10,... | collective-permute-start | bytes 884744 | tf_op jit(solution)/shard_map/ppermute | solution.py:377
  72.7 4.4 %collective-permute-done.5.refs_6_ = bf16[768,256]{1,0:T(8,128)(2,1)S(1)} collective-permute-done((bf16[768,256]{1,0:T(8,128)(2,1)}, bf16[768,256]{1,0:T(8,128)(2,1)S(1)}, u32[]{:S(2)}, u32[]{:S(2)}) %collective-permute-start.5) | collective-permute-done | bytes 393248 | tf_op jit(solution)/shard_map/ppermute | solution.py:374
  77.1 0.0 collective-permute-done.4.refs_5_
  77.1 0.0 collective-permute-done.9.refs_11_
  77.1 0.0 collective-permute-done.10.refs_12_
  77.1 2.9 %outer_first.1 = (bf16[384,1152]{1,0:T(8,128)(2,1)S(1)}, bf16[768,1024]{1,0:T(8,128)(2,1)S(1)}, bf16[768,1024]{1,0:T(8,128)(2,1)S(1)}, bf16[1024,1152]{1,0:T(8,128)(2,1)S(1)}) custom-call(bf16[768,256]{1,0:T(8,128)(2,1)S(1)} %get-tuple-element.24.refs_0_, bf16[768,256]{1,0:T(8,128)(2,1)S(1)} %collective-permute-done.2.refs_1_, ...), custom_call_target="tpu_custom_call" | custom-call | flops 1811939328 | bytes 8388608 | tf_op jit(solution)/shard_map/outer_first/pallas_call | solution.py:308
  80.1 3.6 %collective-permute-start.12 = (bf16[384,1152]{1,0:T(8,128)(2,1)S(1)}, bf16[384,1152]{1,0:T(8,128)(2,1)S(1)}, u32[]{:S(2)}, u32[]{:S(2)}) collective-permute-start(bf16[384,1152]{1,0:T(8,128)(2,1)S(1)} %get-tuple-element.40), channel_id=1, source_target_pairs={{0,1},{1,0},{2,3},{3,2},{4,5},{5,4},{6,7},{7,6},{8,9},{9,8},{10,11... | collective-permute-start | bytes 2654216 | tf_op jit(solution)/shard_map/ppermute | solution.py:381
  83.7 1.2 %outer_rows.3 = bf16[384,1152]{1,0:T(8,128)(2,1)S(1)} custom-call(bf16[768,1024]{1,0:T(8,128)(2,1)S(1)} %get-tuple-element.39.x_ref, bf16[1024,1152]{1,0:T(8,128)(2,1)S(1)} %get-tuple-element.38.g_ref), custom_call_target="tpu_custom_call" | custom-call | flops 905969664 | bytes 4194304 | tf_op jit(solution)/shard_map/outer_rows/pallas_call | solution.py:337
  84.9 0.1 collective-permute-start.11
  85.0 0.8 collective-permute-done.12.refs_0_
  85.8 1.2 %outer_rows.5 = bf16[384,1152]{1,0:T(8,128)(2,1)S(1)} custom-call(bf16[768,1024]{1,0:T(8,128)(2,1)S(1)} %get-tuple-element.37.x_ref, bf16[1024,1152]{1,0:T(8,128)(2,1)S(1)} %get-tuple-element.38.g_ref, bf16[384,1152]{1,0:T(8,128)(2,1)S(1)} %collective-permute-done.12.refs_0_), custom_call_target="tpu_custom_call" | custom-call | flops 905969664 | bytes 4194304 | tf_op jit(solution)/shard_map/outer_rows/pallas_call | solution.py:337
  87.0 0.7 collective-permute-start.13
  87.6 0.0 collective-permute-done.11.refs_0_
  87.6 1.2 %outer_rows.4 = f32[384,1152]{1,0:T(8,128)S(1)} custom-call(bf16[768,1024]{1,0:T(8,128)(2,1)S(1)} %get-tuple-element.37.x_ref, bf16[1024,1152]{1,0:T(8,128)(2,1)S(1)} %get-tuple-element.38.g_ref, bf16[384,1152]{1,0:T(8,128)(2,1)S(1)} %collective-permute-done.11.refs_0_), custom_call_target="tpu_custom_call" | custom-call | flops 905969664 | bytes 4194304 | tf_op jit(solution)/shard_map/outer_rows/pallas_call | solution.py:337
  88.8 19.1 %collective-permute-done.13 = bf16[384,1152]{1,0:T(8,128)(2,1)S(1)} collective-permute-done((bf16[384,1152]{1,0:T(8,128)(2,1)S(1)}, bf16[384,1152]{1,0:T(8,128)(2,1)S(1)}, u32[]{:S(2)}, u32[]{:S(2)}) %collective-permute-start.13) | collective-permute-done | bytes 884768 | tf_op jit(solution)/shard_map/ppermute | solution.py:386
  107.9 1.1 %add_convert_fusion = bf16[384,1152]{1,0:T(8,128)(2,1)} fusion(f32[384,1152]{1,0:T(8,128)S(1)} %outer_rows.4, bf16[384,1152]{1,0:T(8,128)(2,1)S(1)} %collective-permute-done.13), kind=kLoop, calls=%fused_computation | loop fusion | flops 1327104 | bytes 3538944 | tf_op jit(solution)/shard_map/convert_element_type | solution.py:386
  (2 shorter events, 0.0 us)
Async XLA Ops:
  3.3 21.8 %all-to-all-start = ((bf16[16,32,896]{2,1,0:T(8,128)(2,1)}), bf16[16,32,896]{2,1,0:T(8,128)(2,1)S(1)}, u32[]{:S(2)}, u32[]{:S(2)}) async-start(bf16[16,32,896]{2,1,0:T(8,128)(2,1)} %bitcast.16), calls=%async_computation | async-start | bytes 1835008 | tf_op jit(solution)/shard_map/all_to_all | solution.py:353
  23.9 14.1 %copy-start.1 = (bf16[1,16,16,1152]{3,2,1,0:T(8,128)(2,1)S(1)}, bf16[1,16,16,1152]{3,2,1,0:T(8,128)(2,1)}, u32[]{:S(2)}) copy-start(bf16[1,16,16,1152]{3,2,1,0:T(8,128)(2,1)} %param.8) | copy-start | bytes 1769476
  23.9 14.1 %copy-start.3 = (s32[1,64]{1,0:T(1,128)S(1)}, s32[1,64]{1,0:T(1,128)}, u32[]{:S(2)}) copy-start(s32[1,64]{1,0:T(1,128)} %param.11) | copy-start | bytes 772
  26.0 26.1 %all-to-all-start.1 = ((bf16[16,32,1152]{2,1,0:T(8,128)(2,1)}), bf16[16,32,1152]{2,1,0:T(8,128)(2,1)S(1)}, u32[]{:S(2)}, u32[]{:S(2)}) async-start(bf16[16,32,1152]{2,1,0:T(8,128)(2,1)} %bitcast.5), calls=%async_computation.1 | async-start | bytes 2359296 | tf_op jit(solution)/shard_map/all_to_all | solution.py:358
  30.5 24.9 %collective-permute-start.3 = (bf16[768,256]{1,0:T(8,128)(2,1)S(1)}, bf16[768,256]{1,0:T(8,128)(2,1)S(1)}, u32[]{:S(2)}, u32[]{:S(2)}) collective-permute-start(bf16[768,256]{1,0:T(8,128)(2,1)S(1)} %get-tuple-element.24.refs_0_), channel_id=1, source_target_pairs={{0,32},{16,48},{32,0},{48,16},{64,96},{80,112},{96,64},{112,80},{1... | collective-permute-start | bytes 1179656 | tf_op jit(solution)/shard_map/ppermute | solution.py:363
  33.3 22.2 %collective-permute-start.2 = (bf16[768,256]{1,0:T(8,128)(2,1)S(1)}, bf16[768,256]{1,0:T(8,128)(2,1)S(1)}, u32[]{:S(2)}, u32[]{:S(2)}) collective-permute-start(bf16[768,256]{1,0:T(8,128)(2,1)S(1)} %get-tuple-element.24.refs_0_), channel_id=1, source_target_pairs={{0,48},{16,0},{32,16},{48,32},{64,112},{80,64},{96,80},{112,96},{1... | collective-permute-start | bytes 1179656 | tf_op jit(solution)/shard_map/ppermute | solution.py:362
  34.1 21.3 %collective-permute-start.1 = (bf16[768,256]{1,0:T(8,128)(2,1)S(1)}, bf16[768,256]{1,0:T(8,128)(2,1)}, u32[]{:S(2)}, u32[]{:S(2)}) collective-permute-start(bf16[768,256]{1,0:T(8,128)(2,1)S(1)} %get-tuple-element.24.refs_0_), channel_id=1, source_target_pairs={{0,16},{16,32},{32,48},{48,0},{64,80},{80,96},{96,112},{112,64},{1... | collective-permute-start | bytes 1179656 | tf_op jit(solution)/shard_map/ppermute | solution.py:361
  34.8 21.5 %collective-permute-start = (bf16[768,256]{1,0:T(8,128)(2,1)S(1)}, bf16[768,256]{1,0:T(8,128)(2,1)}, u32[]{:S(2)}, u32[]{:S(2)}) collective-permute-start(bf16[768,256]{1,0:T(8,128)(2,1)S(1)} %get-tuple-element.24.refs_0_), channel_id=1, source_target_pairs={{0,64},{16,80},{32,96},{48,112},{64,0},{80,16},{96,32},{112,48},{1... | collective-permute-start | bytes 1179656 | tf_op jit(solution)/shard_map/ppermute | solution.py:360
  38.1 2.8 %copy-start = (bf16[128,64,384]{2,1,0:T(8,128)(2,1)S(1)}, bf16[128,64,384]{2,1,0:T(8,128)(2,1)}, u32[]{:S(2)}) copy-start(bf16[128,64,384]{2,1,0:T(8,128)(2,1)} %pool_ref.1) | copy-start | bytes 18874372
  40.8 0.9 copy-start.2
  52.8 14.5 %collective-permute-start.7 = (bf16[256,1152]{1,0:T(8,128)(2,1)S(1)}, bf16[256,1152]{1,0:T(8,128)(2,1)S(1)}, u32[]{:S(2)}, u32[]{:S(2)}) collective-permute-start(bf16[256,1152]{1,0:T(8,128)(2,1)S(1)} %grad_pred.1.refs_8_), channel_id=1, source_target_pairs={{0,6},{1,7},{2,0},{3,1},{4,2},{5,3},{6,4},{7,5},{8,14},{9,15},{10,... | collective-permute-start | bytes 1769480 | tf_op jit(solution)/shard_map/ppermute | solution.py:370
  55.4 14.3 %collective-permute-start.6 = (bf16[256,1152]{1,0:T(8,128)(2,1)S(1)}, bf16[256,1152]{1,0:T(8,128)(2,1)S(1)}, u32[]{:S(2)}, u32[]{:S(2)}) collective-permute-start(bf16[256,1152]{1,0:T(8,128)(2,1)S(1)} %grad_pred.1.refs_8_), channel_id=1, source_target_pairs={{0,2},{1,3},{2,4},{3,5},{4,6},{5,7},{6,0},{7,1},{8,10},{9,11},{10,... | collective-permute-start | bytes 1769480 | tf_op jit(solution)/shard_map/ppermute | solution.py:369
  56.3 11.0 %collective-permute-start.8 = (bf16[768,256]{1,0:T(8,128)(2,1)}, bf16[768,256]{1,0:T(8,128)(2,1)S(1)}, u32[]{:S(2)}, u32[]{:S(2)}) collective-permute-start(bf16[768,256]{1,0:T(8,128)(2,1)} %collective-permute-done.refs_4_), channel_id=1, source_target_pairs={{0,16},{16,32},{32,48},{48,0},{64,80},{80,96},{96,112},{112,64},{1... | collective-permute-start | bytes 1179656 | tf_op jit(solution)/shard_map/ppermute | solution.py:372
  57.5 19.6 %collective-permute-start.5 = (bf16[768,256]{1,0:T(8,128)(2,1)}, bf16[768,256]{1,0:T(8,128)(2,1)S(1)}, u32[]{:S(2)}, u32[]{:S(2)}) collective-permute-start(bf16[768,256]{1,0:T(8,128)(2,1)} %collective-permute-done.refs_4_), channel_id=1, source_target_pairs={{0,32},{16,48},{32,0},{48,16},{64,96},{80,112},{96,64},{112,80},{1... | collective-permute-start | bytes 1179656 | tf_op jit(solution)/shard_map/ppermute | solution.py:374
  59.9 17.2 %collective-permute-start.4 = (bf16[768,256]{1,0:T(8,128)(2,1)}, bf16[768,256]{1,0:T(8,128)(2,1)S(1)}, u32[]{:S(2)}, u32[]{:S(2)}) collective-permute-start(bf16[768,256]{1,0:T(8,128)(2,1)} %collective-permute-done.refs_4_), channel_id=1, source_target_pairs={{0,48},{16,0},{32,16},{48,32},{64,112},{80,64},{96,80},{112,96},{1... | collective-permute-start | bytes 1179656 | tf_op jit(solution)/shard_map/ppermute | solution.py:373
  69.8 7.4 %collective-permute-start.9 = (bf16[128,1152]{1,0:T(8,128)(2,1)S(1)}, bf16[128,1152]{1,0:T(8,128)(2,1)S(1)}, u32[]{:S(2)}, u32[]{:S(2)}) collective-permute-start(bf16[128,1152]{1,0:T(8,128)(2,1)S(1)} %slice.6), channel_id=1, source_target_pairs={{0,2},{1,3},{2,4},{3,5},{4,6},{5,7},{6,0},{7,1},{8,10},{9,11},{10,... | collective-permute-start | bytes 884744 | tf_op jit(solution)/shard_map/ppermute | solution.py:376
  70.1 7.1 %collective-permute-start.10 = (bf16[128,1152]{1,0:T(8,128)(2,1)S(1)}, bf16[128,1152]{1,0:T(8,128)(2,1)S(1)}, u32[]{:S(2)}, u32[]{:S(2)}) collective-permute-start(bf16[128,1152]{1,0:T(8,128)(2,1)S(1)} %slice.7), channel_id=1, source_target_pairs={{0,6},{1,7},{2,0},{3,1},{4,2},{5,3},{6,4},{7,5},{8,14},{9,15},{10,... | collective-permute-start | bytes 884744 | tf_op jit(solution)/shard_map/ppermute | solution.py:377
  80.1 5.7 %collective-permute-start.12 = (bf16[384,1152]{1,0:T(8,128)(2,1)S(1)}, bf16[384,1152]{1,0:T(8,128)(2,1)S(1)}, u32[]{:S(2)}, u32[]{:S(2)}) collective-permute-start(bf16[384,1152]{1,0:T(8,128)(2,1)S(1)} %get-tuple-element.40), channel_id=1, source_target_pairs={{0,1},{1,0},{2,3},{3,2},{4,5},{5,4},{6,7},{7,6},{8,9},{9,8},{10,11... | collective-permute-start | bytes 2654216 | tf_op jit(solution)/shard_map/ppermute | solution.py:381
  84.9 2.7 %collective-permute-start.11 = (bf16[384,1152]{1,0:T(8,128)(2,1)S(1)}, bf16[384,1152]{1,0:T(8,128)(2,1)S(1)}, u32[]{:S(2)}, u32[]{:S(2)}) collective-permute-start(bf16[384,1152]{1,0:T(8,128)(2,1)S(1)} %outer_rows.3), channel_id=1, source_target_pairs={{0,1},{1,0},{2,3},{3,2},{4,5},{5,4},{6,7},{7,6},{8,9},{9,8},{10,11... | collective-permute-start | bytes 2654216 | tf_op jit(solution)/shard_map/ppermute | solution.py:383
  87.0 20.9 %collective-permute-start.13 = (bf16[384,1152]{1,0:T(8,128)(2,1)S(1)}, bf16[384,1152]{1,0:T(8,128)(2,1)S(1)}, u32[]{:S(2)}, u32[]{:S(2)}) collective-permute-start(bf16[384,1152]{1,0:T(8,128)(2,1)S(1)} %outer_rows.5), channel_id=1, source_target_pairs={{0,8},{1,9},{2,10},{3,11},{4,12},{5,13},{6,14},{7,15},{8,0},{9,1},... | collective-permute-start | bytes 2654216 | tf_op jit(solution)/shard_map/ppermute | solution.py:386
